TPU v7x, 32 devices: a whole 2x2x4 slice. The times are simulated.
32 devices in a mesh: dp: 8 (over y, x, core), phase: 4 (over z).
Axes of the slice: x: 2, y: 2, z: 4, core: 2. Of those that a mesh axis runs over, the one named last changes fastest.
Arguments:
- patches: bfloat16 [4096, 1280], P(('dp', 'phase')), may hold values from -6 to 6
- window_ids: int32 [32, 128], P(('dp', 'phase')), may hold values from 0 to 3, never falling along the last dimension, each value on 1 to 64 neighbouring positions
- norm_gain: float32 [4, 1280], replicated, may hold values from 0.1 to 1.9
- w_qkv: bfloat16 [4, 1280, 1920], P(None, 'dp')
- w_out: bfloat16 [4, 640, 1280], P(None, 'dp'), may hold values from -0.25 to 0.25
- merge_gain: float32 [1280], replicated, may hold values from 0.1 to 1.9
Outputs:
- merged: bfloat16 [1024, 5120], P(('dp', 'phase'))
Inputs may be any that keep to these rules, and one draw needn't show every extreme that they name: `window_ids`: window numbers never fall along a micro-batch; each window holds 1 to 64 patches, one exactly 64.
All inputs are finite; a program needn't handle non-finite values.
Results may differ from a plain program's by a relative error of at most 0.028.
Values may be sent and summed in bfloat16 or wider, within the bound.
No kernel may reach another device: no remote copies, remote signals or barrier semaphores. Data moves between devices by JAX's collectives and lax.ppermute only.
A program may use at most 64 MiB of HBM per device.

v0:
```python
import jax
import jax.numpy as jnp
from jax import lax
from jax.sharding import PartitionSpec as P

D_VIS = 1280
HEADS = 8
HEAD_DIM = 80
SECTIONS = 4


def shifted(block, axis, distance):
    devices = range(lax.axis_size(axis))
    route = [((i - distance) % len(devices), i) for i in devices]
    return lax.ppermute(block, axis, route)


def rms_scale(values, gain):
    return values * lax.rsqrt(jnp.mean(values * values, axis=-1, keepdims=True) + 1e-06) * gain


def finish(acts, gain):
    return rms_scale(acts.astype(jnp.float32), gain).astype(jnp.bfloat16)


def section(acts, marks, gain, weight_qkv, weight_out):
    width = HEADS * HEAD_DIM
    rows = acts.shape[0]
    values_f = acts.astype(jnp.float32)
    normed = rms_scale(values_f, gain).astype(jnp.bfloat16)
    qkv = jnp.dot(normed, weight_qkv, preferred_element_type=jnp.float32).astype(jnp.bfloat16)
    query = qkv[:, :width].reshape(rows, HEADS, HEAD_DIM)
    keys = qkv[:, width : 2 * width].reshape(rows, HEADS, HEAD_DIM)
    vals = qkv[:, 2 * width :].reshape(rows, HEADS, HEAD_DIM)
    scores = jnp.einsum(
        "qhd,khd->hqk", query, keys, preferred_element_type=jnp.float32
    ) * HEAD_DIM ** (-0.5)
    same = marks[:, None] == marks[None, :]
    scores = jnp.where(same[None], scores, jnp.float32(-1e30))
    highest = jnp.max(scores, axis=-1, keepdims=True)
    weights = jnp.exp(scores - highest)
    probs = (weights / jnp.sum(weights, axis=-1, keepdims=True)).astype(jnp.bfloat16)
    context = jnp.einsum("hqk,khd->qhd", probs, vals, preferred_element_type=jnp.float32).astype(
        jnp.bfloat16
    )
    update = jnp.dot(context.reshape(rows, width), weight_out, preferred_element_type=jnp.float32)
    return (values_f + update).astype(jnp.bfloat16)


def body(patches, window_ids, norm_gain, w_qkv, w_out, merge_gain):
    place = lax.axis_index("phase")
    count = w_qkv.shape[0]
    mine = place % count
    local_qkv = lax.dynamic_index_in_dim(w_qkv, mine, 0, keepdims=False)
    local_out = lax.dynamic_index_in_dim(w_out, mine, 0, keepdims=False)
    weight_qkv, weight_out = (
        lax.all_gather(local_qkv, "dp", axis=0, tiled=True),
        lax.all_gather(local_out, "dp", axis=0, tiled=True),
    )
    gain = lax.dynamic_index_in_dim(norm_gain, mine, 0, keepdims=False)
    marks_start = window_ids[0].astype(jnp.bfloat16)

    def work(step, acts, marks):
        delay = (step - place) % count
        active = step - delay == mine

        def run(values):
            return section(values, marks, gain, weight_qkv, weight_out)

        def keep(values):
            return values

        return lax.cond(active, run, keep, acts)

    def advance(step, carry):
        acts, marks = carry
        acts = work(step, acts, marks)
        return shifted((acts, marks), "phase", 1)

    acts, marks = lax.fori_loop(0, 2 * SECTIONS - 1, advance, (patches, marks_start))
    acts = shifted(acts, "phase", -(2 * SECTIONS - 1))
    final = finish(acts, merge_gain)
    return final.reshape(-1, 4 * D_VIS)


def solution(mesh):
    in_specs = (
        P(("dp", "phase"), None),
        P(("dp", "phase"), None),
        P(),
        P(None, "dp", None),
        P(None, "dp", None),
        P(),
    )
    out_specs = P(("dp", "phase"), None)
    return jax.shard_map(body, mesh=mesh, in_specs=in_specs, out_specs=out_specs, check_vma=False)
```

profile of v0, /device:TPU:0, one launch (start us, length us, event | category | flops | bytes accessed | tf_op | source)
XLA Modules:
  0.0 223.2 jit_solution(1411961527915390373)
XLA Ops:
  6.6 1.8 constant_dynamic-slice_fusion
  10.1 27.8 %all-gather.7.cloned.1.call-done = bf16[1,640,1280]{2,1,0:T(8,128)(2,1)} async-done(((bf16[1,80,1280]{2,1,0:T(8,128)(2,1)}), bf16[1,640,1280]{2,1,0:T(8,128)(2,1)}) %all-gather.7.cloned.1.call-update) | async-done | bytes 1638416 | tf_op jit(solution)/shard_map/all_gather | solution.py:58
  38.0 41.7 %all-gather.5.cloned.1.call-done = bf16[1,1280,1920]{2,1,0:T(8,128)(2,1)} async-done(((bf16[1,160,1920]{2,1,0:T(8,128)(2,1)}), bf16[1,1280,1920]{2,1,0:T(8,128)(2,1)}) %all-gather.5.cloned.1.call-update) | async-done | bytes 4915216 | tf_op jit(solution)/shard_map/all_gather | solution.py:57
  79.6 126.6 %while.20 = (s32[]{:T(128)}, bf16[128,1280]{1,0:T(8,128)(2,1)S(1)}, bf16[128]{0:T(256)(128)(2,1)S(1)}, s32[]{:T(128)}, s32[]{:T(128)}, /*index=5*/f32[1280]{0:T(...) while((s32[]{:T(128)}, bf16[128,1280]{1,0:T(8,128)(2,1)S(1)}, ...), condition=%wide.region_6.7_spmd, body=%wide.region_0.6_spmd.sunk | while | flops 904938880 | bytes 14550152 | solution.py:80
  79.6 9.0 %conditional.2 = (bf16[128,1280]{1,0:T(8,128)(2,1)S(1)}) conditional(s32[]{:T(128)} %convert_element_type.75, bf16[128,1280]{1,0:T(8,128)(2,1)S(1)} %get-tuple-element.312, (bf16[128,1280]{1,0:T(8,128)(2,1)S(1)}, f32[1280]{0:T(1024)S(1)}, bf16[1280,1920]{1,0:T(8,128)(2,1)}, bf16[128]{0:T(256)(128)(2,1)S(1)}, bf16[640,1280]{1,0:T(8,128)(2,1)}) %tuple.52), branch_computations={%region_1.1_spmd, %region_2.5_spmd} | conditional | flops 904938880 | bytes 12582152 | solution.py:73
  79.8 3.4 %convolution_convert_fusion = bf16[128,1920]{1,0:T(8,128)(2,1)S(1)} fusion(bf16[1280,1920]{1,0:T(8,128)(2,1)} %get-tuple-element.217, bf16[128,1280]{1,0:T(8,128)(2,1)S(1)} %get-tuple-element.215, f32[1280]{0:T(1024)S(1)} %get-tuple-element.216, f32[128]{0:T(128)S(1)} %add_rsqrt_fusion), kind=kOutput, calls=%fused_computation.3 | convolution fusion | flops 630046720 | bytes 5740032 | tf_op jit(solution)/shard_map/while/body/eval_jaxpr/cond/branch_1_fun/dot_general | solution.py:31
  85.3 1.5 convolution_convert_fusion.1
  86.8 1.9 fusion.1
  88.8 11.6 %collective-permute-done = bf16[128,1280]{1,0:T(8,128)(2,1)S(1)} collective-permute-done((bf16[128,1280]{1,0:T(8,128)(2,1)S(1)}, bf16[128,1280]{1,0:T(8,128)(2,1)S(1)}, u32[]{:S(2)}, u32[]{:S(2)}) %collective-permute-start) | collective-permute-done | bytes 327712 | tf_op jit(solution)/shard_map/while/body/eval_jaxpr/ppermute | solution.py:15
  100.5 9.0 %conditional.2 = (bf16[128,1280]{1,0:T(8,128)(2,1)S(1)}) conditional(s32[]{:T(128)} %convert_element_type.75, bf16[128,1280]{1,0:T(8,128)(2,1)S(1)} %get-tuple-element.312, (bf16[128,1280]{1,0:T(8,128)(2,1)S(1)}, f32[1280]{0:T(1024)S(1)}, bf16[1280,1920]{1,0:T(8,128)(2,1)}, bf16[128]{0:T(256)(128)(2,1)S(1)}, bf16[640,1280]{1,0:T(8,128)(2,1)}) %tuple.52), branch_computations={%region_1.1_spmd, %region_2.5_spmd} | conditional | flops 904938880 | bytes 12582152 | solution.py:73
  100.7 3.3 %convolution_convert_fusion = bf16[128,1920]{1,0:T(8,128)(2,1)S(1)} fusion(bf16[1280,1920]{1,0:T(8,128)(2,1)} %get-tuple-element.217, bf16[128,1280]{1,0:T(8,128)(2,1)S(1)} %get-tuple-element.215, f32[1280]{0:T(1024)S(1)} %get-tuple-element.216, f32[128]{0:T(128)S(1)} %add_rsqrt_fusion), kind=kOutput, calls=%fused_computation.3 | convolution fusion | flops 630046720 | bytes 5740032 | tf_op jit(solution)/shard_map/while/body/eval_jaxpr/cond/branch_1_fun/dot_general | solution.py:31
  106.1 1.5 convolution_convert_fusion.1
  107.6 1.9 fusion.1
  109.7 10.8 %collective-permute-done = bf16[128,1280]{1,0:T(8,128)(2,1)S(1)} collective-permute-done((bf16[128,1280]{1,0:T(8,128)(2,1)S(1)}, bf16[128,1280]{1,0:T(8,128)(2,1)S(1)}, u32[]{:S(2)}, u32[]{:S(2)}) %collective-permute-start) | collective-permute-done | bytes 327712 | tf_op jit(solution)/shard_map/while/body/eval_jaxpr/ppermute | solution.py:15
  120.5 9.0 %conditional.2 = (bf16[128,1280]{1,0:T(8,128)(2,1)S(1)}) conditional(s32[]{:T(128)} %convert_element_type.75, bf16[128,1280]{1,0:T(8,128)(2,1)S(1)} %get-tuple-element.312, (bf16[128,1280]{1,0:T(8,128)(2,1)S(1)}, f32[1280]{0:T(1024)S(1)}, bf16[1280,1920]{1,0:T(8,128)(2,1)}, bf16[128]{0:T(256)(128)(2,1)S(1)}, bf16[640,1280]{1,0:T(8,128)(2,1)}) %tuple.52), branch_computations={%region_1.1_spmd, %region_2.5_spmd} | conditional | flops 904938880 | bytes 12582152 | solution.py:73
  120.7 3.4 %convolution_convert_fusion = bf16[128,1920]{1,0:T(8,128)(2,1)S(1)} fusion(bf16[1280,1920]{1,0:T(8,128)(2,1)} %get-tuple-element.217, bf16[128,1280]{1,0:T(8,128)(2,1)S(1)} %get-tuple-element.215, f32[1280]{0:T(1024)S(1)} %get-tuple-element.216, f32[128]{0:T(128)S(1)} %add_rsqrt_fusion), kind=kOutput, calls=%fused_computation.3 | convolution fusion | flops 630046720 | bytes 5740032 | tf_op jit(solution)/shard_map/while/body/eval_jaxpr/cond/branch_1_fun/dot_general | solution.py:31
  126.2 1.5 convolution_convert_fusion.1
  127.7 1.9 fusion.1
  129.7 9.9 %collective-permute-done = bf16[128,1280]{1,0:T(8,128)(2,1)S(1)} collective-permute-done((bf16[128,1280]{1,0:T(8,128)(2,1)S(1)}, bf16[128,1280]{1,0:T(8,128)(2,1)S(1)}, u32[]{:S(2)}, u32[]{:S(2)}) %collective-permute-start) | collective-permute-done | bytes 327712 | tf_op jit(solution)/shard_map/while/body/eval_jaxpr/ppermute | solution.py:15
  139.7 9.0 %conditional.2 = (bf16[128,1280]{1,0:T(8,128)(2,1)S(1)}) conditional(s32[]{:T(128)} %convert_element_type.75, bf16[128,1280]{1,0:T(8,128)(2,1)S(1)} %get-tuple-element.312, (bf16[128,1280]{1,0:T(8,128)(2,1)S(1)}, f32[1280]{0:T(1024)S(1)}, bf16[1280,1920]{1,0:T(8,128)(2,1)}, bf16[128]{0:T(256)(128)(2,1)S(1)}, bf16[640,1280]{1,0:T(8,128)(2,1)}) %tuple.52), branch_computations={%region_1.1_spmd, %region_2.5_spmd} | conditional | flops 904938880 | bytes 12582152 | solution.py:73
  139.9 3.4 %convolution_convert_fusion = bf16[128,1920]{1,0:T(8,128)(2,1)S(1)} fusion(bf16[1280,1920]{1,0:T(8,128)(2,1)} %get-tuple-element.217, bf16[128,1280]{1,0:T(8,128)(2,1)S(1)} %get-tuple-element.215, f32[1280]{0:T(1024)S(1)} %get-tuple-element.216, f32[128]{0:T(128)S(1)} %add_rsqrt_fusion), kind=kOutput, calls=%fused_computation.3 | convolution fusion | flops 630046720 | bytes 5740032 | tf_op jit(solution)/shard_map/while/body/eval_jaxpr/cond/branch_1_fun/dot_general | solution.py:31
  145.3 1.5 convolution_convert_fusion.1
  146.8 1.9 fusion.1
  148.9 8.9 %collective-permute-done = bf16[128,1280]{1,0:T(8,128)(2,1)S(1)} collective-permute-done((bf16[128,1280]{1,0:T(8,128)(2,1)S(1)}, bf16[128,1280]{1,0:T(8,128)(2,1)S(1)}, u32[]{:S(2)}, u32[]{:S(2)}) %collective-permute-start) | collective-permute-done | bytes 327712 | tf_op jit(solution)/shard_map/while/body/eval_jaxpr/ppermute | solution.py:15
  157.9 7.6 %collective-permute-start = (bf16[128,1280]{1,0:T(8,128)(2,1)S(1)}, bf16[128,1280]{1,0:T(8,128)(2,1)S(1)}, u32[]{:S(2)}, u32[]{:S(2)}) collective-permute-start(bf16[128,1280]{1,0:T(8,128)(2,1)S(1)} %get-tuple-element.335), channel_id=1, source_target_pairs={{3,0},{0,1},{1,2},{2,3},{7,4},{4,5},{5,6},{6,7},{11,8},{8,9},{9,10... | collective-permute-start | bytes 983048 | tf_op jit(solution)/shard_map/while/body/eval_jaxpr/ppermute | solution.py:15
  165.5 6.0 %collective-permute-done = bf16[128,1280]{1,0:T(8,128)(2,1)S(1)} collective-permute-done((bf16[128,1280]{1,0:T(8,128)(2,1)S(1)}, bf16[128,1280]{1,0:T(8,128)(2,1)S(1)}, u32[]{:S(2)}, u32[]{:S(2)}) %collective-permute-start) | collective-permute-done | bytes 327712 | tf_op jit(solution)/shard_map/while/body/eval_jaxpr/ppermute | solution.py:15
  171.7 2.4 %collective-permute-start = (bf16[128,1280]{1,0:T(8,128)(2,1)S(1)}, bf16[128,1280]{1,0:T(8,128)(2,1)S(1)}, u32[]{:S(2)}, u32[]{:S(2)}) collective-permute-start(bf16[128,1280]{1,0:T(8,128)(2,1)S(1)} %get-tuple-element.335), channel_id=1, source_target_pairs={{3,0},{0,1},{1,2},{2,3},{7,4},{4,5},{5,6},{6,7},{11,8},{8,9},{9,10... | collective-permute-start | bytes 983048 | tf_op jit(solution)/shard_map/while/body/eval_jaxpr/ppermute | solution.py:15
  174.1 7.7 %collective-permute-start.1 = (bf16[128]{0:T(256)(128)(2,1)S(1)}, bf16[128]{0:T(256)(128)(2,1)S(1)}, u32[]{:S(2)}, u32[]{:S(2)}) collective-permute-start(bf16[128]{0:T(256)(128)(2,1)S(1)} %copy.23), channel_id=1, source_target_pairs={{3,0},{0,1},{1,2},{2,3},{7,4},{4,5},{5,6},{6,7},{11,8},{8,9},{9,10... | collective-permute-start | bytes 776 | tf_op jit(solution)/shard_map/while/body/eval_jaxpr/ppermute | solution.py:15
  181.7 6.1 %collective-permute-done = bf16[128,1280]{1,0:T(8,128)(2,1)S(1)} collective-permute-done((bf16[128,1280]{1,0:T(8,128)(2,1)S(1)}, bf16[128,1280]{1,0:T(8,128)(2,1)S(1)}, u32[]{:S(2)}, u32[]{:S(2)}) %collective-permute-start) | collective-permute-done | bytes 327712 | tf_op jit(solution)/shard_map/while/body/eval_jaxpr/ppermute | solution.py:15
  188.8 2.5 %collective-permute-start.1 = (bf16[128]{0:T(256)(128)(2,1)S(1)}, bf16[128]{0:T(256)(128)(2,1)S(1)}, u32[]{:S(2)}, u32[]{:S(2)}) collective-permute-start(bf16[128]{0:T(256)(128)(2,1)S(1)} %copy.23), channel_id=1, source_target_pairs={{3,0},{0,1},{1,2},{2,3},{7,4},{4,5},{5,6},{6,7},{11,8},{8,9},{9,10... | collective-permute-start | bytes 776 | tf_op jit(solution)/shard_map/while/body/eval_jaxpr/ppermute | solution.py:15
  191.3 14.9 %collective-permute-done = bf16[128,1280]{1,0:T(8,128)(2,1)S(1)} collective-permute-done((bf16[128,1280]{1,0:T(8,128)(2,1)S(1)}, bf16[128,1280]{1,0:T(8,128)(2,1)S(1)}, u32[]{:S(2)}, u32[]{:S(2)}) %collective-permute-start) | collective-permute-done | bytes 327712 | tf_op jit(solution)/shard_map/while/body/eval_jaxpr/ppermute | solution.py:15
  206.3 8.9 %collective-permute-done.2 = bf16[128,1280]{1,0:T(8,128)(2,1)S(1)} collective-permute-done((bf16[128,1280]{1,0:T(8,128)(2,1)S(1)}, bf16[128,1280]{1,0:T(8,128)(2,1)S(1)}, u32[]{:S(2)}, u32[]{:S(2)}) %collective-permute-start.2) | collective-permute-done | bytes 327712 | tf_op jit(solution)/shard_map/ppermute | solution.py:15
  (90 shorter events, 13.9 us)
Async XLA Ops:
  6.5 1.9 copy-start
  6.5 73.1 %copy-start.1 = (bf16[128,1280]{1,0:T(8,128)(2,1)S(1)}, bf16[128,1280]{1,0:T(8,128)(2,1)}, u32[]{:S(2)}) copy-start(bf16[128,1280]{1,0:T(8,128)(2,1)} %param.10) | copy-start | bytes 983044
  6.5 3.5 %copy-start.3 = (s32[1,128]{1,0:T(1,128)S(1)}, s32[1,128]{1,0:T(1,128)}, u32[]{:S(2)}) copy-start(s32[1,128]{1,0:T(1,128)} %param.11) | copy-start | bytes 1540
  6.5 31.4 %all-gather.7.cloned.1.call-start = ((), (), s32[]{:S(2)}) async-start(), calls=%async_computation.1 | async-start | bytes 1843200 | tf_op jit(solution)/shard_map/all_gather | solution.py:58
  8.4 71.2 %all-gather.5.cloned.1.call-start = ((), (), s32[]{:S(2)}) async-start(), calls=%async_computation | async-start | bytes 5529600 | tf_op jit(solution)/shard_map/all_gather | solution.py:57
  79.6 135.7 %copy-start.2 = (f32[1280]{0:T(1024)S(1)}, f32[1280]{0:T(1024)}, u32[]{:S(2)}) copy-start(f32[1280]{0:T(1024)} %param.15) | copy-start | bytes 15364
  88.7 11.7 %collective-permute-start = (bf16[128,1280]{1,0:T(8,128)(2,1)S(1)}, bf16[128,1280]{1,0:T(8,128)(2,1)S(1)}, u32[]{:S(2)}, u32[]{:S(2)}) collective-permute-start(bf16[128,1280]{1,0:T(8,128)(2,1)S(1)} %get-tuple-element.335), channel_id=1, source_target_pairs={{3,0},{0,1},{1,2},{2,3},{7,4},{4,5},{5,6},{6,7},{11,8},{8,9},{9,10... | collective-permute-start | bytes 983048 | tf_op jit(solution)/shard_map/while/body/eval_jaxpr/ppermute | solution.py:15
  88.7 11.7 %collective-permute-start.1 = (bf16[128]{0:T(256)(128)(2,1)S(1)}, bf16[128]{0:T(256)(128)(2,1)S(1)}, u32[]{:S(2)}, u32[]{:S(2)}) collective-permute-start(bf16[128]{0:T(256)(128)(2,1)S(1)} %copy.23), channel_id=1, source_target_pairs={{3,0},{0,1},{1,2},{2,3},{7,4},{4,5},{5,6},{6,7},{11,8},{8,9},{9,10... | collective-permute-start | bytes 776 | tf_op jit(solution)/shard_map/while/body/eval_jaxpr/ppermute | solution.py:15
  109.5 10.9 %collective-permute-start = (bf16[128,1280]{1,0:T(8,128)(2,1)S(1)}, bf16[128,1280]{1,0:T(8,128)(2,1)S(1)}, u32[]{:S(2)}, u32[]{:S(2)}) collective-permute-start(bf16[128,1280]{1,0:T(8,128)(2,1)S(1)} %get-tuple-element.335), channel_id=1, source_target_pairs={{3,0},{0,1},{1,2},{2,3},{7,4},{4,5},{5,6},{6,7},{11,8},{8,9},{9,10... | collective-permute-start | bytes 983048 | tf_op jit(solution)/shard_map/while/body/eval_jaxpr/ppermute | solution.py:15
  109.6 10.9 %collective-permute-start.1 = (bf16[128]{0:T(256)(128)(2,1)S(1)}, bf16[128]{0:T(256)(128)(2,1)S(1)}, u32[]{:S(2)}, u32[]{:S(2)}) collective-permute-start(bf16[128]{0:T(256)(128)(2,1)S(1)} %copy.23), channel_id=1, source_target_pairs={{3,0},{0,1},{1,2},{2,3},{7,4},{4,5},{5,6},{6,7},{11,8},{8,9},{9,10... | collective-permute-start | bytes 776 | tf_op jit(solution)/shard_map/while/body/eval_jaxpr/ppermute | solution.py:15
  129.6 10.0 %collective-permute-start = (bf16[128,1280]{1,0:T(8,128)(2,1)S(1)}, bf16[128,1280]{1,0:T(8,128)(2,1)S(1)}, u32[]{:S(2)}, u32[]{:S(2)}) collective-permute-start(bf16[128,1280]{1,0:T(8,128)(2,1)S(1)} %get-tuple-element.335), channel_id=1, source_target_pairs={{3,0},{0,1},{1,2},{2,3},{7,4},{4,5},{5,6},{6,7},{11,8},{8,9},{9,10... | collective-permute-start | bytes 983048 | tf_op jit(solution)/shard_map/while/body/eval_jaxpr/ppermute | solution.py:15
  129.7 10.0 %collective-permute-start.1 = (bf16[128]{0:T(256)(128)(2,1)S(1)}, bf16[128]{0:T(256)(128)(2,1)S(1)}, u32[]{:S(2)}, u32[]{:S(2)}) collective-permute-start(bf16[128]{0:T(256)(128)(2,1)S(1)} %copy.23), channel_id=1, source_target_pairs={{3,0},{0,1},{1,2},{2,3},{7,4},{4,5},{5,6},{6,7},{11,8},{8,9},{9,10... | collective-permute-start | bytes 776 | tf_op jit(solution)/shard_map/while/body/eval_jaxpr/ppermute | solution.py:15
  148.7 9.1 %collective-permute-start = (bf16[128,1280]{1,0:T(8,128)(2,1)S(1)}, bf16[128,1280]{1,0:T(8,128)(2,1)S(1)}, u32[]{:S(2)}, u32[]{:S(2)}) collective-permute-start(bf16[128,1280]{1,0:T(8,128)(2,1)S(1)} %get-tuple-element.335), channel_id=1, source_target_pairs={{3,0},{0,1},{1,2},{2,3},{7,4},{4,5},{5,6},{6,7},{11,8},{8,9},{9,10... | collective-permute-start | bytes 983048 | tf_op jit(solution)/shard_map/while/body/eval_jaxpr/ppermute | solution.py:15
  148.8 9.1 %collective-permute-start.1 = (bf16[128]{0:T(256)(128)(2,1)S(1)}, bf16[128]{0:T(256)(128)(2,1)S(1)}, u32[]{:S(2)}, u32[]{:S(2)}) collective-permute-start(bf16[128]{0:T(256)(128)(2,1)S(1)} %copy.23), channel_id=1, source_target_pairs={{3,0},{0,1},{1,2},{2,3},{7,4},{4,5},{5,6},{6,7},{11,8},{8,9},{9,10... | collective-permute-start | bytes 776 | tf_op jit(solution)/shard_map/while/body/eval_jaxpr/ppermute | solution.py:15
  157.9 13.7 %collective-permute-start = (bf16[128,1280]{1,0:T(8,128)(2,1)S(1)}, bf16[128,1280]{1,0:T(8,128)(2,1)S(1)}, u32[]{:S(2)}, u32[]{:S(2)}) collective-permute-start(bf16[128,1280]{1,0:T(8,128)(2,1)S(1)} %get-tuple-element.335), channel_id=1, source_target_pairs={{3,0},{0,1},{1,2},{2,3},{7,4},{4,5},{5,6},{6,7},{11,8},{8,9},{9,10... | collective-permute-start | bytes 983048 | tf_op jit(solution)/shard_map/while/body/eval_jaxpr/ppermute | solution.py:15
  165.5 6.2 %collective-permute-start.1 = (bf16[128]{0:T(256)(128)(2,1)S(1)}, bf16[128]{0:T(256)(128)(2,1)S(1)}, u32[]{:S(2)}, u32[]{:S(2)}) collective-permute-start(bf16[128]{0:T(256)(128)(2,1)S(1)} %copy.23), channel_id=1, source_target_pairs={{3,0},{0,1},{1,2},{2,3},{7,4},{4,5},{5,6},{6,7},{11,8},{8,9},{9,10... | collective-permute-start | bytes 776 | tf_op jit(solution)/shard_map/while/body/eval_jaxpr/ppermute | solution.py:15
  171.7 16.2 %collective-permute-start = (bf16[128,1280]{1,0:T(8,128)(2,1)S(1)}, bf16[128,1280]{1,0:T(8,128)(2,1)S(1)}, u32[]{:S(2)}, u32[]{:S(2)}) collective-permute-start(bf16[128,1280]{1,0:T(8,128)(2,1)S(1)} %get-tuple-element.335), channel_id=1, source_target_pairs={{3,0},{0,1},{1,2},{2,3},{7,4},{4,5},{5,6},{6,7},{11,8},{8,9},{9,10... | collective-permute-start | bytes 983048 | tf_op jit(solution)/shard_map/while/body/eval_jaxpr/ppermute | solution.py:15
  174.1 13.8 %collective-permute-start.1 = (bf16[128]{0:T(256)(128)(2,1)S(1)}, bf16[128]{0:T(256)(128)(2,1)S(1)}, u32[]{:S(2)}, u32[]{:S(2)}) collective-permute-start(bf16[128]{0:T(256)(128)(2,1)S(1)} %copy.23), channel_id=1, source_target_pairs={{3,0},{0,1},{1,2},{2,3},{7,4},{4,5},{5,6},{6,7},{11,8},{8,9},{9,10... | collective-permute-start | bytes 776 | tf_op jit(solution)/shard_map/while/body/eval_jaxpr/ppermute | solution.py:15
  188.0 18.2 %collective-permute-start = (bf16[128,1280]{1,0:T(8,128)(2,1)S(1)}, bf16[128,1280]{1,0:T(8,128)(2,1)S(1)}, u32[]{:S(2)}, u32[]{:S(2)}) collective-permute-start(bf16[128,1280]{1,0:T(8,128)(2,1)S(1)} %get-tuple-element.335), channel_id=1, source_target_pairs={{3,0},{0,1},{1,2},{2,3},{7,4},{4,5},{5,6},{6,7},{11,8},{8,9},{9,10... | collective-permute-start | bytes 983048 | tf_op jit(solution)/shard_map/while/body/eval_jaxpr/ppermute | solution.py:15
  188.8 17.4 %collective-permute-start.1 = (bf16[128]{0:T(256)(128)(2,1)S(1)}, bf16[128]{0:T(256)(128)(2,1)S(1)}, u32[]{:S(2)}, u32[]{:S(2)}) collective-permute-start(bf16[128]{0:T(256)(128)(2,1)S(1)} %copy.23), channel_id=1, source_target_pairs={{3,0},{0,1},{1,2},{2,3},{7,4},{4,5},{5,6},{6,7},{11,8},{8,9},{9,10... | collective-permute-start | bytes 776 | tf_op jit(solution)/shard_map/while/body/eval_jaxpr/ppermute | solution.py:15
  206.2 8.9 %collective-permute-start.2 = (bf16[128,1280]{1,0:T(8,128)(2,1)S(1)}, bf16[128,1280]{1,0:T(8,128)(2,1)S(1)}, u32[]{:S(2)}, u32[]{:S(2)}) collective-permute-start(bf16[128,1280]{1,0:T(8,128)(2,1)S(1)} %get-tuple-element.230), channel_id=1, source_target_pairs={{3,0},{0,1},{1,2},{2,3},{7,4},{4,5},{5,6},{6,7},{11,8},{8,9},{9,10... | collective-permute-start | bytes 983048 | tf_op jit(solution)/shard_map/ppermute | solution.py:15
Sparse Core Ops, SparseCore 0:
  9.2 28.6 all-gather.6
  39.8 39.7 all-gather.4
where the time goes:
time: 224 us; the launch traced here: 223 us
  waiting for transfers between devices  147 us (66%)
  matrix products  32.8 us (15%)
  starting transfers between devices  21.5 us (10%)
  between operations  13.5 us (6%)
  local copies, waits for them, and re-layouts  6.75 us (3%)
    ppermute x15, waiting for transfers between devices, shifted(): return lax.ppermute(block, axis, route)  77.3 us
    all_gather x1, waiting for transfers between devices, body(): lax.all_gather(local_qkv, 'dp', axis=0, tiled=True)  41.7 us
    all_gather x1, waiting for transfers between devices, body(): lax.all_gather(local_out, 'dp', axis=0, tiled=True)  27.8 us
    ppermute x15, starting transfers between devices, shifted(): return lax.ppermute(block, axis, route)  21.5 us
    dot_general x4, matrix products, section(): jnp.dot(normed, weight_qkv, preferred_element_type=jnp.float32)  13.4 us
    dot_general x4, matrix products, section(): jnp.dot(context.reshape(rows, width), weight_out, preferred_element_type=...  7.61 us
    dot_general x4, matrix products, section(): jnp.einsum('hqk,khd->qhd', probs, vals, preferred_element_type=jnp.float32)  5.9 us
  transfers between devices with their start and end apart: 17, of which 10 were waited for; matrix products, arithmetic and copies ran while one was open for 1% of the time, Pallas kernels for 0%

commit v1 on v0

v1 whole, which is shorter than its diff:
```python
import functools

import jax
import jax.numpy as jnp
from jax import lax
from jax.experimental import pallas as pl
from jax.experimental.pallas import tpu as pltpu
from jax.sharding import PartitionSpec as P

D_VIS = 1280
HEADS = 8
HEAD_DIM = 80
WIDTH = HEADS * HEAD_DIM
SECTIONS = 4
LANES = 128
EPS = 1e-06
NEG = -1e30
BLOCKS = ((0, 0, 160), (2, 0, 160), (4, 0, 160), (6, 0, 80), (6, 80, 80),
          (1, 0, 160), (3, 0, 160), (5, 0, 160), (7, 0, 80), (7, 80, 80))


def normed_rows(values, gain):
    scale = lax.rsqrt(jnp.mean(values * values, axis=-1, keepdims=True) + EPS)
    return values * scale * gain


def attend(qkv, row_ids):
    query, keys, vals = qkv
    rows = query.shape[0]
    across = jnp.broadcast_to(row_ids, (rows, rows))
    same = across == across.T
    lane = lax.broadcasted_iota(jnp.int32, (rows, LANES), 1)
    tiles = [None] * (WIDTH // LANES)
    for head in range(HEADS):
        first, last = head * HEAD_DIM, (head + 1) * HEAD_DIM
        low, high = first // LANES, -(-last // LANES)
        span = slice(low * LANES, high * LANES)
        inside = []
        for tile in range(low, high):
            place = lane + tile * LANES
            inside.append((place >= first) & (place < last))
        part = jnp.concatenate(
            [
                jnp.where(mask, query[:, (low + i) * LANES : (low + i + 1) * LANES], 0)
                for i, mask in enumerate(inside)
            ],
            axis=1,
        )
        scores = lax.dot_general(
            part, keys[:, span], (((1,), (1,)), ((), ())), preferred_element_type=jnp.float32
        )
        scores = jnp.where(same, scores * HEAD_DIM ** (-0.5), NEG)
        weights = jnp.exp(scores - jnp.max(scores, axis=-1, keepdims=True))
        probs = weights * (1.0 / jnp.sum(weights, axis=-1, keepdims=True))
        mixed = jnp.dot(
            probs.astype(jnp.bfloat16), vals[:, span], preferred_element_type=jnp.float32
        )
        for i, mask in enumerate(inside):
            kept = jnp.where(mask, mixed[:, i * LANES : (i + 1) * LANES], 0.0)
            tile = low + i
            tiles[tile] = kept if tiles[tile] is None else tiles[tile] + kept
    return jnp.concatenate(tiles, axis=1).astype(jnp.bfloat16)


def stage_kernel(steps, loads, n_chunks, micros, acts_parts, with_ctx, with_acts, *refs):
    refs = list(refs)
    me_ref = refs.pop(0)
    acts_refs = [refs.pop(0) for _ in acts_parts]
    ctx_ref = refs.pop(0) if with_ctx else None
    ids_refs = [refs.pop(0) for _ in range(micros)]
    gain_ref = refs.pop(0)
    merge_ref = refs.pop(0)
    chunks = [[refs.pop(0) for _ in BLOCKS] for _ in range(n_chunks)]
    out_refs = refs[: with_acts]
    hold, flow, sheets, sems = refs[with_acts:]
    me = me_ref[0]
    for slot, (chunk, unit, is_out) in enumerate(loads):
        for (distance, start, size), block in zip(BLOCKS, chunks[chunk]):
            owner = jnp.bitwise_xor(me, distance)
            if not is_out:
                where = pl.multiple_of(owner * 160 + start, 16)
                pltpu.make_async_copy(
                    block.at[unit], hold.at[slot, pl.ds(where, size)], sems.at[slot]
                ).start()
            else:
                for half in range(start // 80, (start + size) // 80):
                    where = pl.multiple_of(owner * 80 + half * WIDTH, 16)
                    pltpu.make_async_copy(
                        block.at[unit, pl.ds(half * 80 - start, 80)],
                        hold.at[slot, pl.ds(where, 80)],
                        sems.at[slot],
                    ).start()

    def arrive(slot):
        pltpu.make_async_copy(hold.at[slot], hold.at[slot], sems.at[slot]).wait()

    rows = 128
    for m, (ref, row) in enumerate(zip(acts_refs, acts_parts)):
        flow[m * rows : (m + 1) * rows] = ref[row : row + rows].astype(jnp.float32)
    ctx = ctx_ref[...] if with_ctx else None
    for step in steps:
        if step[0] == "att":
            normed = normed_rows(flow[...], gain_ref[step[1]]).astype(jnp.bfloat16)
            qkv = []
            for i in range(3):
                arrive(step[2] + i)
                qkv.append(
                    jnp.dot(
                        normed, hold[step[2] + i], preferred_element_type=jnp.float32
                    ).astype(jnp.bfloat16)
                )
            parts = [
                attend([part[m * rows : (m + 1) * rows] for part in qkv], ids_refs[m][...])
                for m in range(micros)
            ]
            ctx = parts[0] if micros == 1 else jnp.concatenate(parts, axis=0)
        elif step[0] == "out":
            arrive(step[1])
            for half in range(2):
                at = slice(half * WIDTH, (half + 1) * WIDTH)
                moved = jnp.dot(
                    ctx, hold[step[1], half * WIDTH : (half + 1) * WIDTH],
                    preferred_element_type=jnp.float32,
                )
                flow[:, at] = (flow[:, at] + moved).astype(jnp.bfloat16).astype(jnp.float32)
        else:
            final = normed_rows(flow[...], merge_ref[...])
            for tile in range(D_VIS // LANES):
                sheets[tile] = final[:, tile * LANES : (tile + 1) * LANES]
    if steps[-1][0] == "att":
        out_refs[0][...] = ctx
    elif steps[-1][0] == "out":
        out_refs[0][...] = flow[...].astype(jnp.bfloat16)
    else:
        for i in range(4):
            for tile in range(D_VIS // LANES):
                at = i * D_VIS + tile * LANES
                out_refs[0][:, at : at + LANES] = sheets[
                    tile, pl.ds(i, rows // 4, stride=4), :
                ].astype(jnp.bfloat16)


def run_stage(name, steps, loads, me, acts, ctx, ids, gains, merge, chunks):
    micros = len(acts)
    rows = 128
    last = steps[-1][0]
    shape = {
        "att": (micros * rows, WIDTH),
        "out": (micros * rows, D_VIS),
        "norm": (rows // 4, 4 * D_VIS),
    }[last]
    kernel = functools.partial(
        stage_kernel, steps, loads, len(chunks), micros, [row for _, row in acts],
        ctx is not None, 1,
    )
    vmem = pl.BlockSpec(memory_space=pltpu.VMEM)
    args = [me] + [a for a, _ in acts] + ([ctx] if ctx is not None else []) + list(ids)
    args += [gains, merge]
    specs = [pl.BlockSpec(memory_space=pltpu.SMEM)] + [vmem] * (len(args) - 1)
    for chunk in chunks:
        args += list(chunk)
        specs += [pl.BlockSpec(memory_space=pl.ANY)] * len(chunk)
    units = len(loads)
    return pl.pallas_call(
        kernel,
        out_shape=jax.ShapeDtypeStruct(shape, jnp.bfloat16),
        in_specs=specs,
        out_specs=vmem,
        scratch_shapes=[
            pltpu.VMEM((units, D_VIS, WIDTH), jnp.bfloat16),
            pltpu.VMEM((micros * rows, D_VIS), jnp.float32),
            pltpu.VMEM((D_VIS // LANES, rows, LANES), jnp.float32),
            pltpu.SemaphoreType.DMA((units,)),
        ],
        compiler_params=pltpu.CompilerParams(vmem_limit_bytes=40 * 1024 * 1024),
        cost_estimate=pl.CostEstimate(
            flops=2 * micros * rows * D_VIS * WIDTH * units,
            bytes_accessed=units * D_VIS * WIDTH * 2,
            transcendentals=micros * rows * rows * HEADS,
        ),
        name=name,
    )(*args)


def swap(block, bit):
    size = lax.axis_size("dp")
    return lax.ppermute(block, "dp", [(j, j ^ bit) for j in range(size)])


def between(block, from_first):
    size = lax.axis_size("phase")
    pairs = [(j, j ^ 1) for j in range(size) if (j % 4 in (1, 2)) == from_first]
    return lax.ppermute(block, "phase", pairs)


def unit_out(block):
    return block.reshape(80, 2, WIDTH).transpose(1, 0, 2).reshape(160, WIDTH)


def units_qkv(block):
    return block.reshape(160, 3, WIDTH).transpose(1, 0, 2)


def staged_body(patches, window_ids, norm_gain, w_qkv, w_out, merge_gain):
    tie = lax.optimization_barrier
    place = lax.axis_index("phase") % 4
    me = lax.axis_index("dp").astype(jnp.int32).reshape(1)
    first = (place == 1) | (place == 2)

    def pick(array, one, two):
        return lax.dynamic_index_in_dim(array, jnp.where(first, one, two), 0, keepdims=False)

    chunk_a = jnp.concatenate([units_qkv(pick(w_qkv, 0, 2)), unit_out(pick(w_out, 0, 1))[None]])
    chunk_b = units_qkv(pick(w_qkv, 1, 3))
    chunk_c = jnp.stack([unit_out(w_out[2]), unit_out(w_out[3])])
    gains_1 = norm_gain[:2].reshape(2, 1, D_VIS)
    gains_2 = norm_gain[2:].reshape(2, 1, D_VIS)
    merge = merge_gain.reshape(1, D_VIS)

    ax, ay = swap(chunk_a, 2), swap(chunk_a, 4)
    other_ids = lax.ppermute(
        window_ids, "phase", [(j, j ^ 1) for j in range(lax.axis_size("phase"))]
    )
    other = between(patches, False)
    ax, ay, chunk_b = tie((ax, ay, chunk_b))
    ad = [swap(ax[:, :80], 4), swap(ay[:, 80:], 2)]
    bx, by = swap(chunk_b, 2), swap(chunk_b, 4)
    blocks_a = [chunk_a, ax, ay] + ad
    blocks_a += [swap(block, 1) for block in blocks_a]

    bx, by = tie((bx, by))
    bd = [swap(bx[:, :80], 4), swap(by[:, 80:], 2)]
    blocks_b = [chunk_b, bx, by] + bd
    blocks_b += [swap(block, 1) for block in blocks_b]

    bd[0], bd[1], chunk_c = tie((bd[0], bd[1], chunk_c))
    cx, cy = swap(chunk_c, 2), swap(chunk_c, 4)
    cx, cy = tie((cx, cy))
    cd = [swap(cx[:, :80], 4), swap(cy[:, 80:], 2)]
    blocks_c = [chunk_c, cx, cy] + cd
    blocks_c += [swap(block, 1) for block in blocks_c]

    acts = run_stage(
        "section_0", [("att", 0, 0), ("out", 3)],
        [(0, 0, False), (0, 1, False), (0, 2, False), (0, 3, True)],
        me, [(patches, 0), (other, 0)], None, [window_ids, other_ids], gains_1, merge, [blocks_a],
    )
    acts_far = between(acts, True)
    contexts = []
    for m, ids in enumerate((window_ids, other_ids)):
        context = run_stage(
            "attention_1", [("att", 1, 0)], [(0, 0, False), (0, 1, False), (0, 2, False)],
            me, [(acts, 128 * m)], None, [ids], gains_1, merge, [blocks_b],
        )
        contexts.append(between(context, True))
    steps = [("out", 0), ("att", 0, 1), ("out", 4), ("att", 1, 5), ("out", 8), ("norm",)]
    loads = [(0, 3, True), (0, 0, False), (0, 1, False), (0, 2, False), (2, 0, True),
             (1, 0, False), (1, 1, False), (1, 2, False), (2, 1, True)]
    results = []
    for m, ids in enumerate((other_ids, window_ids)):
        results.append(
            run_stage(
                "sections_2_3", steps, loads, me, [(acts_far, 128 * m)], contexts[m], [ids],
                gains_2, merge, [blocks_a, blocks_b, blocks_c],
            )
        )
    back = between(results[0], False)
    return jnp.where(first, back, results[1])


def plain_section(acts, marks, gain, weight_qkv, weight_out):
    rows = acts.shape[0]
    values_f = acts.astype(jnp.float32)
    normed = normed_rows(values_f, gain).astype(jnp.bfloat16)
    qkv = jnp.dot(normed, weight_qkv, preferred_element_type=jnp.float32).astype(jnp.bfloat16)
    query, keys, vals = (
        qkv[:, i * WIDTH : (i + 1) * WIDTH].reshape(rows, HEADS, HEAD_DIM) for i in range(3)
    )
    scores = jnp.einsum(
        "qhd,khd->hqk", query, keys, preferred_element_type=jnp.float32
    ) * HEAD_DIM ** (-0.5)
    same = marks[:, None] == marks[None, :]
    scores = jnp.where(same[None], scores, jnp.float32(NEG))
    probs = jax.nn.softmax(scores, axis=-1).astype(jnp.bfloat16)
    context = jnp.einsum("hqk,khd->qhd", probs, vals, preferred_element_type=jnp.float32)
    context = context.astype(jnp.bfloat16).reshape(rows, WIDTH)
    update = jnp.dot(context, weight_out, preferred_element_type=jnp.float32)
    return (values_f + update).astype(jnp.bfloat16)


def plain_body(patches, window_ids, norm_gain, w_qkv, w_out, merge_gain):
    acts = patches
    for k in range(w_qkv.shape[0]):
        local_qkv, local_out, acts = lax.optimization_barrier((w_qkv[k], w_out[k], acts))
        weight_qkv = lax.all_gather(local_qkv, "dp", axis=0, tiled=True)
        weight_out = lax.all_gather(local_out, "dp", axis=0, tiled=True)
        acts = plain_section(acts, window_ids[0], norm_gain[k], weight_qkv, weight_out)
    final = normed_rows(acts.astype(jnp.float32), merge_gain).astype(jnp.bfloat16)
    return final.reshape(-1, 4 * D_VIS)


def body(patches, window_ids, norm_gain, w_qkv, w_out, merge_gain):
    staged = lax.axis_size("dp") == 8 and lax.axis_size("phase") % 4 == 0
    run = staged_body if staged else plain_body
    return run(patches, window_ids, norm_gain, w_qkv, w_out, merge_gain)


def solution(mesh):
    in_specs = (
        P(("dp", "phase"), None),
        P(("dp", "phase"), None),
        P(),
        P(None, "dp", None),
        P(None, "dp", None),
        P(),
    )
    out_specs = P(("dp", "phase"), None)
    return jax.shard_map(body, mesh=mesh, in_specs=in_specs, out_specs=out_specs, check_vma=False)
```

time: 224 us -> 161 us (0.72)
  waiting for transfers between devices: 147 us -> 44.3 us
  Pallas kernels: 0 us -> 59.5 us
  matrix products: 32.8 us -> 0 us
  local copies, waits for them, and re-layouts: 6.75 us -> 20.6 us
  between operations: 13.5 us -> 0.41 us
  starting transfers between devices: 21.5 us -> 32.5 us
    all_gather x2 -> x0, waiting for transfers between devices: 69.5 us -> none  [the longest x1 41.7 us: body(): lax.all_gather(local_qkv, 'dp', axis=0, tiled=True)]
    pallas_call x0 -> x5, Pallas kernels: none -> 59.5 us  [run_stage(): pl.pallas_call(kernel, out_shape=jax.ShapeDtypeStruct(shape, jnp.bfloat16...]
    ppermute x15 -> x33, waiting for transfers between devices: 77.3 us -> 44.3 us  [the longest x27 33.9 us: swap(): return lax.ppermute(block, 'dp', [(j, j ^ bit) for j in range(size)])]
    dot_general x16 -> x0, matrix products: 31.3 us -> none  [the longest x4 13.4 us: section(): jnp.dot(normed, weight_qkv, preferred_element_type=jnp.float32)]
    ppermute x15 -> x33, starting transfers between devices: 21.5 us -> 32.5 us  [the longest x27 17.9 us: swap(): return lax.ppermute(block, 'dp', [(j, j ^ bit) for j in range(size)])]
    another operation x7 -> x4, local copies, waits for them, and re-layouts: 0.03 us -> 5.94 us  [unit_out(): return block.reshape(80, 2, WIDTH).transpose(1, 0, 2).reshape(160, WIDTH)]
    unnamed x8 -> x28, local copies, waits for them, and re-layouts: 0.02 us -> 5.69 us
    slice x16 -> x8, local copies, waits for them, and re-layouts: 2.21 us -> 4.99 us  [the longest x1 1.94 us: staged_body(): chunk_c = jnp.stack([unit_out(w_out[2]), unit_out(w_out[3])])]
  transfers between devices with their start and end apart: 17 -> 33, of which waited for: 10 -> 7; matrix products, arithmetic and copies ran while one was open for 1% -> 8% of each run, Pallas kernels for 0% -> 37%
where the time goes in v1:
time: 161 us; the launch traced here: 160 us
  Pallas kernels  59.5 us (37%)
  waiting for transfers between devices  44.3 us (28%)
  starting transfers between devices  32.5 us (20%)
  local copies, waits for them, and re-layouts  20.6 us (13%)
  other arithmetic  2.57 us (2%)
    pallas_call x5, Pallas kernels, run_stage(): pl.pallas_call(kernel, out_shape=jax.ShapeDtypeStruct(shape, jnp.bfloat16...  59.5 us
    ppermute x27, waiting for transfers between devices, swap(): return lax.ppermute(block, 'dp', [(j, j ^ bit) for j in range(size)])  33.9 us
    ppermute x27, starting transfers between devices, swap(): return lax.ppermute(block, 'dp', [(j, j ^ bit) for j in range(size)])  17.9 us
    ppermute x5, starting transfers between devices, between(): return lax.ppermute(block, 'phase', pairs)  13.1 us
    ppermute x5, waiting for transfers between devices, between(): return lax.ppermute(block, 'phase', pairs)  8.42 us
    another operation x4, local copies, waits for them, and re-layouts, unit_out(): return block.reshape(80, 2, WIDTH).transpose(1, 0, 2).reshape(160, WIDTH)  5.94 us
    unnamed x28, local copies, waits for them, and re-layouts  5.69 us
  transfers between devices with their start and end apart: 33, of which 7 were waited for; matrix products, arithmetic and copies ran while one was open for 8% of the time, Pallas kernels for 37%

profile of v1, /device:TPU:0, one launch (start us, length us, event | category | flops | bytes accessed | tf_op | source)
XLA Modules:
  0.0 159.8 jit_solution(10629783539372160155)
XLA Ops:
  0.0 1.9 %fusion = (bf16[1,80,1280]{2,1,0:T(8,128)(2,1)}, bf16[1,80,1280]{2,1,0:T(8,128)(2,1)S(1)}, bf16[1,80,1280]{2,1,0:T(8,128)(2,1)}) fusion(bf16[4,80,1280]{2,1,0:T(8,128)(2,1)} %param.10, s32[]{:T(128)S(6)} %select_n.33), kind=kLoop, calls=%fused_computation.8 | loop fusion | bytes 1228804 | tf_op jit(solution)/shard_map/slice | solution.py:215
  2.0 1.4 constant_dynamic-slice_fusion
  3.8 3.0 %collective-permute-start.3 = (bf16[4,160,640]{2,1,0:T(8,128)(2,1)S(1)}, bf16[4,160,640]{2,1,0:T(8,128)(2,1)S(1)}, u32[]{:S(2)}, u32[]{:S(2)}) collective-permute-start(bf16[4,160,640]{2,1,0:T(8,128)(2,1)S(1)} %pad_maximum_fusion.refs_7_.refs_6_), channel_id=1, source_target_pairs={{0,16},{4,20},{8,24},{12,28},{16,0},{20,4},{24,8},{28,12},{1,17},{... | collective-permute-start | bytes 2457608 | tf_op jit(solution)/shard_map/ppermute | solution.py:187
  6.8 1.5 collective-permute-start.2
  8.3 4.2 %collective-permute-start = (bf16[128,1280]{1,0:T(8,128)(2,1)}, bf16[128,1280]{1,0:T(8,128)(2,1)}, u32[]{:S(2)}, u32[]{:S(2)}) collective-permute-start(bf16[128,1280]{1,0:T(8,128)(2,1)} %refs_1_.1), channel_id=1, source_target_pairs={{0,1},{3,2},{4,5},{7,6},{8,9},{11,10},{12,13},{15,14},{16,17},{19,... | collective-permute-start | bytes 983048 | tf_op jit(solution)/shard_map/ppermute | solution.py:193
  14.7 10.3 %collective-permute-done.3.refs_9_.refs_8_ = bf16[4,160,640]{2,1,0:T(8,128)(2,1)S(1)} collective-permute-done((bf16[4,160,640]{2,1,0:T(8,128)(2,1)S(1)}, bf16[4,160,640]{2,1,0:T(8,128)(2,1)S(1)}, u32[]{:S(2)}, u32[]{:S(2)}) %collective-permute-start.3) | collective-permute-done | bytes 819232 | tf_op jit(solution)/shard_map/ppermute | solution.py:187
  25.1 1.5 collective-permute-done.2.refs_8_.refs_7_
  27.8 1.6 %collective-permute-start.12 = (bf16[3,160,640]{2,1,0:T(8,128)(2,1)S(1)}, bf16[3,160,640]{2,1,0:T(8,128)(2,1)S(1)}, u32[]{:S(2)}, u32[]{:S(2)}) collective-permute-start(bf16[3,160,640]{2,1,0:T(8,128)(2,1)S(1)} %bitcast.16), channel_id=1, source_target_pairs={{0,8},{4,12},{8,0},{12,4},{16,24},{20,28},{24,16},{28,20},{1,9},{5... | collective-permute-start | bytes 1843208 | tf_op jit(solution)/shard_map/ppermute | solution.py:187
  29.4 1.6 collective-permute-start.1
  31.1 1.9 %collective-permute-done.1.refs_4_.refs_3_.refs_2_ = s32[1,128]{1,0:T(1,128)S(1)} collective-permute-done((s32[1,128]{1,0:T(1,128)S(1)}, s32[1,128]{1,0:T(1,128)S(1)}, u32[]{:S(2)}, u32[]{:S(2)}) %collective-permute-start.1) | collective-permute-done | bytes 544 | tf_op jit(solution)/shard_map/ppermute | solution.py:221
  34.4 1.7 %collective-permute-start.4 = (bf16[4,80,640]{2,1,0:T(8,128)(2,1)S(1)}, bf16[4,80,640]{2,1,0:T(8,128)(2,1)}, u32[]{:S(2)}, u32[]{:S(2)}) collective-permute-start(bf16[4,80,640]{2,1,0:T(8,128)(2,1)S(1)} %slice.31), channel_id=1, source_target_pairs={{0,16},{4,20},{8,24},{12,28},{16,0},{20,4},{24,8},{28,12},{1,17},{... | collective-permute-start | bytes 1228808 | tf_op jit(solution)/shard_map/ppermute | solution.py:187
  36.2 14.9 %collective-permute-done.5.refs_11_.refs_10_ = bf16[4,80,640]{2,1,0:T(8,128)(2,1)S(1)} collective-permute-done((bf16[4,80,640]{2,1,0:T(8,128)(2,1)S(1)}, bf16[4,80,640]{2,1,0:T(8,128)(2,1)S(1)}, u32[]{:S(2)}, u32[]{:S(2)}) %collective-permute-start.5) | collective-permute-done | bytes 409632 | tf_op jit(solution)/shard_map/ppermute | solution.py:187
  51.7 1.5 collective-permute-start.15
  54.0 1.4 collective-permute-start.14
  56.2 5.3 %collective-permute-done.15.refs_9_.refs_20_ = bf16[3,80,640]{2,1,0:T(8,128)(2,1)} collective-permute-done((bf16[3,80,640]{2,1,0:T(8,128)(2,1)S(1)}, bf16[3,80,640]{2,1,0:T(8,128)(2,1)}, u32[]{:S(2)}, u32[]{:S(2)}) %collective-permute-start.15) | collective-permute-done | bytes 307232 | tf_op jit(solution)/shard_map/ppermute | solution.py:187
  61.5 2.0 %collective-permute-done.14.refs_8_.refs_19_ = bf16[3,80,640]{2,1,0:T(8,128)(2,1)} collective-permute-done((bf16[3,80,640]{2,1,0:T(8,128)(2,1)S(1)}, bf16[3,80,640]{2,1,0:T(8,128)(2,1)}, u32[]{:S(2)}, u32[]{:S(2)}) %collective-permute-start.14) | collective-permute-done | bytes 307232 | tf_op jit(solution)/shard_map/ppermute | solution.py:187
  63.5 1.7 %reshape_squeeze.6 = bf16[80,2,640]{2,1,0:T(2,128)(2,1)} reshape(bf16[1,80,1280]{2,1,0:T(8,128)(2,1)} %get-tuple-element.23) | data formatting | bytes 409600 | tf_op jit(solution)/shard_map/reshape;squeeze | solution.py:197
  65.1 1.6 %copy.12 = bf16[80,2,640]{2,0,1:T(8,128)(2,1)} copy(bf16[80,2,640]{2,1,0:T(2,128)(2,1)} %reshape_squeeze.6) | data formatting | bytes 409600 | tf_op jit(solution)/shard_map/reshape;squeeze | solution.py:197
  66.8 1.7 %reshape_squeeze.7 = bf16[80,2,640]{2,1,0:T(2,128)(2,1)} reshape(bf16[1,80,1280]{2,1,0:T(8,128)(2,1)} %get-tuple-element.25) | data formatting | bytes 409600 | tf_op jit(solution)/shard_map/reshape;squeeze | solution.py:197
  70.0 1.7 %pad_maximum_fusion.1.refs_26_ = bf16[2,160,640]{2,1,0:T(8,128)(2,1)} fusion(bf16[1,160,640]{2,1,0:T(8,128)(2,1)S(1)} %bitcast.25, bf16[1,160,640]{2,1,0:T(8,128)(2,1)} %bitcast.24), kind=kLoop, calls=%fused_computation.3 | loop fusion | flops 204800 | bytes 819200 | tf_op jit(solution)/shard_map/stack | solution.py:215
  72.2 1.4 collective-permute-start.23
  77.4 11.7 %section_0.1.refs_1_ = bf16[256,1280]{1,0:T(8,128)(2,1)S(1)} custom-call(s32[1]{0:T(128)} %bitcast.refs_0_, bf16[128,1280]{1,0:T(8,128)(2,1)} %refs_1_.1, bf16[128,1280]{1,0:T(8,128)(2,1)} %collective-permute-done.refs_2_, s32[1,128]{1,0:T(1,128)S(1)} %copy-done.11, s32[1,128]{1,0:T(1,128)S(1)} %collective-permute-done.1.refs_4_.refs_3_.refs_2_, ...), custom_call_target="tpu_custom_call" | custom-call | flops 1677721600 | bytes 6553600 | tf_op jit(solution)/shard_map/section_0/pallas_call | solution.py:164
  89.1 1.3 collective-permute-start.11
  90.4 6.2 %attention_1.2 = bf16[128,640]{1,0:T(8,128)(2,1)S(1)} custom-call(s32[1]{0:T(128)} %bitcast.refs_0_, bf16[256,1280]{1,0:T(8,128)(2,1)S(1)} %section_0.1.refs_1_, s32[1,128]{1,0:T(1,128)S(1)} %copy-done.11, f32[2,1,1280]{2,1,0:T(1,128)S(1)} %reshape.25.refs_5_.refs_3_, f32[1,1280]{1,0:T(1,128)S(1)} %reshape.26.refs_6_.refs_4_.refs_5_, ...), custom_call_target="tpu_custom_call" | custom-call | flops 629145600 | bytes 4915200 | tf_op jit(solution)/shard_map/attention_1/pallas_call | solution.py:164
  96.7 1.5 collective-permute-start.21
  100.1 1.6 collective-permute-start.25
  102.2 8.4 %collective-permute-done.21.refs_2_ = bf16[128,640]{1,0:T(8,128)(2,1)S(1)} collective-permute-done((bf16[128,640]{1,0:T(8,128)(2,1)S(1)}, bf16[128,640]{1,0:T(8,128)(2,1)S(1)}, u32[]{:S(2)}, u32[]{:S(2)}) %collective-permute-start.21) | collective-permute-done | bytes 163872 | tf_op jit(solution)/shard_map/ppermute | solution.py:193
  111.3 6.2 %attention_1.3 = bf16[128,640]{1,0:T(8,128)(2,1)S(1)} custom-call(s32[1]{0:T(128)} %bitcast.refs_0_, bf16[256,1280]{1,0:T(8,128)(2,1)S(1)} %section_0.1.refs_1_, s32[1,128]{1,0:T(1,128)S(1)} %collective-permute-done.1.refs_4_.refs_3_.refs_2_, f32[2,1,1280]{2,1,0:T(1,128)S(1)} %reshape.25.refs_5_.refs_3_, f32[1,1280]{1,0:T(1,128)S(1)} %reshape.26.refs_6_.refs_4_.refs_5_, ...), custom_call_target="tpu_custom_call" | custom-call | flops 629145600 | bytes 4915200 | tf_op jit(solution)/shard_map/attention_1/pallas_call | solution.py:164
  117.5 1.3 collective-permute-start.32
  118.9 17.7 %sections_2_3.2 = bf16[32,5120]{1,0:T(8,128)(2,1)S(1)} custom-call(s32[1]{0:T(128)} %bitcast.refs_0_, bf16[256,1280]{1,0:T(8,128)(2,1)S(1)} %collective-permute-done.11.refs_1_, bf16[128,640]{1,0:T(8,128)(2,1)S(1)} %collective-permute-done.21.refs_2_, s32[1,128]{1,0:T(1,128)S(1)} %collective-permute-done.1.refs_4_.refs_3_.refs_2_, ...), custom_call_target="tpu_custom_call" | custom-call | flops 1887436800 | bytes 14745600 | tf_op jit(solution)/shard_map/sections_2_3/pallas_call | solution.py:164
  136.6 4.8 %collective-permute-start.31 = (bf16[32,5120]{1,0:T(8,128)(2,1)S(1)}, bf16[32,5120]{1,0:T(8,128)(2,1)S(1)}, u32[]{:S(2)}, u32[]{:S(2)}) collective-permute-start(bf16[32,5120]{1,0:T(8,128)(2,1)S(1)} %sections_2_3.2), channel_id=1, source_target_pairs={{0,1},{3,2},{4,5},{7,6},{8,9},{11,10},{12,13},{15,14},{16,17},{19,... | collective-permute-start | bytes 983048 | tf_op jit(solution)/shard_map/ppermute | solution.py:193
  141.4 17.7 %sections_2_3.3 = bf16[32,5120]{1,0:T(8,128)(2,1)S(1)} custom-call(s32[1]{0:T(128)} %bitcast.refs_0_, bf16[256,1280]{1,0:T(8,128)(2,1)S(1)} %collective-permute-done.11.refs_1_, bf16[128,640]{1,0:T(8,128)(2,1)S(1)} %collective-permute-done.32.refs_2_, s32[1,128]{1,0:T(1,128)S(1)} %copy-done.11, f32[2,1,1280]{2,1,0:T(1,128)S(1)} %reshape.30.refs_4_, ...), custom_call_target="tpu_custom_call" | custom-call | flops 1887436800 | bytes 14745600 | tf_op jit(solution)/shard_map/sections_2_3/pallas_call | solution.py:164
  (92 shorter events, 17.3 us)
Async XLA Ops:
  3.8 21.3 %collective-permute-start.3 = (bf16[4,160,640]{2,1,0:T(8,128)(2,1)S(1)}, bf16[4,160,640]{2,1,0:T(8,128)(2,1)S(1)}, u32[]{:S(2)}, u32[]{:S(2)}) collective-permute-start(bf16[4,160,640]{2,1,0:T(8,128)(2,1)S(1)} %pad_maximum_fusion.refs_7_.refs_6_), channel_id=1, source_target_pairs={{0,16},{4,20},{8,24},{12,28},{16,0},{20,4},{24,8},{28,12},{1,17},{... | collective-permute-start | bytes 2457608 | tf_op jit(solution)/shard_map/ppermute | solution.py:187
  6.8 19.7 %collective-permute-start.2 = (bf16[4,160,640]{2,1,0:T(8,128)(2,1)S(1)}, bf16[4,160,640]{2,1,0:T(8,128)(2,1)S(1)}, u32[]{:S(2)}, u32[]{:S(2)}) collective-permute-start(bf16[4,160,640]{2,1,0:T(8,128)(2,1)S(1)} %pad_maximum_fusion.refs_7_.refs_6_), channel_id=1, source_target_pairs={{0,8},{4,12},{8,0},{12,4},{16,24},{20,28},{24,16},{28,20},{1,9},{5... | collective-permute-start | bytes 2457608 | tf_op jit(solution)/shard_map/ppermute | solution.py:187
  8.3 26.1 %collective-permute-start.6 = (bf16[4,160,640]{2,1,0:T(8,128)(2,1)S(1)}, bf16[4,160,640]{2,1,0:T(8,128)(2,1)}, u32[]{:S(2)}, u32[]{:S(2)}) collective-permute-start(bf16[4,160,640]{2,1,0:T(8,128)(2,1)S(1)} %pad_maximum_fusion.refs_7_.refs_6_), channel_id=1, source_target_pairs={{0,4},{4,0},{8,12},{12,8},{16,20},{20,16},{24,28},{28,24},{1,5},{5... | collective-permute-start | bytes 2457608 | tf_op jit(solution)/shard_map/ppermute | solution.py:187
  8.3 25.0 %collective-permute-start = (bf16[128,1280]{1,0:T(8,128)(2,1)}, bf16[128,1280]{1,0:T(8,128)(2,1)}, u32[]{:S(2)}, u32[]{:S(2)}) collective-permute-start(bf16[128,1280]{1,0:T(8,128)(2,1)} %refs_1_.1), channel_id=1, source_target_pairs={{0,1},{3,2},{4,5},{7,6},{8,9},{11,10},{12,13},{15,14},{16,17},{19,... | collective-permute-start | bytes 983048 | tf_op jit(solution)/shard_map/ppermute | solution.py:193
  27.4 23.6 %collective-permute-start.13 = (bf16[3,160,640]{2,1,0:T(8,128)(2,1)S(1)}, bf16[3,160,640]{2,1,0:T(8,128)(2,1)S(1)}, u32[]{:S(2)}, u32[]{:S(2)}) collective-permute-start(bf16[3,160,640]{2,1,0:T(8,128)(2,1)S(1)} %bitcast.15), channel_id=1, source_target_pairs={{0,16},{4,20},{8,24},{12,28},{16,0},{20,4},{24,8},{28,12},{1,17},{... | collective-permute-start | bytes 1843208 | tf_op jit(solution)/shard_map/ppermute | solution.py:187
  27.8 23.7 %collective-permute-start.12 = (bf16[3,160,640]{2,1,0:T(8,128)(2,1)S(1)}, bf16[3,160,640]{2,1,0:T(8,128)(2,1)S(1)}, u32[]{:S(2)}, u32[]{:S(2)}) collective-permute-start(bf16[3,160,640]{2,1,0:T(8,128)(2,1)S(1)} %bitcast.16), channel_id=1, source_target_pairs={{0,8},{4,12},{8,0},{12,4},{16,24},{20,28},{24,16},{28,20},{1,9},{5... | collective-permute-start | bytes 1843208 | tf_op jit(solution)/shard_map/ppermute | solution.py:187
  33.0 18.0 %collective-permute-start.5 = (bf16[4,80,640]{2,1,0:T(8,128)(2,1)S(1)}, bf16[4,80,640]{2,1,0:T(8,128)(2,1)S(1)}, u32[]{:S(2)}, u32[]{:S(2)}) collective-permute-start(bf16[4,80,640]{2,1,0:T(8,128)(2,1)S(1)} %slice.32), channel_id=1, source_target_pairs={{0,8},{4,12},{8,0},{12,4},{16,24},{20,28},{24,16},{28,20},{1,9},{5... | collective-permute-start | bytes 1228808 | tf_op jit(solution)/shard_map/ppermute | solution.py:187
  33.4 19.8 %collective-permute-start.16 = (bf16[3,160,640]{2,1,0:T(8,128)(2,1)S(1)}, bf16[3,160,640]{2,1,0:T(8,128)(2,1)S(1)}, u32[]{:S(2)}, u32[]{:S(2)}) collective-permute-start(bf16[3,160,640]{2,1,0:T(8,128)(2,1)S(1)} %bitcast.17), channel_id=1, source_target_pairs={{0,4},{4,0},{8,12},{12,8},{16,20},{20,16},{24,28},{28,24},{1,5},{5... | collective-permute-start | bytes 1843208 | tf_op jit(solution)/shard_map/ppermute | solution.py:187
  34.4 17.3 %collective-permute-start.4 = (bf16[4,80,640]{2,1,0:T(8,128)(2,1)S(1)}, bf16[4,80,640]{2,1,0:T(8,128)(2,1)}, u32[]{:S(2)}, u32[]{:S(2)}) collective-permute-start(bf16[4,80,640]{2,1,0:T(8,128)(2,1)S(1)} %slice.31), channel_id=1, source_target_pairs={{0,16},{4,20},{8,24},{12,28},{16,0},{20,4},{24,8},{28,12},{1,17},{... | collective-permute-start | bytes 1228808 | tf_op jit(solution)/shard_map/ppermute | solution.py:187
  51.0 4.4 %collective-permute-start.10 = (bf16[4,80,640]{2,1,0:T(8,128)(2,1)S(1)}, bf16[4,80,640]{2,1,0:T(8,128)(2,1)S(1)}, u32[]{:S(2)}, u32[]{:S(2)}) collective-permute-start(bf16[4,80,640]{2,1,0:T(8,128)(2,1)S(1)} %collective-permute-done.5.refs_11_.refs_10_), channel_id=1, source_target_pairs={{0,4},{4,0},{8,12},{12,8},{16,20},{20,16},{24,28},{28,24},{1,5},{5... | collective-permute-start | bytes 1228808 | tf_op jit(solution)/shard_map/ppermute | solution.py:187
  51.0 20.7 %collective-permute-start.7 = (bf16[4,160,640]{2,1,0:T(8,128)(2,1)}, bf16[4,160,640]{2,1,0:T(8,128)(2,1)}, u32[]{:S(2)}, u32[]{:S(2)}) collective-permute-start(bf16[4,160,640]{2,1,0:T(8,128)(2,1)} %copy-done), channel_id=1, source_target_pairs={{0,4},{4,0},{8,12},{12,8},{16,20},{20,16},{24,28},{28,24},{1,5},{5... | collective-permute-start | bytes 2457608 | tf_op jit(solution)/shard_map/ppermute | solution.py:187
  51.5 20.2 %collective-permute-start.8 = (bf16[4,160,640]{2,1,0:T(8,128)(2,1)S(1)}, bf16[4,160,640]{2,1,0:T(8,128)(2,1)}, u32[]{:S(2)}, u32[]{:S(2)}) collective-permute-start(bf16[4,160,640]{2,1,0:T(8,128)(2,1)S(1)} %collective-permute-done.3.refs_9_.refs_8_), channel_id=1, source_target_pairs={{0,4},{4,0},{8,12},{12,8},{16,20},{20,16},{24,28},{28,24},{1,5},{5... | collective-permute-start | bytes 2457608 | tf_op jit(solution)/shard_map/ppermute | solution.py:187
  51.7 9.8 %collective-permute-start.15 = (bf16[3,80,640]{2,1,0:T(8,128)(2,1)S(1)}, bf16[3,80,640]{2,1,0:T(8,128)(2,1)}, u32[]{:S(2)}, u32[]{:S(2)}) collective-permute-start(bf16[3,80,640]{2,1,0:T(8,128)(2,1)S(1)} %slice.34), channel_id=1, source_target_pairs={{0,8},{4,12},{8,0},{12,4},{16,24},{20,28},{24,16},{28,20},{1,9},{5... | collective-permute-start | bytes 921608 | tf_op jit(solution)/shard_map/ppermute | solution.py:187
  54.0 9.4 %collective-permute-start.14 = (bf16[3,80,640]{2,1,0:T(8,128)(2,1)S(1)}, bf16[3,80,640]{2,1,0:T(8,128)(2,1)}, u32[]{:S(2)}, u32[]{:S(2)}) collective-permute-start(bf16[3,80,640]{2,1,0:T(8,128)(2,1)S(1)} %slice.33), channel_id=1, source_target_pairs={{0,16},{4,20},{8,24},{12,28},{16,0},{20,4},{24,8},{28,12},{1,17},{... | collective-permute-start | bytes 921608 | tf_op jit(solution)/shard_map/ppermute | solution.py:187
  56.2 13.2 %collective-permute-start.9 = (bf16[4,80,640]{2,1,0:T(8,128)(2,1)}, bf16[4,80,640]{2,1,0:T(8,128)(2,1)}, u32[]{:S(2)}, u32[]{:S(2)}) collective-permute-start(bf16[4,80,640]{2,1,0:T(8,128)(2,1)} %collective-permute-done.4.refs_10_.refs_9_), channel_id=1, source_target_pairs={{0,4},{4,0},{8,12},{12,8},{16,20},{20,16},{24,28},{28,24},{1,5},{5... | collective-permute-start | bytes 1228808 | tf_op jit(solution)/shard_map/ppermute | solution.py:187
  61.5 10.7 %collective-permute-start.20 = (bf16[3,80,640]{2,1,0:T(8,128)(2,1)}, bf16[3,80,640]{2,1,0:T(8,128)(2,1)}, u32[]{:S(2)}, u32[]{:S(2)}) collective-permute-start(bf16[3,80,640]{2,1,0:T(8,128)(2,1)} %collective-permute-done.15.refs_9_.refs_20_), channel_id=1, source_target_pairs={{0,4},{4,0},{8,12},{12,8},{16,20},{20,16},{24,28},{28,24},{1,5},{5... | collective-permute-start | bytes 921608 | tf_op jit(solution)/shard_map/ppermute | solution.py:187
  63.5 10.2 %collective-permute-start.19 = (bf16[3,80,640]{2,1,0:T(8,128)(2,1)}, bf16[3,80,640]{2,1,0:T(8,128)(2,1)}, u32[]{:S(2)}, u32[]{:S(2)}) collective-permute-start(bf16[3,80,640]{2,1,0:T(8,128)(2,1)} %collective-permute-done.14.refs_8_.refs_19_), channel_id=1, source_target_pairs={{0,4},{4,0},{8,12},{12,8},{16,20},{20,16},{24,28},{28,24},{1,5},{5... | collective-permute-start | bytes 921608 | tf_op jit(solution)/shard_map/ppermute | solution.py:187
  69.4 19.7 %collective-permute-start.17 = (bf16[3,160,640]{2,1,0:T(8,128)(2,1)S(1)}, bf16[3,160,640]{2,1,0:T(8,128)(2,1)}, u32[]{:S(2)}, u32[]{:S(2)}) collective-permute-start(bf16[3,160,640]{2,1,0:T(8,128)(2,1)S(1)} %collective-permute-done.12.refs_6_.refs_17_), channel_id=1, source_target_pairs={{0,4},{4,0},{8,12},{12,8},{16,20},{20,16},{24,28},{28,24},{1,5},{5... | collective-permute-start | bytes 1843208 | tf_op jit(solution)/shard_map/ppermute | solution.py:187
  71.7 18.7 %collective-permute-start.18 = (bf16[3,160,640]{2,1,0:T(8,128)(2,1)S(1)}, bf16[3,160,640]{2,1,0:T(8,128)(2,1)}, u32[]{:S(2)}, u32[]{:S(2)}) collective-permute-start(bf16[3,160,640]{2,1,0:T(8,128)(2,1)S(1)} %collective-permute-done.13.refs_7_.refs_18_), channel_id=1, source_target_pairs={{0,4},{4,0},{8,12},{12,8},{16,20},{20,16},{24,28},{28,24},{1,5},{5... | collective-permute-start | bytes 1843208 | tf_op jit(solution)/shard_map/ppermute | solution.py:187
  71.7 30.5 %collective-permute-start.26 = (bf16[2,160,640]{2,1,0:T(8,128)(2,1)}, bf16[2,160,640]{2,1,0:T(8,128)(2,1)}, u32[]{:S(2)}, u32[]{:S(2)}) collective-permute-start(bf16[2,160,640]{2,1,0:T(8,128)(2,1)} %pad_maximum_fusion.1.refs_26_), channel_id=1, source_target_pairs={{0,4},{4,0},{8,12},{12,8},{16,20},{20,16},{24,28},{28,24},{1,5},{5... | collective-permute-start | bytes 1228808 | tf_op jit(solution)/shard_map/ppermute | solution.py:187
  72.2 25.9 %collective-permute-start.23 = (bf16[2,160,640]{2,1,0:T(8,128)(2,1)}, bf16[2,160,640]{2,1,0:T(8,128)(2,1)}, u32[]{:S(2)}, u32[]{:S(2)}) collective-permute-start(bf16[2,160,640]{2,1,0:T(8,128)(2,1)} %pad_maximum_fusion.1.refs_26_), channel_id=1, source_target_pairs={{0,16},{4,20},{8,24},{12,28},{16,0},{20,4},{24,8},{28,12},{1,17},{... | collective-permute-start | bytes 1228808 | tf_op jit(solution)/shard_map/ppermute | solution.py:187
  73.6 24.5 %collective-permute-start.22 = (bf16[2,160,640]{2,1,0:T(8,128)(2,1)}, bf16[2,160,640]{2,1,0:T(8,128)(2,1)}, u32[]{:S(2)}, u32[]{:S(2)}) collective-permute-start(bf16[2,160,640]{2,1,0:T(8,128)(2,1)} %pad_maximum_fusion.1.refs_26_), channel_id=1, source_target_pairs={{0,8},{4,12},{8,0},{12,4},{16,24},{20,28},{24,16},{28,20},{1,9},{5... | collective-permute-start | bytes 1228808 | tf_op jit(solution)/shard_map/ppermute | solution.py:187
  89.1 28.4 %collective-permute-start.11 = (bf16[256,1280]{1,0:T(8,128)(2,1)S(1)}, bf16[256,1280]{1,0:T(8,128)(2,1)S(1)}, u32[]{:S(2)}, u32[]{:S(2)}) collective-permute-start(bf16[256,1280]{1,0:T(8,128)(2,1)S(1)} %section_0.1.refs_1_), channel_id=1, source_target_pairs={{1,0},{2,3},{5,4},{6,7},{9,8},{10,11},{13,12},{14,15},{17,16},{18,... | collective-permute-start | bytes 1966088 | tf_op jit(solution)/shard_map/ppermute | solution.py:193
  96.7 14.0 %collective-permute-start.21 = (bf16[128,640]{1,0:T(8,128)(2,1)S(1)}, bf16[128,640]{1,0:T(8,128)(2,1)S(1)}, u32[]{:S(2)}, u32[]{:S(2)}) collective-permute-start(bf16[128,640]{1,0:T(8,128)(2,1)S(1)} %attention_1.2), channel_id=1, source_target_pairs={{1,0},{2,3},{5,4},{6,7},{9,8},{10,11},{13,12},{14,15},{17,16},{18,... | collective-permute-start | bytes 491528 | tf_op jit(solution)/shard_map/ppermute | solution.py:193
  100.1 10.6 %collective-permute-start.25 = (bf16[2,80,640]{2,1,0:T(8,128)(2,1)S(1)}, bf16[2,80,640]{2,1,0:T(8,128)(2,1)S(1)}, u32[]{:S(2)}, u32[]{:S(2)}) collective-permute-start(bf16[2,80,640]{2,1,0:T(8,128)(2,1)S(1)} %slice.39), channel_id=1, source_target_pairs={{0,8},{4,12},{8,0},{12,4},{16,24},{20,28},{24,16},{28,20},{1,9},{5... | collective-permute-start | bytes 614408 | tf_op jit(solution)/shard_map/ppermute | solution.py:187
  101.6 9.5 %collective-permute-start.24 = (bf16[2,80,640]{2,1,0:T(8,128)(2,1)S(1)}, bf16[2,80,640]{2,1,0:T(8,128)(2,1)S(1)}, u32[]{:S(2)}, u32[]{:S(2)}) collective-permute-start(bf16[2,80,640]{2,1,0:T(8,128)(2,1)S(1)} %slice.38), channel_id=1, source_target_pairs={{0,16},{4,20},{8,24},{12,28},{16,0},{20,4},{24,8},{28,12},{1,17},{... | collective-permute-start | bytes 614408 | tf_op jit(solution)/shard_map/ppermute | solution.py:187
  102.2 16.6 %collective-permute-start.27 = (bf16[2,160,640]{2,1,0:T(8,128)(2,1)}, bf16[2,160,640]{2,1,0:T(8,128)(2,1)S(1)}, u32[]{:S(2)}, u32[]{:S(2)}) collective-permute-start(bf16[2,160,640]{2,1,0:T(8,128)(2,1)} %collective-permute-done.22.refs_27_), channel_id=1, source_target_pairs={{0,4},{4,0},{8,12},{12,8},{16,20},{20,16},{24,28},{28,24},{1,5},{5... | collective-permute-start | bytes 1228808 | tf_op jit(solution)/shard_map/ppermute | solution.py:187
  110.6 8.2 %collective-permute-start.28 = (bf16[2,160,640]{2,1,0:T(8,128)(2,1)}, bf16[2,160,640]{2,1,0:T(8,128)(2,1)S(1)}, u32[]{:S(2)}, u32[]{:S(2)}) collective-permute-start(bf16[2,160,640]{2,1,0:T(8,128)(2,1)} %collective-permute-done.23.refs_28_), channel_id=1, source_target_pairs={{0,4},{4,0},{8,12},{12,8},{16,20},{20,16},{24,28},{28,24},{1,5},{5... | collective-permute-start | bytes 1228808 | tf_op jit(solution)/shard_map/ppermute | solution.py:187
  110.7 8.2 %collective-permute-start.30 = (bf16[2,80,640]{2,1,0:T(8,128)(2,1)S(1)}, bf16[2,80,640]{2,1,0:T(8,128)(2,1)S(1)}, u32[]{:S(2)}, u32[]{:S(2)}) collective-permute-start(bf16[2,80,640]{2,1,0:T(8,128)(2,1)S(1)} %collective-permute-done.25.refs_30_), channel_id=1, source_target_pairs={{0,4},{4,0},{8,12},{12,8},{16,20},{20,16},{24,28},{28,24},{1,5},{5... | collective-permute-start | bytes 614408 | tf_op jit(solution)/shard_map/ppermute | solution.py:187
  111.2 7.7 %collective-permute-start.29 = (bf16[2,80,640]{2,1,0:T(8,128)(2,1)S(1)}, bf16[2,80,640]{2,1,0:T(8,128)(2,1)S(1)}, u32[]{:S(2)}, u32[]{:S(2)}) collective-permute-start(bf16[2,80,640]{2,1,0:T(8,128)(2,1)S(1)} %collective-permute-done.24.refs_29_), channel_id=1, source_target_pairs={{0,4},{4,0},{8,12},{12,8},{16,20},{20,16},{24,28},{28,24},{1,5},{5... | collective-permute-start | bytes 614408 | tf_op jit(solution)/shard_map/ppermute | solution.py:187
  117.5 23.8 %collective-permute-start.32 = (bf16[128,640]{1,0:T(8,128)(2,1)S(1)}, bf16[128,640]{1,0:T(8,128)(2,1)S(1)}, u32[]{:S(2)}, u32[]{:S(2)}) collective-permute-start(bf16[128,640]{1,0:T(8,128)(2,1)S(1)} %attention_1.3), channel_id=1, source_target_pairs={{1,0},{2,3},{5,4},{6,7},{9,8},{10,11},{13,12},{14,15},{17,16},{18,... | collective-permute-start | bytes 491528 | tf_op jit(solution)/shard_map/ppermute | solution.py:193
  136.6 22.5 %collective-permute-start.31 = (bf16[32,5120]{1,0:T(8,128)(2,1)S(1)}, bf16[32,5120]{1,0:T(8,128)(2,1)S(1)}, u32[]{:S(2)}, u32[]{:S(2)}) collective-permute-start(bf16[32,5120]{1,0:T(8,128)(2,1)S(1)} %sections_2_3.2), channel_id=1, source_target_pairs={{0,1},{3,2},{4,5},{7,6},{8,9},{11,10},{12,13},{15,14},{16,17},{19,... | collective-permute-start | bytes 983048 | tf_op jit(solution)/shard_map/ppermute | solution.py:193
  (15 other events, 159.3 us)

commit v2 on v1

v2 whole, which is shorter than its diff:
```python
import functools

import jax
import jax.numpy as jnp
from jax import lax
from jax.experimental import pallas as pl
from jax.experimental.pallas import tpu as pltpu
from jax.sharding import PartitionSpec as P

D_VIS = 1280
HEADS = 8
HEAD_DIM = 80
WIDTH = HEADS * HEAD_DIM
SECTIONS = 4
LANES = 128
EPS = 1e-06
NEG = -1e30


def normed_rows(values, gain):
    scale = lax.rsqrt(jnp.mean(values * values, axis=-1, keepdims=True) + EPS)
    return values * scale * gain


def attend(qkv, row_ids):
    query, keys, vals = qkv
    rows = query.shape[0]
    across = jnp.broadcast_to(row_ids, (rows, rows))
    same = across == across.T
    lane = lax.broadcasted_iota(jnp.int32, (rows, LANES), 1)
    tiles = [None] * (WIDTH // LANES)
    for head in range(HEADS):
        first, last = head * HEAD_DIM, (head + 1) * HEAD_DIM
        low, high = first // LANES, -(-last // LANES)
        span = slice(low * LANES, high * LANES)
        inside = []
        for tile in range(low, high):
            place = lane + tile * LANES
            inside.append((place >= first) & (place < last))
        part = jnp.concatenate(
            [
                jnp.where(mask, query[:, (low + i) * LANES : (low + i + 1) * LANES], 0)
                for i, mask in enumerate(inside)
            ],
            axis=1,
        )
        scores = lax.dot_general(
            part, keys[:, span], (((1,), (1,)), ((), ())), preferred_element_type=jnp.float32
        )
        scores = jnp.where(same, scores * HEAD_DIM ** (-0.5), NEG)
        weights = jnp.exp(scores - jnp.max(scores, axis=-1, keepdims=True))
        probs = weights * (1.0 / jnp.sum(weights, axis=-1, keepdims=True))
        mixed = jnp.dot(
            probs.astype(jnp.bfloat16), vals[:, span], preferred_element_type=jnp.float32
        )
        for i, mask in enumerate(inside):
            kept = jnp.where(mask, mixed[:, i * LANES : (i + 1) * LANES], 0.0)
            tile = low + i
            tiles[tile] = kept if tiles[tile] is None else tiles[tile] + kept
    return jnp.concatenate(tiles, axis=1).astype(jnp.bfloat16)


def stage_kernel(steps, n_weights, micros, acts_parts, with_ctx, *refs):
    refs = list(refs)
    acts_refs = [refs.pop(0) for _ in acts_parts]
    ctx_ref = refs.pop(0) if with_ctx else None
    ids_refs = [refs.pop(0) for _ in range(micros)]
    gain_ref = refs.pop(0)
    merge_ref = refs.pop(0)
    held = [refs.pop(0) for _ in range(n_weights)]
    sheets, flow = refs.pop(), refs.pop()
    out_refs = refs

    rows = 128
    for m, (ref, row) in enumerate(zip(acts_refs, acts_parts)):
        flow[m * rows : (m + 1) * rows] = ref[row : row + rows].astype(jnp.float32)
    ctx = ctx_ref[...] if with_ctx else None
    for step in steps:
        if step[0] == "att":
            normed = normed_rows(flow[...], gain_ref[step[1]]).astype(jnp.bfloat16)
            qkv = [
                jnp.dot(
                    normed, held[step[2]][step[3] + i], preferred_element_type=jnp.float32
                ).astype(jnp.bfloat16)
                for i in range(3)
            ]
            parts = [
                attend([part[m * rows : (m + 1) * rows] for part in qkv], ids_refs[m][...])
                for m in range(micros)
            ]
            ctx = parts[0] if micros == 1 else jnp.concatenate(parts, axis=0)
        elif step[0] == "out":
            for half in range(2):
                at = slice(half * WIDTH, (half + 1) * WIDTH)
                moved = jnp.dot(
                    ctx, held[step[1]][step[2], half * WIDTH : (half + 1) * WIDTH],
                    preferred_element_type=jnp.float32,
                )
                flow[:, at] = (flow[:, at] + moved).astype(jnp.bfloat16).astype(jnp.float32)
        else:
            final = normed_rows(flow[...], merge_ref[...])
            for tile in range(D_VIS // LANES):
                sheets[tile] = final[:, tile * LANES : (tile + 1) * LANES]
            for i in range(4):
                for tile in range(D_VIS // LANES):
                    at = i * D_VIS + tile * LANES
                    out_refs[0][:, at : at + LANES] = sheets[
                        tile, pl.ds(i, rows // 4, stride=4), :
                    ].astype(jnp.bfloat16)
    if steps[-1][0] == "att":
        out_refs[-1][...] = ctx
    if steps[-1][0] != "norm" and len(steps) > 1:
        out_refs[0][...] = flow[...].astype(jnp.bfloat16)


def run_stage(name, steps, acts, ctx, ids, gains, merge, weights):
    micros = len(acts)
    rows = 128
    shapes = []
    if steps[-1][0] == "norm":
        shapes.append((rows // 4, 4 * D_VIS))
    elif len(steps) > 1:
        shapes.append((micros * rows, D_VIS))
    if steps[-1][0] == "att":
        shapes.append((micros * rows, WIDTH))
    kernel = functools.partial(
        stage_kernel, steps, len(weights), micros, [row for _, row in acts], ctx is not None
    )
    vmem = pl.BlockSpec(memory_space=pltpu.VMEM)
    args = [a for a, _ in acts] + ([ctx] if ctx is not None else []) + list(ids)
    args += [gains, merge] + list(weights)
    units = sum({"att": 3, "out": 1, "norm": 0}[step[0]] for step in steps)
    return pl.pallas_call(
        kernel,
        out_shape=[jax.ShapeDtypeStruct(shape, jnp.bfloat16) for shape in shapes],
        in_specs=[vmem] * len(args),
        out_specs=[vmem] * len(shapes),
        scratch_shapes=[
            pltpu.VMEM((micros * rows, D_VIS), jnp.float32),
            pltpu.VMEM((D_VIS // LANES, rows, LANES), jnp.float32),
        ],
        compiler_params=pltpu.CompilerParams(vmem_limit_bytes=8 * 1024 * 1024),
        cost_estimate=pl.CostEstimate(
            flops=2 * micros * rows * D_VIS * WIDTH * units,
            bytes_accessed=units * D_VIS * WIDTH * 2,
            transcendentals=micros * rows * rows * HEADS,
        ),
        name=name,
    )(*args)


def assemble_kernel(units, outs, pieces, *refs):
    whole = refs[-1]
    me = lax.axis_index("dp")
    for (first, distance, start, size), block in zip(pieces, refs[:-1]):
        owner = jnp.bitwise_xor(me, distance)
        for unit in range(units):
            if unit not in outs:
                where = pl.multiple_of(owner * 160 + start, 16)
                whole[unit, pl.ds(where, size)] = block[first + unit]
            else:
                for half in range(start // 80, (start + size) // 80):
                    where = pl.multiple_of(owner * 80 + half * WIDTH, 16)
                    at = half * 80 - start
                    whole[unit, pl.ds(where, 80)] = block[first + unit, at : at + 80]


def assemble(name, units, outs, pieces):
    vmem = pl.BlockSpec(memory_space=pltpu.VMEM)
    return pl.pallas_call(
        functools.partial(assemble_kernel, units, outs, [piece[1:] for piece in pieces]),
        out_shape=jax.ShapeDtypeStruct((units, D_VIS, WIDTH), jnp.bfloat16),
        in_specs=[vmem] * len(pieces),
        out_specs=vmem,
        compiler_params=pltpu.CompilerParams(vmem_limit_bytes=8 * 1024 * 1024),
        name=name,
    )(*[piece[0] for piece in pieces])


def first_stage():
    place = lax.axis_index("phase") % 4
    return (place == 1) | (place == 2)


def pack_kernel(qkv, out, chunk_a, chunk_b, chunk_c, chunks):
    first = first_stage()
    picks = [jnp.where(first, one, two) for one, two in ((0, 2), (0, 1), (1, 3))]
    for i in range(3):
        at = slice(i * WIDTH, (i + 1) * WIDTH)
        chunk_a[i] = qkv[picks[0], :, at]
        chunk_b[i] = qkv[picks[2], :, at]
    for half in range(2):
        at = slice(half * WIDTH, (half + 1) * WIDTH)
        to = slice(half * 80, (half + 1) * 80)
        chunk_a[3, to] = out[picks[1], :, at]
        chunk_c[0, to] = out[2, :, at]
        chunk_c[1, to] = out[3, :, at]
    chunks[0:4] = chunk_a[...]
    chunks[4:7] = chunk_b[...]
    chunks[7:9] = chunk_c[...]


def pack(w_qkv, w_out):
    vmem = pl.BlockSpec(memory_space=pltpu.VMEM)
    return pl.pallas_call(
        pack_kernel,
        out_shape=[jax.ShapeDtypeStruct((n, 160, WIDTH), jnp.bfloat16) for n in (4, 3, 2, 9)],
        in_specs=[vmem] * 2,
        out_specs=[vmem] * 4,
        compiler_params=pltpu.CompilerParams(vmem_limit_bytes=8 * 1024 * 1024),
        name="pack",
    )(w_qkv, w_out)


def swap(block, bit):
    size = lax.axis_size("dp")
    return lax.ppermute(block, "dp", [(j, j ^ bit) for j in range(size)])


def across(block):
    size = lax.axis_size("phase")
    return lax.ppermute(block, "phase", [(j, j ^ 1) for j in range(size)])


def staged_body(patches, window_ids, norm_gain, w_qkv, w_out, merge_gain):
    tie = lax.optimization_barrier
    gains_1 = norm_gain[:2].reshape(2, 1, D_VIS)
    gains_2 = norm_gain[2:].reshape(2, 1, D_VIS)
    merge = merge_gain.reshape(1, D_VIS)

    def arranged(name, outs, own, own_other, first, x, y, d):
        pieces = [(own, 0, 0, 0, 160), (own_other, first, 1, 0, 160)]
        for distance, block, start in ((2, x, 0), (4, y, 0), (6, d[0], 0), (6, d[1], 80)):
            size = block.shape[1]
            pieces.append((block, 0, distance, start, size))
            pieces.append((swap(block, 1), 0, distance + 1, start, size))
        return assemble(name, own.shape[0], outs, pieces)

    chunk_a, chunk_b, chunk_c, chunks = pack(w_qkv, w_out)
    ax, ay = swap(chunk_a, 2), swap(chunk_a, 4)
    bx, by = swap(chunk_b, 2), swap(chunk_b, 4)
    other, other_ids = across(patches), across(window_ids)
    own_other = swap(chunks, 1)
    ax, ay, other, other_ids = tie((ax, ay, other, other_ids))
    ad = swap(ax[:, :80], 4), swap(ay[:, 80:], 2)
    bx, by, own_other = tie((bx, by, own_other))
    bd = swap(bx[:, :80], 4), swap(by[:, 80:], 2)

    weights_a = arranged("weights_a", (3,), chunk_a, own_other, 0, ax, ay, ad)
    acts = run_stage(
        "section_0", [("att", 0, 0, 0), ("out", 0, 3)], [(patches, 0), (other, 0)], None,
        [window_ids, other_ids], gains_1, merge, [weights_a],
    )[0]
    *bd, acts, chunk_c = tie((*bd, acts, chunk_c))
    cx, cy = swap(chunk_c, 2), swap(chunk_c, 4)
    weights_b = arranged("weights_b", (), chunk_b, own_other, 4, bx, by, bd)
    acts_far = across(acts)
    contexts = [
        run_stage(
            "attention_1", [("att", 1, 0, 0)], [(acts, 128 * m)], None, [ids], gains_1, merge,
            [weights_b],
        )[0]
        for m, ids in enumerate((window_ids, other_ids))
    ]
    contexts_far = [across(context) for context in contexts]
    cx, cy, _ = tie((cx, cy, contexts[1]))
    cd = swap(cx[:, :80], 4), swap(cy[:, 80:], 2)
    halfway = [
        run_stage(
            "section_2", [("out", 0, 3), ("att", 0, 0, 0)], [(acts_far, 128 * m)],
            contexts_far[m], [ids], gains_2, merge, [weights_a],
        )
        for m, ids in enumerate((other_ids, window_ids))
    ]
    weights_c = arranged("weights_c", (0, 1), chunk_c, own_other, 7, cx, cy, cd)
    results = [
        run_stage(
            "section_3", [("out", 1, 0), ("att", 1, 0, 0), ("out", 1, 1), ("norm",)],
            [(halfway[m][0], 0)], halfway[m][1], [ids], gains_2, merge, [weights_b, weights_c],
        )[0]
        for m, ids in enumerate((other_ids, window_ids))
    ]
    back = across(results[0])
    return jnp.where(first_stage(), back, results[1])


def plain_section(acts, marks, gain, weight_qkv, weight_out):
    rows = acts.shape[0]
    values_f = acts.astype(jnp.float32)
    normed = normed_rows(values_f, gain).astype(jnp.bfloat16)
    qkv = jnp.dot(normed, weight_qkv, preferred_element_type=jnp.float32).astype(jnp.bfloat16)
    query, keys, vals = (
        qkv[:, i * WIDTH : (i + 1) * WIDTH].reshape(rows, HEADS, HEAD_DIM) for i in range(3)
    )
    scores = jnp.einsum(
        "qhd,khd->hqk", query, keys, preferred_element_type=jnp.float32
    ) * HEAD_DIM ** (-0.5)
    same = marks[:, None] == marks[None, :]
    scores = jnp.where(same[None], scores, jnp.float32(NEG))
    probs = jax.nn.softmax(scores, axis=-1).astype(jnp.bfloat16)
    context = jnp.einsum("hqk,khd->qhd", probs, vals, preferred_element_type=jnp.float32)
    context = context.astype(jnp.bfloat16).reshape(rows, WIDTH)
    update = jnp.dot(context, weight_out, preferred_element_type=jnp.float32)
    return (values_f + update).astype(jnp.bfloat16)


def plain_body(patches, window_ids, norm_gain, w_qkv, w_out, merge_gain):
    acts = patches
    for k in range(w_qkv.shape[0]):
        local_qkv, local_out, acts = lax.optimization_barrier((w_qkv[k], w_out[k], acts))
        weight_qkv = lax.all_gather(local_qkv, "dp", axis=0, tiled=True)
        weight_out = lax.all_gather(local_out, "dp", axis=0, tiled=True)
        acts = plain_section(acts, window_ids[0], norm_gain[k], weight_qkv, weight_out)
    final = normed_rows(acts.astype(jnp.float32), merge_gain).astype(jnp.bfloat16)
    return final.reshape(-1, 4 * D_VIS)


def body(patches, window_ids, norm_gain, w_qkv, w_out, merge_gain):
    staged = lax.axis_size("dp") == 8 and lax.axis_size("phase") % 4 == 0
    run = staged_body if staged else plain_body
    return run(patches, window_ids, norm_gain, w_qkv, w_out, merge_gain)


def solution(mesh):
    in_specs = (
        P(("dp", "phase"), None),
        P(("dp", "phase"), None),
        P(),
        P(None, "dp", None),
        P(None, "dp", None),
        P(),
    )
    out_specs = P(("dp", "phase"), None)
    return jax.shard_map(body, mesh=mesh, in_specs=in_specs, out_specs=out_specs, check_vma=False)
```

time: 161 us -> 105 us (0.65)
  Pallas kernels: 59.5 us -> 24.9 us
  local copies, waits for them, and re-layouts: 20.6 us -> 7.49 us
  starting transfers between devices: 32.5 us -> 22.5 us
  waiting for transfers between devices: 44.3 us -> 48.4 us
  other arithmetic: 2.57 us -> 0.78 us
    pallas_call x5 -> x11, Pallas kernels: 59.5 us -> 24.9 us  [the longest x7 23.3 us: run_stage(): pl.pallas_call(kernel, out_shape=[jax.ShapeDtypeStruct(shape, jnp.bfloat1...]
    ppermute x6, starting transfers between devices: 14.6 us -> 7.56 us  [across(): return lax.ppermute(block, 'phase', [(j, j ^ 1) for j in range(size)])]
    another operation x4 -> x0, local copies, waits for them, and re-layouts: 5.94 us -> none  [unit_out(): return block.reshape(80, 2, WIDTH).transpose(1, 0, 2).reshape(160, WIDTH)]
    ppermute x6, waiting for transfers between devices: 10.3 us -> 15.4 us  [across(): return lax.ppermute(block, 'phase', [(j, j ^ 1) for j in range(size)])]
    slice x7 -> x6, local copies, waits for them, and re-layouts: 4.98 us -> 0.16 us  [the longest x2 0.07 us: staged_body(): ad = (swap(ax[:, :80], 4), swap(ay[:, 80:], 2))]
    ppermute x27 -> x25, starting transfers between devices: 17.9 us -> 14.9 us  [swap(): return lax.ppermute(block, 'dp', [(j, j ^ bit) for j in range(size)])]
    reshape x5 -> x0, local copies, waits for them, and re-layouts: 2.54 us -> none  [the longest x4 2.49 us: units_qkv(): return block.reshape(160, 3, WIDTH).transpose(1, 0, 2)]
    another operation x1 -> x0, other arithmetic: 1.72 us -> none  [staged_body(): chunk_c = jnp.stack([unit_out(w_out[2]), unit_out(w_out[3])])]
  transfers between devices with their start and end apart: 33 -> 31, of which waited for: 7 -> 13; matrix products, arithmetic and copies ran while one was open for 8% -> 0% of each run, Pallas kernels for 37% -> 24%
where the time goes in v2:
time: 105 us; the launch traced here: 104 us
  waiting for transfers between devices  48.4 us (46%)
  Pallas kernels  24.9 us (24%)
  starting transfers between devices  22.5 us (21%)
  local copies, waits for them, and re-layouts  7.49 us (7%)
    ppermute x25, waiting for transfers between devices, swap(): return lax.ppermute(block, 'dp', [(j, j ^ bit) for j in range(size)])  33 us
    pallas_call x7, Pallas kernels, run_stage(): pl.pallas_call(kernel, out_shape=[jax.ShapeDtypeStruct(shape, jnp.bfloat1...  23.3 us
    ppermute x6, waiting for transfers between devices, across(): return lax.ppermute(block, 'phase', [(j, j ^ 1) for j in range(size)])  15.4 us
    ppermute x25, starting transfers between devices, swap(): return lax.ppermute(block, 'dp', [(j, j ^ bit) for j in range(size)])  14.9 us
    ppermute x6, starting transfers between devices, across(): return lax.ppermute(block, 'phase', [(j, j ^ 1) for j in range(size)])  7.56 us
    unnamed x24, local copies, waits for them, and re-layouts  7.29 us
  transfers between devices with their start and end apart: 31, of which 13 were waited for; matrix products, arithmetic and copies ran while one was open for 0% of the time, Pallas kernels for 24%

profile of v2, /device:TPU:0, one launch (start us, length us, event | category | flops | bytes accessed | tf_op | source)
XLA Modules:
  0.0 104.3 jit_solution(2615798302194166398)
XLA Ops:
  0.0 1.7 %copy-done.6 = bf16[4,160,1920]{2,1,0:T(8,128)(2,1)S(1)} copy-done((bf16[4,160,1920]{2,1,0:T(8,128)(2,1)S(1)}, bf16[4,160,1920]{2,1,0:T(8,128)(2,1)}, u32[]{:S(2)}) %copy-start.6) | copy-done | bytes 2457624
  1.7 1.1 %copy-done.7 = bf16[4,80,1280]{2,1,0:T(8,128)(2,1)S(1)} copy-done((bf16[4,80,1280]{2,1,0:T(8,128)(2,1)S(1)}, bf16[4,80,1280]{2,1,0:T(8,128)(2,1)}, u32[]{:S(2)}) %copy-start.7) | copy-done | bytes 819224
  3.7 2.6 %collective-permute-start.6 = (bf16[4,160,640]{2,1,0:T(8,128)(2,1)S(1)}, bf16[4,160,640]{2,1,0:T(8,128)(2,1)S(1)}, u32[]{:S(2)}, u32[]{:S(2)}) collective-permute-start(bf16[4,160,640]{2,1,0:T(8,128)(2,1)S(1)} %get-tuple-element.30.refs_0_), channel_id=1, source_target_pairs={{0,16},{4,20},{8,24},{12,28},{16,0},{20,4},{24,8},{28,12},{1,17},{... | collective-permute-start | bytes 2457608 | tf_op jit(solution)/shard_map/ppermute | solution.py:217
  6.3 1.5 %collective-permute-start.5 = (bf16[4,160,640]{2,1,0:T(8,128)(2,1)S(1)}, bf16[4,160,640]{2,1,0:T(8,128)(2,1)S(1)}, u32[]{:S(2)}, u32[]{:S(2)}) collective-permute-start(bf16[4,160,640]{2,1,0:T(8,128)(2,1)S(1)} %get-tuple-element.30.refs_0_), channel_id=1, source_target_pairs={{0,8},{4,12},{8,0},{12,4},{16,24},{20,28},{24,16},{28,20},{1,9},{5... | collective-permute-start | bytes 2457608 | tf_op jit(solution)/shard_map/ppermute | solution.py:217
  8.3 1.6 %collective-permute-start.8 = (s32[1,128]{1,0:T(1,128)S(1)}, s32[1,128]{1,0:T(1,128)S(1)}, u32[]{:S(2)}, u32[]{:S(2)}) collective-permute-start(s32[1,128]{1,0:T(1,128)S(1)} %copy-done.9), channel_id=1, source_target_pairs={{0,1},{1,0},{2,3},{3,2},{4,5},{5,4},{6,7},{7,6},{8,9},{9,8},{10,11... | collective-permute-start | bytes 1544 | tf_op jit(solution)/shard_map/ppermute | solution.py:222
  9.9 2.0 %collective-permute-done.8.refs_3_.refs_2_.refs_1_ = s32[1,128]{1,0:T(1,128)S(1)} collective-permute-done((s32[1,128]{1,0:T(1,128)S(1)}, s32[1,128]{1,0:T(1,128)S(1)}, u32[]{:S(2)}, u32[]{:S(2)}) %collective-permute-start.8) | collective-permute-done | bytes 544 | tf_op jit(solution)/shard_map/ppermute | solution.py:222
  11.8 1.6 %collective-permute-start.7 = (bf16[128,1280]{1,0:T(8,128)(2,1)S(1)}, bf16[128,1280]{1,0:T(8,128)(2,1)S(1)}, u32[]{:S(2)}, u32[]{:S(2)}) collective-permute-start(bf16[128,1280]{1,0:T(8,128)(2,1)S(1)} %copy-done.8), channel_id=1, source_target_pairs={{0,1},{1,0},{2,3},{3,2},{4,5},{5,4},{6,7},{7,6},{8,9},{9,8},{10,11... | collective-permute-start | bytes 983048 | tf_op jit(solution)/shard_map/ppermute | solution.py:222
  13.4 6.8 %collective-permute-done.7.refs_1_ = bf16[128,1280]{1,0:T(8,128)(2,1)S(1)} collective-permute-done((bf16[128,1280]{1,0:T(8,128)(2,1)S(1)}, bf16[128,1280]{1,0:T(8,128)(2,1)S(1)}, u32[]{:S(2)}, u32[]{:S(2)}) %collective-permute-start.7) | collective-permute-done | bytes 327712 | tf_op jit(solution)/shard_map/ppermute | solution.py:222
  20.6 4.8 %collective-permute-done.6.refs_4_ = bf16[4,160,640]{2,1,0:T(8,128)(2,1)S(1)} collective-permute-done((bf16[4,160,640]{2,1,0:T(8,128)(2,1)S(1)}, bf16[4,160,640]{2,1,0:T(8,128)(2,1)S(1)}, u32[]{:S(2)}, u32[]{:S(2)}) %collective-permute-start.6) | collective-permute-done | bytes 819232 | tf_op jit(solution)/shard_map/ppermute | solution.py:217
  25.4 2.0 %collective-permute-done.5.refs_2_ = bf16[4,160,640]{2,1,0:T(8,128)(2,1)S(1)} collective-permute-done((bf16[4,160,640]{2,1,0:T(8,128)(2,1)S(1)}, bf16[4,160,640]{2,1,0:T(8,128)(2,1)S(1)}, u32[]{:S(2)}, u32[]{:S(2)}) %collective-permute-start.5) | collective-permute-done | bytes 819232 | tf_op jit(solution)/shard_map/ppermute | solution.py:217
  27.4 1.6 %collective-permute-start.13 = (bf16[4,80,640]{2,1,0:T(8,128)(2,1)S(1)}, bf16[4,80,640]{2,1,0:T(8,128)(2,1)S(1)}, u32[]{:S(2)}, u32[]{:S(2)}) collective-permute-start(bf16[4,80,640]{2,1,0:T(8,128)(2,1)S(1)} %slice.28), channel_id=1, source_target_pairs={{0,8},{4,12},{8,0},{12,4},{16,24},{20,28},{24,16},{28,20},{1,9},{5... | collective-permute-start | bytes 1228808 | tf_op jit(solution)/shard_map/ppermute | solution.py:217
  29.6 9.0 %collective-permute-done.1.refs_4_ = bf16[3,160,640]{2,1,0:T(8,128)(2,1)S(1)} collective-permute-done((bf16[3,160,640]{2,1,0:T(8,128)(2,1)S(1)}, bf16[3,160,640]{2,1,0:T(8,128)(2,1)S(1)}, u32[]{:S(2)}, u32[]{:S(2)}) %collective-permute-start.1) | collective-permute-done | bytes 614432 | tf_op jit(solution)/shard_map/ppermute | solution.py:217
  38.5 10.0 %collective-permute-done.13.refs_8_ = bf16[4,80,640]{2,1,0:T(8,128)(2,1)S(1)} collective-permute-done((bf16[4,80,640]{2,1,0:T(8,128)(2,1)S(1)}, bf16[4,80,640]{2,1,0:T(8,128)(2,1)S(1)}, u32[]{:S(2)}, u32[]{:S(2)}) %collective-permute-start.13) | collective-permute-done | bytes 409632 | tf_op jit(solution)/shard_map/ppermute | solution.py:217
  49.7 0.6 collective-permute-done.14.refs_9_
  50.9 1.5 %collective-permute-start.4 = (bf16[3,80,640]{2,1,0:T(8,128)(2,1)S(1)}, bf16[3,80,640]{2,1,0:T(8,128)(2,1)S(1)}, u32[]{:S(2)}, u32[]{:S(2)}) collective-permute-start(bf16[3,80,640]{2,1,0:T(8,128)(2,1)S(1)} %slice.25), channel_id=1, source_target_pairs={{0,8},{4,12},{8,0},{12,4},{16,24},{20,28},{24,16},{28,20},{1,9},{5... | collective-permute-start | bytes 921608 | tf_op jit(solution)/shard_map/ppermute | solution.py:217
  53.5 5.4 %section_0.1.refs_0_ = bf16[256,1280]{1,0:T(8,128)(2,1)S(1)} custom-call(bf16[128,1280]{1,0:T(8,128)(2,1)S(1)} %copy-done.8, bf16[128,1280]{1,0:T(8,128)(2,1)S(1)} %collective-permute-done.7.refs_1_, s32[1,128]{1,0:T(1,128)S(1)} %copy-done.9, s32[1,128]{1,0:T(1,128)S(1)} %collective-permute-done.8.refs_3_.refs_2_.refs_1_, ...), custom_call_target="tpu_custom_call" | custom-call | flops 1677721600 | bytes 6553600 | tf_op jit(solution)/shard_map/section_0/pallas_call | solution.py:133
  58.8 1.3 %collective-permute-done.4.refs_8_ = bf16[3,80,640]{2,1,0:T(8,128)(2,1)S(1)} collective-permute-done((bf16[3,80,640]{2,1,0:T(8,128)(2,1)S(1)}, bf16[3,80,640]{2,1,0:T(8,128)(2,1)S(1)}, u32[]{:S(2)}, u32[]{:S(2)}) %collective-permute-start.4) | collective-permute-done | bytes 307232 | tf_op jit(solution)/shard_map/ppermute | solution.py:217
  60.2 1.2 %collective-permute-done.3.refs_6_ = bf16[3,80,640]{2,1,0:T(8,128)(2,1)S(1)} collective-permute-done((bf16[3,80,640]{2,1,0:T(8,128)(2,1)S(1)}, bf16[3,80,640]{2,1,0:T(8,128)(2,1)S(1)}, u32[]{:S(2)}, u32[]{:S(2)}) %collective-permute-start.3) | collective-permute-done | bytes 307232 | tf_op jit(solution)/shard_map/ppermute | solution.py:217
  62.7 1.8 %collective-permute-start.15 = (bf16[256,1280]{1,0:T(8,128)(2,1)S(1)}, bf16[256,1280]{1,0:T(8,128)(2,1)S(1)}, u32[]{:S(2)}, u32[]{:S(2)}) collective-permute-start(bf16[256,1280]{1,0:T(8,128)(2,1)S(1)} %section_0.1.refs_0_), channel_id=1, source_target_pairs={{0,1},{1,0},{2,3},{3,2},{4,5},{5,4},{6,7},{7,6},{8,9},{9,8},{10,11... | collective-permute-start | bytes 1966088 | tf_op jit(solution)/shard_map/ppermute | solution.py:222
  65.0 2.2 %attention_1.2 = bf16[128,640]{1,0:T(8,128)(2,1)S(1)} custom-call(bf16[256,1280]{1,0:T(8,128)(2,1)S(1)} %section_0.1.refs_0_, s32[1,128]{1,0:T(1,128)S(1)} %copy-done.9, f32[2,1,1280]{2,1,0:T(1,128)S(1)} %reshape.9.refs_4_.refs_2_, f32[1,1280]{1,0:T(1,128)S(1)} %reshape.10.refs_5_.refs_3_.refs_4_, bf16[3,1280,640]{2,1,0:T(8,128)(2,1)S(1)} %weights_b.1.refs_4_.refs_5_), custom_call_target="tpu_custom_call" | custom-call | flops 629145600 | bytes 4915200 | tf_op jit(solution)/shard_map/attention_1/pallas_call | solution.py:133
  67.7 2.2 %attention_1.3 = bf16[128,640]{1,0:T(8,128)(2,1)S(1)} custom-call(bf16[256,1280]{1,0:T(8,128)(2,1)S(1)} %section_0.1.refs_0_, s32[1,128]{1,0:T(1,128)S(1)} %collective-permute-done.8.refs_3_.refs_2_.refs_1_, f32[2,1,1280]{2,1,0:T(1,128)S(1)} %reshape.9.refs_4_.refs_2_, f32[1,1280]{1,0:T(1,128)S(1)} %reshape.10.refs_5_.refs_3_.refs_4_, ...), custom_call_target="tpu_custom_call" | custom-call | flops 629145600 | bytes 4915200 | tf_op jit(solution)/shard_map/attention_1/pallas_call | solution.py:133
  69.9 3.4 %collective-permute-done.22.refs_4_ = bf16[2,160,640]{2,1,0:T(8,128)(2,1)S(1)} collective-permute-done((bf16[2,160,640]{2,1,0:T(8,128)(2,1)S(1)}, bf16[2,160,640]{2,1,0:T(8,128)(2,1)S(1)}, u32[]{:S(2)}, u32[]{:S(2)}) %collective-permute-start.22) | collective-permute-done | bytes 409632 | tf_op jit(solution)/shard_map/ppermute | solution.py:217
  74.0 1.7 %collective-permute-start.25 = (bf16[2,80,640]{2,1,0:T(8,128)(2,1)S(1)}, bf16[2,80,640]{2,1,0:T(8,128)(2,1)S(1)}, u32[]{:S(2)}, u32[]{:S(2)}) collective-permute-start(bf16[2,80,640]{2,1,0:T(8,128)(2,1)S(1)} %slice.30), channel_id=1, source_target_pairs={{0,16},{4,20},{8,24},{12,28},{16,0},{20,4},{24,8},{28,12},{1,17},{... | collective-permute-start | bytes 614408 | tf_op jit(solution)/shard_map/ppermute | solution.py:217
  75.7 6.6 %collective-permute-done.20.refs_1_ = bf16[128,640]{1,0:T(8,128)(2,1)S(1)} collective-permute-done((bf16[128,640]{1,0:T(8,128)(2,1)S(1)}, bf16[128,640]{1,0:T(8,128)(2,1)S(1)}, u32[]{:S(2)}, u32[]{:S(2)}) %collective-permute-start.20) | collective-permute-done | bytes 163872 | tf_op jit(solution)/shard_map/ppermute | solution.py:222
  83.0 1.8 %collective-permute-start.30 = (bf16[128,640]{1,0:T(8,128)(2,1)S(1)}, bf16[128,640]{1,0:T(8,128)(2,1)}, u32[]{:S(2)}, u32[]{:S(2)}) collective-permute-start(bf16[128,640]{1,0:T(8,128)(2,1)S(1)} %attention_1.3), channel_id=1, source_target_pairs={{0,1},{1,0},{2,3},{3,2},{4,5},{5,4},{6,7},{7,6},{8,9},{9,8},{10,11... | collective-permute-start | bytes 491528 | tf_op jit(solution)/shard_map/ppermute | solution.py:222
  84.8 2.9 %section_2.2 = (bf16[128,1280]{1,0:T(8,128)(2,1)S(1)}, bf16[128,640]{1,0:T(8,128)(2,1)S(1)}) custom-call(bf16[256,1280]{1,0:T(8,128)(2,1)S(1)} %collective-permute-done.15.refs_0_, bf16[128,640]{1,0:T(8,128)(2,1)S(1)} %collective-permute-done.20.refs_1_, s32[1,128]{1,0:T(1,128)S(1)} %collective-permute-done.8.refs_3_.refs_2_.refs_1_, ...), custom_call_target="tpu_custom_call" | custom-call | flops 838860800 | bytes 6553600 | tf_op jit(solution)/shard_map/section_2/pallas_call | solution.py:133
  88.0 4.0 %section_3.2 = bf16[32,5120]{1,0:T(8,128)(2,1)} custom-call(bf16[128,1280]{1,0:T(8,128)(2,1)S(1)} %get-tuple-element.40.refs_0_, bf16[128,640]{1,0:T(8,128)(2,1)S(1)} %get-tuple-element.41.refs_1_, s32[1,128]{1,0:T(1,128)S(1)} %collective-permute-done.8.refs_3_.refs_2_.refs_1_, f32[2,1,1280]{2,1,0:T(1,128)S(1)} %reshape.11.refs_3_, ...), custom_call_target="tpu_custom_call" | custom-call | flops 1048576000 | bytes 8192000 | tf_op jit(solution)/shard_map/section_3/pallas_call | solution.py:133
  92.3 3.0 %copy-done.3 = bf16[4,1280,640]{2,1,0:T(8,128)(2,1)S(1)} copy-done((bf16[4,1280,640]{2,1,0:T(8,128)(2,1)S(1)}, bf16[4,1280,640]{2,1,0:T(8,128)(2,1)}, u32[]{:S(2)}) %copy-start.3) | copy-done | bytes 6553624
  95.3 1.4 %copy-done.5 = bf16[256,1280]{1,0:T(8,128)(2,1)S(1)} copy-done((bf16[256,1280]{1,0:T(8,128)(2,1)S(1)}, bf16[256,1280]{1,0:T(8,128)(2,1)}, u32[]{:S(2)}) %copy-start.5) | copy-done | bytes 655384
  96.7 3.6 %section_2.3 = (bf16[128,1280]{1,0:T(8,128)(2,1)S(1)}, bf16[128,640]{1,0:T(8,128)(2,1)S(1)}) custom-call(bf16[256,1280]{1,0:T(8,128)(2,1)S(1)} %copy-done.5, bf16[128,640]{1,0:T(8,128)(2,1)} %collective-permute-done.30.refs_1_, s32[1,128]{1,0:T(1,128)S(1)} %copy-done.9, f32[2,1,1280]{2,1,0:T(1,128)S(1)} %reshape.11.refs_3_, ...), custom_call_target="tpu_custom_call" | custom-call | flops 838860800 | bytes 6553600 | tf_op jit(solution)/shard_map/section_2/pallas_call | solution.py:133
  100.3 3.2 %section_3.3 = bf16[32,5120]{1,0:T(8,128)(2,1)S(1)} custom-call(bf16[128,1280]{1,0:T(8,128)(2,1)S(1)} %get-tuple-element.45.refs_0_, bf16[128,640]{1,0:T(8,128)(2,1)S(1)} %get-tuple-element.46.refs_1_, s32[1,128]{1,0:T(1,128)S(1)} %copy-done.9, f32[2,1,1280]{2,1,0:T(1,128)S(1)} %reshape.11.refs_3_, f32[1,1280]{1,0:T(1,128)S(1)} %reshape.10.refs_5_.refs_3_.refs_4_, ...), custom_call_target="tpu_custom_call" | custom-call | flops 1048576000 | bytes 8192000 | tf_op jit(solution)/shard_map/section_3/pallas_call | solution.py:133
  103.5 0.8 broadcast_select_fusion
  (76 shorter events, 9.3 us)
Async XLA Ops:
  2.8 50.0 %copy-start.11 = (f32[1280]{0:T(1024)S(1)}, f32[1280]{0:T(1024)}, u32[]{:S(2)}) copy-start(f32[1280]{0:T(1024)} %param.11) | copy-start | bytes 15364
  3.2 46.0 %collective-permute-start.2 = (bf16[9,160,640]{2,1,0:T(8,128)(2,1)S(1)}, bf16[9,160,640]{2,1,0:T(8,128)(2,1)S(1)}, u32[]{:S(2)}, u32[]{:S(2)}) collective-permute-start(bf16[9,160,640]{2,1,0:T(8,128)(2,1)S(1)} %get-tuple-element.27), channel_id=1, source_target_pairs={{0,4},{4,0},{8,12},{12,8},{16,20},{20,16},{24,28},{28,24},{1,5},{5... | collective-permute-start | bytes 5529608 | tf_op jit(solution)/shard_map/ppermute | solution.py:217
  3.7 21.7 %collective-permute-start.6 = (bf16[4,160,640]{2,1,0:T(8,128)(2,1)S(1)}, bf16[4,160,640]{2,1,0:T(8,128)(2,1)S(1)}, u32[]{:S(2)}, u32[]{:S(2)}) collective-permute-start(bf16[4,160,640]{2,1,0:T(8,128)(2,1)S(1)} %get-tuple-element.30.refs_0_), channel_id=1, source_target_pairs={{0,16},{4,20},{8,24},{12,28},{16,0},{20,4},{24,8},{28,12},{1,17},{... | collective-permute-start | bytes 2457608 | tf_op jit(solution)/shard_map/ppermute | solution.py:217
  6.3 21.1 %collective-permute-start.5 = (bf16[4,160,640]{2,1,0:T(8,128)(2,1)S(1)}, bf16[4,160,640]{2,1,0:T(8,128)(2,1)S(1)}, u32[]{:S(2)}, u32[]{:S(2)}) collective-permute-start(bf16[4,160,640]{2,1,0:T(8,128)(2,1)S(1)} %get-tuple-element.30.refs_0_), channel_id=1, source_target_pairs={{0,8},{4,12},{8,0},{12,4},{16,24},{20,28},{24,16},{28,20},{1,9},{5... | collective-permute-start | bytes 2457608 | tf_op jit(solution)/shard_map/ppermute | solution.py:217
  7.8 30.8 %collective-permute-start.1 = (bf16[3,160,640]{2,1,0:T(8,128)(2,1)S(1)}, bf16[3,160,640]{2,1,0:T(8,128)(2,1)S(1)}, u32[]{:S(2)}, u32[]{:S(2)}) collective-permute-start(bf16[3,160,640]{2,1,0:T(8,128)(2,1)S(1)} %get-tuple-element.26.refs_0_), channel_id=1, source_target_pairs={{0,16},{4,20},{8,24},{12,28},{16,0},{20,4},{24,8},{28,12},{1,17},{... | collective-permute-start | bytes 1843208 | tf_op jit(solution)/shard_map/ppermute | solution.py:217
  8.3 3.5 %collective-permute-start.8 = (s32[1,128]{1,0:T(1,128)S(1)}, s32[1,128]{1,0:T(1,128)S(1)}, u32[]{:S(2)}, u32[]{:S(2)}) collective-permute-start(s32[1,128]{1,0:T(1,128)S(1)} %copy-done.9), channel_id=1, source_target_pairs={{0,1},{1,0},{2,3},{3,2},{4,5},{5,4},{6,7},{7,6},{8,9},{9,8},{10,11... | collective-permute-start | bytes 1544 | tf_op jit(solution)/shard_map/ppermute | solution.py:222
  11.8 8.4 %collective-permute-start.7 = (bf16[128,1280]{1,0:T(8,128)(2,1)S(1)}, bf16[128,1280]{1,0:T(8,128)(2,1)S(1)}, u32[]{:S(2)}, u32[]{:S(2)}) collective-permute-start(bf16[128,1280]{1,0:T(8,128)(2,1)S(1)} %copy-done.8), channel_id=1, source_target_pairs={{0,1},{1,0},{2,3},{3,2},{4,5},{5,4},{6,7},{7,6},{8,9},{9,8},{10,11... | collective-permute-start | bytes 983048 | tf_op jit(solution)/shard_map/ppermute | solution.py:222
  20.2 28.9 %collective-permute-start = (bf16[3,160,640]{2,1,0:T(8,128)(2,1)S(1)}, bf16[3,160,640]{2,1,0:T(8,128)(2,1)S(1)}, u32[]{:S(2)}, u32[]{:S(2)}) collective-permute-start(bf16[3,160,640]{2,1,0:T(8,128)(2,1)S(1)} %get-tuple-element.26.refs_0_), channel_id=1, source_target_pairs={{0,8},{4,12},{8,0},{12,4},{16,24},{20,28},{24,16},{28,20},{1,9},{5... | collective-permute-start | bytes 1843208 | tf_op jit(solution)/shard_map/ppermute | solution.py:217
  27.4 21.1 %collective-permute-start.13 = (bf16[4,80,640]{2,1,0:T(8,128)(2,1)S(1)}, bf16[4,80,640]{2,1,0:T(8,128)(2,1)S(1)}, u32[]{:S(2)}, u32[]{:S(2)}) collective-permute-start(bf16[4,80,640]{2,1,0:T(8,128)(2,1)S(1)} %slice.28), channel_id=1, source_target_pairs={{0,8},{4,12},{8,0},{12,4},{16,24},{20,28},{24,16},{28,20},{1,9},{5... | collective-permute-start | bytes 1228808 | tf_op jit(solution)/shard_map/ppermute | solution.py:217
  29.0 19.5 %collective-permute-start.11 = (bf16[4,80,640]{2,1,0:T(8,128)(2,1)S(1)}, bf16[4,80,640]{2,1,0:T(8,128)(2,1)S(1)}, u32[]{:S(2)}, u32[]{:S(2)}) collective-permute-start(bf16[4,80,640]{2,1,0:T(8,128)(2,1)S(1)} %slice.27), channel_id=1, source_target_pairs={{0,16},{4,20},{8,24},{12,28},{16,0},{20,4},{24,8},{28,12},{1,17},{... | collective-permute-start | bytes 1228808 | tf_op jit(solution)/shard_map/ppermute | solution.py:217
  38.5 13.8 %collective-permute-start.9 = (bf16[4,160,640]{2,1,0:T(8,128)(2,1)S(1)}, bf16[4,160,640]{2,1,0:T(8,128)(2,1)S(1)}, u32[]{:S(2)}, u32[]{:S(2)}) collective-permute-start(bf16[4,160,640]{2,1,0:T(8,128)(2,1)S(1)} %collective-permute-done.5.refs_2_), channel_id=1, source_target_pairs={{0,4},{4,0},{8,12},{12,8},{16,20},{20,16},{24,28},{28,24},{1,5},{5... | collective-permute-start | bytes 2457608 | tf_op jit(solution)/shard_map/ppermute | solution.py:217
  48.5 1.7 %collective-permute-start.14 = (bf16[4,80,640]{2,1,0:T(8,128)(2,1)S(1)}, bf16[4,80,640]{2,1,0:T(8,128)(2,1)S(1)}, u32[]{:S(2)}, u32[]{:S(2)}) collective-permute-start(bf16[4,80,640]{2,1,0:T(8,128)(2,1)S(1)} %collective-permute-done.13.refs_8_), channel_id=1, source_target_pairs={{0,4},{4,0},{8,12},{12,8},{16,20},{20,16},{24,28},{28,24},{1,5},{5... | collective-permute-start | bytes 1228808 | tf_op jit(solution)/shard_map/ppermute | solution.py:217
  48.5 2.3 %collective-permute-start.12 = (bf16[4,80,640]{2,1,0:T(8,128)(2,1)S(1)}, bf16[4,80,640]{2,1,0:T(8,128)(2,1)S(1)}, u32[]{:S(2)}, u32[]{:S(2)}) collective-permute-start(bf16[4,80,640]{2,1,0:T(8,128)(2,1)S(1)} %collective-permute-done.11.refs_6_), channel_id=1, source_target_pairs={{0,4},{4,0},{8,12},{12,8},{16,20},{20,16},{24,28},{28,24},{1,5},{5... | collective-permute-start | bytes 1228808 | tf_op jit(solution)/shard_map/ppermute | solution.py:217
  49.0 3.9 %collective-permute-start.10 = (bf16[4,160,640]{2,1,0:T(8,128)(2,1)S(1)}, bf16[4,160,640]{2,1,0:T(8,128)(2,1)S(1)}, u32[]{:S(2)}, u32[]{:S(2)}) collective-permute-start(bf16[4,160,640]{2,1,0:T(8,128)(2,1)S(1)} %collective-permute-done.6.refs_4_), channel_id=1, source_target_pairs={{0,4},{4,0},{8,12},{12,8},{16,20},{20,16},{24,28},{28,24},{1,5},{5... | collective-permute-start | bytes 2457608 | tf_op jit(solution)/shard_map/ppermute | solution.py:217
  49.2 13.3 %collective-permute-start.16 = (bf16[3,160,640]{2,1,0:T(8,128)(2,1)S(1)}, bf16[3,160,640]{2,1,0:T(8,128)(2,1)S(1)}, u32[]{:S(2)}, u32[]{:S(2)}) collective-permute-start(bf16[3,160,640]{2,1,0:T(8,128)(2,1)S(1)} %collective-permute-done.refs_2_), channel_id=1, source_target_pairs={{0,4},{4,0},{8,12},{12,8},{16,20},{20,16},{24,28},{28,24},{1,5},{5... | collective-permute-start | bytes 1843208 | tf_op jit(solution)/shard_map/ppermute | solution.py:217
  50.3 12.5 %collective-permute-start.17 = (bf16[3,160,640]{2,1,0:T(8,128)(2,1)S(1)}, bf16[3,160,640]{2,1,0:T(8,128)(2,1)S(1)}, u32[]{:S(2)}, u32[]{:S(2)}) collective-permute-start(bf16[3,160,640]{2,1,0:T(8,128)(2,1)S(1)} %collective-permute-done.1.refs_4_), channel_id=1, source_target_pairs={{0,4},{4,0},{8,12},{12,8},{16,20},{20,16},{24,28},{28,24},{1,5},{5... | collective-permute-start | bytes 1843208 | tf_op jit(solution)/shard_map/ppermute | solution.py:217
  50.9 9.3 %collective-permute-start.4 = (bf16[3,80,640]{2,1,0:T(8,128)(2,1)S(1)}, bf16[3,80,640]{2,1,0:T(8,128)(2,1)S(1)}, u32[]{:S(2)}, u32[]{:S(2)}) collective-permute-start(bf16[3,80,640]{2,1,0:T(8,128)(2,1)S(1)} %slice.25), channel_id=1, source_target_pairs={{0,8},{4,12},{8,0},{12,4},{16,24},{20,28},{24,16},{28,20},{1,9},{5... | collective-permute-start | bytes 921608 | tf_op jit(solution)/shard_map/ppermute | solution.py:217
  52.4 9.0 %collective-permute-start.3 = (bf16[3,80,640]{2,1,0:T(8,128)(2,1)S(1)}, bf16[3,80,640]{2,1,0:T(8,128)(2,1)S(1)}, u32[]{:S(2)}, u32[]{:S(2)}) collective-permute-start(bf16[3,80,640]{2,1,0:T(8,128)(2,1)S(1)} %slice.24), channel_id=1, source_target_pairs={{0,16},{4,20},{8,24},{12,28},{16,0},{20,4},{24,8},{28,12},{1,17},{... | collective-permute-start | bytes 921608 | tf_op jit(solution)/shard_map/ppermute | solution.py:217
  61.4 3.1 %collective-permute-start.18 = (bf16[3,80,640]{2,1,0:T(8,128)(2,1)S(1)}, bf16[3,80,640]{2,1,0:T(8,128)(2,1)S(1)}, u32[]{:S(2)}, u32[]{:S(2)}) collective-permute-start(bf16[3,80,640]{2,1,0:T(8,128)(2,1)S(1)} %collective-permute-done.3.refs_6_), channel_id=1, source_target_pairs={{0,4},{4,0},{8,12},{12,8},{16,20},{20,16},{24,28},{28,24},{1,5},{5... | collective-permute-start | bytes 921608 | tf_op jit(solution)/shard_map/ppermute | solution.py:217
  61.4 3.1 %collective-permute-start.19 = (bf16[3,80,640]{2,1,0:T(8,128)(2,1)S(1)}, bf16[3,80,640]{2,1,0:T(8,128)(2,1)S(1)}, u32[]{:S(2)}, u32[]{:S(2)}) collective-permute-start(bf16[3,80,640]{2,1,0:T(8,128)(2,1)S(1)} %collective-permute-done.4.refs_8_), channel_id=1, source_target_pairs={{0,4},{4,0},{8,12},{12,8},{16,20},{20,16},{24,28},{28,24},{1,5},{5... | collective-permute-start | bytes 921608 | tf_op jit(solution)/shard_map/ppermute | solution.py:217
  61.9 11.4 %collective-permute-start.22 = (bf16[2,160,640]{2,1,0:T(8,128)(2,1)S(1)}, bf16[2,160,640]{2,1,0:T(8,128)(2,1)S(1)}, u32[]{:S(2)}, u32[]{:S(2)}) collective-permute-start(bf16[2,160,640]{2,1,0:T(8,128)(2,1)S(1)} %get-tuple-element.42.refs_0_), channel_id=1, source_target_pairs={{0,16},{4,20},{8,24},{12,28},{16,0},{20,4},{24,8},{28,12},{1,17},{... | collective-permute-start | bytes 1228808 | tf_op jit(solution)/shard_map/ppermute | solution.py:217
  62.4 11.1 %collective-permute-start.21 = (bf16[2,160,640]{2,1,0:T(8,128)(2,1)S(1)}, bf16[2,160,640]{2,1,0:T(8,128)(2,1)S(1)}, u32[]{:S(2)}, u32[]{:S(2)}) collective-permute-start(bf16[2,160,640]{2,1,0:T(8,128)(2,1)S(1)} %get-tuple-element.42.refs_0_), channel_id=1, source_target_pairs={{0,8},{4,12},{8,0},{12,4},{16,24},{20,28},{24,16},{28,20},{1,9},{5... | collective-permute-start | bytes 1228808 | tf_op jit(solution)/shard_map/ppermute | solution.py:217
  62.7 20.3 %collective-permute-start.15 = (bf16[256,1280]{1,0:T(8,128)(2,1)S(1)}, bf16[256,1280]{1,0:T(8,128)(2,1)S(1)}, u32[]{:S(2)}, u32[]{:S(2)}) collective-permute-start(bf16[256,1280]{1,0:T(8,128)(2,1)S(1)} %section_0.1.refs_0_), channel_id=1, source_target_pairs={{0,1},{1,0},{2,3},{3,2},{4,5},{5,4},{6,7},{7,6},{8,9},{9,8},{10,11... | collective-permute-start | bytes 1966088 | tf_op jit(solution)/shard_map/ppermute | solution.py:222
  67.2 15.2 %collective-permute-start.20 = (bf16[128,640]{1,0:T(8,128)(2,1)S(1)}, bf16[128,640]{1,0:T(8,128)(2,1)S(1)}, u32[]{:S(2)}, u32[]{:S(2)}) collective-permute-start(bf16[128,640]{1,0:T(8,128)(2,1)S(1)} %attention_1.2), channel_id=1, source_target_pairs={{0,1},{1,0},{2,3},{3,2},{4,5},{5,4},{6,7},{7,6},{8,9},{9,8},{10,11... | collective-permute-start | bytes 491528 | tf_op jit(solution)/shard_map/ppermute | solution.py:222
  73.5 8.9 %collective-permute-start.27 = (bf16[2,80,640]{2,1,0:T(8,128)(2,1)S(1)}, bf16[2,80,640]{2,1,0:T(8,128)(2,1)S(1)}, u32[]{:S(2)}, u32[]{:S(2)}) collective-permute-start(bf16[2,80,640]{2,1,0:T(8,128)(2,1)S(1)} %slice.31), channel_id=1, source_target_pairs={{0,8},{4,12},{8,0},{12,4},{16,24},{20,28},{24,16},{28,20},{1,9},{5... | collective-permute-start | bytes 614408 | tf_op jit(solution)/shard_map/ppermute | solution.py:217
  74.0 8.9 %collective-permute-start.25 = (bf16[2,80,640]{2,1,0:T(8,128)(2,1)S(1)}, bf16[2,80,640]{2,1,0:T(8,128)(2,1)S(1)}, u32[]{:S(2)}, u32[]{:S(2)}) collective-permute-start(bf16[2,80,640]{2,1,0:T(8,128)(2,1)S(1)} %slice.30), channel_id=1, source_target_pairs={{0,16},{4,20},{8,24},{12,28},{16,0},{20,4},{24,8},{28,12},{1,17},{... | collective-permute-start | bytes 614408 | tf_op jit(solution)/shard_map/ppermute | solution.py:217
  75.7 12.0 %collective-permute-start.23 = (bf16[2,160,640]{2,1,0:T(8,128)(2,1)S(1)}, bf16[2,160,640]{2,1,0:T(8,128)(2,1)S(1)}, u32[]{:S(2)}, u32[]{:S(2)}) collective-permute-start(bf16[2,160,640]{2,1,0:T(8,128)(2,1)S(1)} %collective-permute-done.21.refs_2_), channel_id=1, source_target_pairs={{0,4},{4,0},{8,12},{12,8},{16,20},{20,16},{24,28},{28,24},{1,5},{5... | collective-permute-start | bytes 1228808 | tf_op jit(solution)/shard_map/ppermute | solution.py:217
  82.4 5.3 %collective-permute-start.24 = (bf16[2,160,640]{2,1,0:T(8,128)(2,1)S(1)}, bf16[2,160,640]{2,1,0:T(8,128)(2,1)S(1)}, u32[]{:S(2)}, u32[]{:S(2)}) collective-permute-start(bf16[2,160,640]{2,1,0:T(8,128)(2,1)S(1)} %collective-permute-done.22.refs_4_), channel_id=1, source_target_pairs={{0,4},{4,0},{8,12},{12,8},{16,20},{20,16},{24,28},{28,24},{1,5},{5... | collective-permute-start | bytes 1228808 | tf_op jit(solution)/shard_map/ppermute | solution.py:217
  82.4 5.3 %collective-permute-start.28 = (bf16[2,80,640]{2,1,0:T(8,128)(2,1)S(1)}, bf16[2,80,640]{2,1,0:T(8,128)(2,1)S(1)}, u32[]{:S(2)}, u32[]{:S(2)}) collective-permute-start(bf16[2,80,640]{2,1,0:T(8,128)(2,1)S(1)} %collective-permute-done.27.refs_8_), channel_id=1, source_target_pairs={{0,4},{4,0},{8,12},{12,8},{16,20},{20,16},{24,28},{28,24},{1,5},{5... | collective-permute-start | bytes 614408 | tf_op jit(solution)/shard_map/ppermute | solution.py:217
  82.9 4.8 %collective-permute-start.26 = (bf16[2,80,640]{2,1,0:T(8,128)(2,1)S(1)}, bf16[2,80,640]{2,1,0:T(8,128)(2,1)S(1)}, u32[]{:S(2)}, u32[]{:S(2)}) collective-permute-start(bf16[2,80,640]{2,1,0:T(8,128)(2,1)S(1)} %collective-permute-done.25.refs_6_), channel_id=1, source_target_pairs={{0,4},{4,0},{8,12},{12,8},{16,20},{20,16},{24,28},{28,24},{1,5},{5... | collective-permute-start | bytes 614408 | tf_op jit(solution)/shard_map/ppermute | solution.py:217
  83.0 9.3 %collective-permute-start.30 = (bf16[128,640]{1,0:T(8,128)(2,1)S(1)}, bf16[128,640]{1,0:T(8,128)(2,1)}, u32[]{:S(2)}, u32[]{:S(2)}) collective-permute-start(bf16[128,640]{1,0:T(8,128)(2,1)S(1)} %attention_1.3), channel_id=1, source_target_pairs={{0,1},{1,0},{2,3},{3,2},{4,5},{5,4},{6,7},{7,6},{8,9},{9,8},{10,11... | collective-permute-start | bytes 491528 | tf_op jit(solution)/shard_map/ppermute | solution.py:222
  92.0 11.5 %collective-permute-start.29 = (bf16[32,5120]{1,0:T(8,128)(2,1)}, bf16[32,5120]{1,0:T(8,128)(2,1)}, u32[]{:S(2)}, u32[]{:S(2)}) collective-permute-start(bf16[32,5120]{1,0:T(8,128)(2,1)} %section_3.2), channel_id=1, source_target_pairs={{0,1},{1,0},{2,3},{3,2},{4,5},{5,4},{6,7},{7,6},{8,9},{9,8},{10,11... | collective-permute-start | bytes 983048 | tf_op jit(solution)/shard_map/ppermute | solution.py:222
  (11 other events, 138.8 us)

commit v3 on v0

v3 whole, which is shorter than its diff:
```python
import functools

import jax
import jax.numpy as jnp
from jax import lax
from jax.experimental import pallas as pl
from jax.experimental.pallas import tpu as pltpu
from jax.sharding import PartitionSpec as P

D_VIS = 1280
HEADS = 8
HEAD_DIM = 80
WIDTH = HEADS * HEAD_DIM
SECTIONS = 4
LANES = 128
EPS = 1e-06
NEG = -1e30
SMALL = pl.CostEstimate(flops=1, bytes_accessed=1, transcendentals=1)


def normed_rows(values, gain):
    scale = lax.rsqrt(jnp.mean(values * values, axis=-1, keepdims=True) + EPS)
    return values * scale * gain


def attend(qkv, row_ids):
    query, keys, vals = qkv
    rows = query.shape[0]
    across = jnp.broadcast_to(row_ids, (rows, rows))
    same = across == across.T
    lane = lax.broadcasted_iota(jnp.int32, (rows, LANES), 1)
    tiles = [None] * (WIDTH // LANES)
    for head in range(HEADS):
        first, last = head * HEAD_DIM, (head + 1) * HEAD_DIM
        low, high = first // LANES, -(-last // LANES)
        span = slice(low * LANES, high * LANES)
        inside = []
        for tile in range(low, high):
            place = lane + tile * LANES
            inside.append((place >= first) & (place < last))
        part = jnp.concatenate(
            [
                jnp.where(mask, query[:, (low + i) * LANES : (low + i + 1) * LANES], 0)
                for i, mask in enumerate(inside)
            ],
            axis=1,
        )
        scores = lax.dot_general(
            part, keys[:, span], (((1,), (1,)), ((), ())), preferred_element_type=jnp.float32
        )
        scores = jnp.where(same, scores * HEAD_DIM ** (-0.5), NEG)
        weights = jnp.exp(scores - jnp.max(scores, axis=-1, keepdims=True))
        probs = weights * (1.0 / jnp.sum(weights, axis=-1, keepdims=True))
        mixed = jnp.dot(
            probs.astype(jnp.bfloat16), vals[:, span], preferred_element_type=jnp.float32
        )
        for i, mask in enumerate(inside):
            kept = jnp.where(mask, mixed[:, i * LANES : (i + 1) * LANES], 0.0)
            tile = low + i
            tiles[tile] = kept if tiles[tile] is None else tiles[tile] + kept
    return jnp.concatenate(tiles, axis=1).astype(jnp.bfloat16)


def stage_kernel(stage, *refs):
    pl.when(first_stage() == (stage == 1))(functools.partial(two_sections, stage, *refs))


def two_sections(stage, acts_ref, ids_ref, gain_ref, merge_ref, one_ref, two_ref, out_ref, flow, sheets):
    rows = flow.shape[0]
    flow[...] = acts_ref[...].astype(jnp.float32)
    for i, held in enumerate((one_ref, two_ref)):
        normed = normed_rows(flow[...], gain_ref[2 * stage - 2 + i]).astype(jnp.bfloat16)
        qkv = [
            jnp.dot(normed, held[j], preferred_element_type=jnp.float32).astype(jnp.bfloat16)
            for j in range(3)
        ]
        context = attend(qkv, ids_ref[...])
        for half in range(2):
            at = slice(half * WIDTH, (half + 1) * WIDTH)
            moved = jnp.dot(context, held[3, at], preferred_element_type=jnp.float32)
            flow[:, at] = (flow[:, at] + moved).astype(jnp.bfloat16).astype(jnp.float32)
    if stage == 1:
        out_ref[...] = flow[...].astype(jnp.bfloat16)
    else:
        final = normed_rows(flow[...], merge_ref[...])
        for tile in range(D_VIS // LANES):
            sheets[tile] = final[:, tile * LANES : (tile + 1) * LANES]
        for i in range(4):
            for tile in range(D_VIS // LANES):
                at = i * D_VIS + tile * LANES
                out_ref[:, at : at + LANES] = sheets[
                    tile, pl.ds(i, rows // 4, stride=4), :
                ].astype(jnp.bfloat16)


def run_stage(stage, acts, ids, gains, merge, weights):
    rows = acts.shape[0]
    vmem = pl.BlockSpec(memory_space=pltpu.VMEM)
    args = [acts, ids, gains, merge] + list(weights)
    return pl.pallas_call(
        functools.partial(stage_kernel, stage),
        out_shape=jax.ShapeDtypeStruct(
            (rows, D_VIS) if stage == 1 else (rows // 4, 4 * D_VIS), jnp.bfloat16
        ),
        in_specs=[vmem] * len(args),
        out_specs=vmem,
        scratch_shapes=[
            pltpu.VMEM((rows, D_VIS), jnp.float32),
            pltpu.VMEM((D_VIS // LANES, rows, LANES), jnp.float32),
        ],
        compiler_params=pltpu.CompilerParams(vmem_limit_bytes=8 * 1024 * 1024),
        cost_estimate=SMALL,
        name=f"stage_{stage}",
    )(*args)


def assemble_kernel(first, *refs):
    *blocks, whole = refs
    me = lax.axis_index("dp")
    one = jnp.where(me % 2 == 0, 2, 4)
    distances = (0, 1, one, 6 - one, 6, 7 - one, 1 + one, 7)
    for i, (distance, block) in enumerate(zip(distances, blocks)):
        owner = jnp.bitwise_xor(me, distance)
        for unit in range(whole.shape[0]):
            at = unit + (first if i == 1 else 0)
            if unit < 3:
                whole[unit, pl.ds(pl.multiple_of(owner * 160, 16), 160)] = block[at]
            else:
                for half in range(2):
                    where = pl.multiple_of(owner * 80 + half * WIDTH, 16)
                    whole[unit, pl.ds(where, 80)] = block[at, half * 80 : half * 80 + 80]


def assemble(name, own, own_other, first, blocks, others):
    vmem = pl.BlockSpec(memory_space=pltpu.VMEM)
    return pl.pallas_call(
        functools.partial(assemble_kernel, first),
        out_shape=jax.ShapeDtypeStruct((own.shape[0], D_VIS, WIDTH), jnp.bfloat16),
        in_specs=[vmem] * 8,
        out_specs=vmem,
        compiler_params=pltpu.CompilerParams(vmem_limit_bytes=8 * 1024 * 1024),
        cost_estimate=SMALL,
        name=name,
    )(own, own_other, *blocks, *others)


def first_stage():
    place = lax.axis_index("phase") % 4
    return (place == 1) | (place == 2)


def pack_kernel(qkv, out, chunk_a, chunk_b, chunks):
    section = jnp.where(first_stage(), 0, 2)
    for which, chunk in enumerate((chunk_a, chunk_b)):
        for i in range(3):
            unit = qkv[section + which, :, i * WIDTH : (i + 1) * WIDTH]
            chunk[i] = unit
            chunks[4 * which + i] = unit
        for half in range(2):
            unit = out[section + which, :, half * WIDTH : (half + 1) * WIDTH]
            chunk[3, half * 80 : half * 80 + 80] = unit
            chunks[4 * which + 3, half * 80 : half * 80 + 80] = unit


def pack(w_qkv, w_out):
    vmem = pl.BlockSpec(memory_space=pltpu.VMEM)
    return pl.pallas_call(
        pack_kernel,
        out_shape=[jax.ShapeDtypeStruct((n, 160, WIDTH), jnp.bfloat16) for n in (4, 4, 8)],
        in_specs=[vmem] * 2,
        out_specs=[vmem] * 3,
        compiler_params=pltpu.CompilerParams(vmem_limit_bytes=8 * 1024 * 1024),
        cost_estimate=SMALL,
        name="pack",
    )(w_qkv, w_out)


def cores(block):
    return lax.ppermute(block, "dp", [(j, j ^ 1) for j in range(lax.axis_size("dp"))])


def plane(block, turn):
    pairs = [(j, j ^ (2 if j % 2 == turn else 4)) for j in range(lax.axis_size("dp"))]
    return lax.ppermute(block, "dp", pairs)


def across(block):
    size = lax.axis_size("phase")
    return lax.ppermute(block, "phase", [(j, j ^ 1) for j in range(size)])


def staged_body(patches, window_ids, norm_gain, w_qkv, w_out, merge_gain):
    tie = lax.optimization_barrier
    gains = norm_gain.reshape(SECTIONS, 1, D_VIS)
    merge = merge_gain.reshape(1, D_VIS)

    chunk_a, chunk_b, chunks = pack(w_qkv, w_out)
    a1, a2 = plane(chunk_a, 0), plane(chunk_a, 1)
    own_other = cores(chunks)
    own_other, b, theirs, their_ids = tie((own_other, chunk_b, patches, window_ids))
    b1, b2 = plane(b, 0), plane(b, 1)
    other, other_ids = across(theirs), across(their_ids)
    a1, a2, b1, b2, other, other_ids = tie((a1, a2, b1, b2, other, other_ids))
    a3, b3 = plane(a1, 1), plane(b2, 0)
    a1_other, a2_other, b1_other, b2_other = (cores(block) for block in (a1, a2, b1, b2))
    a3, b3, a1_other, a2_other, b1_other, b2_other = tie(
        (a3, b3, a1_other, a2_other, b1_other, b2_other)
    )
    weights = [
        assemble(
            "weights_a", chunk_a, own_other, 0, (a1, a2, a3), (a1_other, a2_other, cores(a3))
        ),
        assemble(
            "weights_b", chunk_b, own_other, 4, (b1, b2, b3), (b1_other, b2_other, cores(b3))
        ),
    ]

    half_own = run_stage(1, patches, window_ids, gains, merge, weights)
    half_own_far = across(half_own)
    half_own, other = tie((half_own, other))
    half_other = run_stage(1, other, other_ids, gains, merge, weights)
    half_other_far = across(half_other)
    result_other = run_stage(2, half_own_far, other_ids, gains, merge, weights)
    back = across(result_other)
    half_other_far, result_other = tie((half_other_far, result_other))
    result_own = run_stage(2, half_other_far, window_ids, gains, merge, weights)
    return jnp.where(first_stage(), back, result_own)


def plain_section(acts, marks, gain, weight_qkv, weight_out):
    rows = acts.shape[0]
    values_f = acts.astype(jnp.float32)
    normed = normed_rows(values_f, gain).astype(jnp.bfloat16)
    qkv = jnp.dot(normed, weight_qkv, preferred_element_type=jnp.float32).astype(jnp.bfloat16)
    query, keys, vals = (
        qkv[:, i * WIDTH : (i + 1) * WIDTH].reshape(rows, HEADS, HEAD_DIM) for i in range(3)
    )
    scores = jnp.einsum(
        "qhd,khd->hqk", query, keys, preferred_element_type=jnp.float32
    ) * HEAD_DIM ** (-0.5)
    same = marks[:, None] == marks[None, :]
    scores = jnp.where(same[None], scores, jnp.float32(NEG))
    probs = jax.nn.softmax(scores, axis=-1).astype(jnp.bfloat16)
    context = jnp.einsum("hqk,khd->qhd", probs, vals, preferred_element_type=jnp.float32)
    context = context.astype(jnp.bfloat16).reshape(rows, WIDTH)
    update = jnp.dot(context, weight_out, preferred_element_type=jnp.float32)
    return (values_f + update).astype(jnp.bfloat16)


def plain_body(patches, window_ids, norm_gain, w_qkv, w_out, merge_gain):
    acts = patches
    for k in range(w_qkv.shape[0]):
        local_qkv, local_out, acts = lax.optimization_barrier((w_qkv[k], w_out[k], acts))
        weight_qkv = lax.all_gather(local_qkv, "dp", axis=0, tiled=True)
        weight_out = lax.all_gather(local_out, "dp", axis=0, tiled=True)
        acts = plain_section(acts, window_ids[0], norm_gain[k], weight_qkv, weight_out)
    final = normed_rows(acts.astype(jnp.float32), merge_gain).astype(jnp.bfloat16)
    return final.reshape(-1, 4 * D_VIS)


def body(patches, window_ids, norm_gain, w_qkv, w_out, merge_gain):
    staged = lax.axis_size("dp") == 8 and lax.axis_size("phase") % 4 == 0
    run = staged_body if staged else plain_body
    return run(patches, window_ids, norm_gain, w_qkv, w_out, merge_gain)


def solution(mesh):
    in_specs = (
        P(("dp", "phase"), None),
        P(("dp", "phase"), None),
        P(),
        P(None, "dp", None),
        P(None, "dp", None),
        P(),
    )
    out_specs = P(("dp", "phase"), None)
    return jax.shard_map(body, mesh=mesh, in_specs=in_specs, out_specs=out_specs, check_vma=False)
```

time: 224 us -> 102 us (0.46)
  waiting for transfers between devices: 147 us -> 51.2 us
  matrix products: 32.8 us -> 0 us
  between operations: 13.5 us -> 0.15 us
  Pallas kernels: 0 us -> 11.9 us
  starting transfers between devices: 21.5 us -> 29.1 us
    all_gather x2 -> x0, waiting for transfers between devices: 69.5 us -> none  [the longest x1 41.7 us: body(): lax.all_gather(local_qkv, 'dp', axis=0, tiled=True)]
    dot_general x16 -> x0, matrix products: 31.3 us -> none  [the longest x4 13.4 us: section(): jnp.dot(normed, weight_qkv, preferred_element_type=jnp.float32)]
    ppermute x15 -> x18, waiting for transfers between devices: 77.3 us -> 51.2 us  [the longest x6 43.1 us: plane(): return lax.ppermute(block, 'dp', pairs)]
    pallas_call x0 -> x7, Pallas kernels: none -> 11.9 us  [the longest x4 10.5 us: run_stage(): pl.pallas_call(functools.partial(stage_kernel, stage), out_shape=jax.Shap...]
    unnamed x8 -> x20, local copies, waits for them, and re-layouts: 0.02 us -> 8.58 us
    ppermute x15 -> x18, starting transfers between devices: 21.5 us -> 29.1 us  [the longest x5 16.5 us: across(): return lax.ppermute(block, 'phase', [(j, j ^ 1) for j in range(size)])]
    dynamic_slice x3 -> x0, local copies, waits for them, and re-layouts: 3.41 us -> none  [the longest x1 1.78 us: body(): local_out = lax.dynamic_index_in_dim(w_out, mine, 0, keepdims=False)]
  transfers between devices with their start and end apart: 17 -> 18, of which waited for: 10 -> 10; matrix products, arithmetic and copies ran while one was open for 1% -> 0% of each run, Pallas kernels for 0% -> 11%
where the time goes in v3:
time: 102 us
  waiting for transfers between devices  51.2 us (50%)
  starting transfers between devices  29.1 us (29%)
  Pallas kernels  11.9 us (12%)
  local copies, waits for them, and re-layouts  8.6 us (8%)
    ppermute x6, waiting for transfers between devices, plane(): return lax.ppermute(block, 'dp', pairs)  43.1 us
    ppermute x5, starting transfers between devices, across(): return lax.ppermute(block, 'phase', [(j, j ^ 1) for j in range(size)])  16.5 us
    ppermute x6, starting transfers between devices, plane(): return lax.ppermute(block, 'dp', pairs)  10.9 us
    pallas_call x4, Pallas kernels, run_stage(): pl.pallas_call(functools.partial(stage_kernel, stage), out_shape=jax.Shap...  10.5 us
    unnamed x20, local copies, waits for them, and re-layouts  8.58 us
    ppermute x5, waiting for transfers between devices, across(): return lax.ppermute(block, 'phase', [(j, j ^ 1) for j in range(size)])  5.63 us
    ppermute x7, waiting for transfers between devices, cores(): lax.ppermute(block, 'dp', [(j, j ^ 1) for j in range(lax.axis_size('dp'))])  2.44 us
  transfers between devices with their start and end apart: 18, of which 10 were waited for; matrix products, arithmetic and copies ran while one was open for 0% of the time, Pallas kernels for 11%

profile of v3, /device:TPU:0, one launch (start us, length us, event | category | flops | bytes accessed | tf_op | source)
XLA Modules:
  0.0 101.7 jit_solution(8179689479828109216)
XLA Ops:
  0.0 1.7 %copy-done.4 = bf16[4,160,1920]{2,1,0:T(8,128)(2,1)S(1)} copy-done((bf16[4,160,1920]{2,1,0:T(8,128)(2,1)S(1)}, bf16[4,160,1920]{2,1,0:T(8,128)(2,1)}, u32[]{:S(2)}) %copy-start.4) | copy-done | bytes 2457624
  1.7 1.1 %copy-done.5 = bf16[4,80,1280]{2,1,0:T(8,128)(2,1)S(1)} copy-done((bf16[4,80,1280]{2,1,0:T(8,128)(2,1)S(1)}, bf16[4,80,1280]{2,1,0:T(8,128)(2,1)}, u32[]{:S(2)}) %copy-start.5) | copy-done | bytes 819224
  3.1 0.5 collective-permute-start
  3.6 2.6 %collective-permute-start.1 = (bf16[4,160,640]{2,1,0:T(8,128)(2,1)S(1)}, bf16[4,160,640]{2,1,0:T(8,128)(2,1)S(1)}, u32[]{:S(2)}, u32[]{:S(2)}) collective-permute-start(bf16[4,160,640]{2,1,0:T(8,128)(2,1)S(1)} %get-tuple-element.26.refs_0_), channel_id=1, source_target_pairs={{0,8},{4,20},{8,0},{12,28},{16,24},{20,4},{24,16},{28,12},{1,9},{5... | collective-permute-start | bytes 2457608 | tf_op jit(solution)/shard_map/ppermute | solution.py:184
  6.2 1.5 %collective-permute-start.2 = (bf16[4,160,640]{2,1,0:T(8,128)(2,1)S(1)}, bf16[4,160,640]{2,1,0:T(8,128)(2,1)S(1)}, u32[]{:S(2)}, u32[]{:S(2)}) collective-permute-start(bf16[4,160,640]{2,1,0:T(8,128)(2,1)S(1)} %get-tuple-element.26.refs_0_), channel_id=1, source_target_pairs={{0,16},{4,12},{8,24},{12,4},{16,0},{20,28},{24,8},{28,20},{1,17},{... | collective-permute-start | bytes 2457608 | tf_op jit(solution)/shard_map/ppermute | solution.py:184
  7.7 1.9 %collective-permute-start.3 = (bf16[4,160,640]{2,1,0:T(8,128)(2,1)S(1)}, bf16[4,160,640]{2,1,0:T(8,128)(2,1)S(1)}, u32[]{:S(2)}, u32[]{:S(2)}) collective-permute-start(bf16[4,160,640]{2,1,0:T(8,128)(2,1)S(1)} %get-tuple-element.30.refs_0_), channel_id=1, source_target_pairs={{0,8},{4,20},{8,0},{12,28},{16,24},{20,4},{24,16},{28,12},{1,9},{5... | collective-permute-start | bytes 2457608 | tf_op jit(solution)/shard_map/ppermute | solution.py:184
  9.6 1.5 %collective-permute-start.4 = (bf16[4,160,640]{2,1,0:T(8,128)(2,1)S(1)}, bf16[4,160,640]{2,1,0:T(8,128)(2,1)S(1)}, u32[]{:S(2)}, u32[]{:S(2)}) collective-permute-start(bf16[4,160,640]{2,1,0:T(8,128)(2,1)S(1)} %get-tuple-element.30.refs_0_), channel_id=1, source_target_pairs={{0,16},{4,12},{8,24},{12,4},{16,0},{20,28},{24,8},{28,20},{1,17},{... | collective-permute-start | bytes 2457608 | tf_op jit(solution)/shard_map/ppermute | solution.py:184
  11.2 1.6 %collective-permute-start.5 = (bf16[128,1280]{1,0:T(8,128)(2,1)S(1)}, bf16[128,1280]{1,0:T(8,128)(2,1)S(1)}, u32[]{:S(2)}, u32[]{:S(2)}) collective-permute-start(bf16[128,1280]{1,0:T(8,128)(2,1)S(1)} %copy-done.6), channel_id=1, source_target_pairs={{0,1},{1,0},{2,3},{3,2},{4,5},{5,4},{6,7},{7,6},{8,9},{9,8},{10,11... | collective-permute-start | bytes 983048 | tf_op jit(solution)/shard_map/ppermute | solution.py:189
  12.8 11.4 %collective-permute-done.1.refs_2_ = bf16[4,160,640]{2,1,0:T(8,128)(2,1)S(1)} collective-permute-done((bf16[4,160,640]{2,1,0:T(8,128)(2,1)S(1)}, bf16[4,160,640]{2,1,0:T(8,128)(2,1)S(1)}, u32[]{:S(2)}, u32[]{:S(2)}) %collective-permute-start.1) | collective-permute-done | bytes 819232 | tf_op jit(solution)/shard_map/ppermute | solution.py:184
  24.2 2.6 %collective-permute-start.6 = (s32[1,128]{1,0:T(1,128)S(1)}, s32[1,128]{1,0:T(1,128)S(1)}, u32[]{:S(2)}, u32[]{:S(2)}) collective-permute-start(s32[1,128]{1,0:T(1,128)S(1)} %copy-done.7), channel_id=1, source_target_pairs={{0,1},{1,0},{2,3},{3,2},{4,5},{5,4},{6,7},{7,6},{8,9},{9,8},{10,11... | collective-permute-start | bytes 1544 | tf_op jit(solution)/shard_map/ppermute | solution.py:189
  26.8 0.6 collective-permute-done.2.refs_3_
  27.4 0.9 collective-permute-done.6.refs_1_
  28.3 13.5 %collective-permute-done.3.refs_2_ = bf16[4,160,640]{2,1,0:T(8,128)(2,1)S(1)} collective-permute-done((bf16[4,160,640]{2,1,0:T(8,128)(2,1)S(1)}, bf16[4,160,640]{2,1,0:T(8,128)(2,1)S(1)}, u32[]{:S(2)}, u32[]{:S(2)}) %collective-permute-start.3) | collective-permute-done | bytes 819232 | tf_op jit(solution)/shard_map/ppermute | solution.py:184
  41.7 0.9 collective-permute-done.4.refs_3_
  42.7 2.0 %collective-permute-start.8 = (bf16[4,160,640]{2,1,0:T(8,128)(2,1)S(1)}, bf16[4,160,640]{2,1,0:T(8,128)(2,1)S(1)}, u32[]{:S(2)}, u32[]{:S(2)}) collective-permute-start(bf16[4,160,640]{2,1,0:T(8,128)(2,1)S(1)} %collective-permute-done.4.refs_3_), channel_id=1, source_target_pairs={{0,8},{4,20},{8,0},{12,28},{16,24},{20,4},{24,16},{28,12},{1,9},{5... | collective-permute-start | bytes 2457608 | tf_op jit(solution)/shard_map/ppermute | solution.py:184
  44.7 1.4 %collective-permute-start.7 = (bf16[4,160,640]{2,1,0:T(8,128)(2,1)S(1)}, bf16[4,160,640]{2,1,0:T(8,128)(2,1)S(1)}, u32[]{:S(2)}, u32[]{:S(2)}) collective-permute-start(bf16[4,160,640]{2,1,0:T(8,128)(2,1)S(1)} %collective-permute-done.1.refs_2_), channel_id=1, source_target_pairs={{0,16},{4,12},{8,24},{12,4},{16,0},{20,28},{24,8},{28,20},{1,17},{... | collective-permute-start | bytes 2457608 | tf_op jit(solution)/shard_map/ppermute | solution.py:184
  46.1 0.5 collective-permute-start.10
  46.6 16.7 %collective-permute-done.7.refs_4_ = bf16[4,160,640]{2,1,0:T(8,128)(2,1)S(1)} collective-permute-done((bf16[4,160,640]{2,1,0:T(8,128)(2,1)S(1)}, bf16[4,160,640]{2,1,0:T(8,128)(2,1)S(1)}, u32[]{:S(2)}, u32[]{:S(2)}) %collective-permute-start.7) | collective-permute-done | bytes 819232 | tf_op jit(solution)/shard_map/ppermute | solution.py:184
  63.3 0.5 collective-permute-start.14
  63.9 1.8 %collective-permute-done.14.refs_7_ = bf16[4,160,640]{2,1,0:T(8,128)(2,1)S(1)} collective-permute-done((bf16[4,160,640]{2,1,0:T(8,128)(2,1)S(1)}, bf16[4,160,640]{2,1,0:T(8,128)(2,1)S(1)}, u32[]{:S(2)}, u32[]{:S(2)}) %collective-permute-start.14) | collective-permute-done | bytes 819232 | tf_op jit(solution)/shard_map/ppermute | solution.py:179
  65.7 0.5 weights_b.1.refs_5_
  66.3 0.6 collective-permute-done.13.refs_7_
  66.9 0.5 weights_a.1.refs_4_
  67.5 7.2 %collective-permute-start.15 = (bf16[128,1280]{1,0:T(8,128)(2,1)S(1)}, bf16[128,1280]{1,0:T(8,128)(2,1)S(1)}, u32[]{:S(2)}, u32[]{:S(2)}) collective-permute-start(bf16[128,1280]{1,0:T(8,128)(2,1)S(1)} %stage_1.2), channel_id=1, source_target_pairs={{0,1},{1,0},{2,3},{3,2},{4,5},{5,4},{6,7},{7,6},{8,9},{9,8},{10,11... | collective-permute-start | bytes 983048 | tf_op jit(solution)/shard_map/ppermute | solution.py:189
  74.6 5.1 %collective-permute-start.17 = (bf16[128,1280]{1,0:T(8,128)(2,1)S(1)}, bf16[128,1280]{1,0:T(8,128)(2,1)S(1)}, u32[]{:S(2)}, u32[]{:S(2)}) collective-permute-start(bf16[128,1280]{1,0:T(8,128)(2,1)S(1)} %stage_1.3), channel_id=1, source_target_pairs={{0,1},{1,0},{2,3},{3,2},{4,5},{5,4},{6,7},{7,6},{8,9},{9,8},{10,11... | collective-permute-start | bytes 983048 | tf_op jit(solution)/shard_map/ppermute | solution.py:189
  79.8 3.4 %collective-permute-done.15.refs_0_ = bf16[128,1280]{1,0:T(8,128)(2,1)S(1)} collective-permute-done((bf16[128,1280]{1,0:T(8,128)(2,1)S(1)}, bf16[128,1280]{1,0:T(8,128)(2,1)S(1)}, u32[]{:S(2)}, u32[]{:S(2)}) %collective-permute-start.15) | collective-permute-done | bytes 327712 | tf_op jit(solution)/shard_map/ppermute | solution.py:189
  83.2 5.3 %stage_2.2 = bf16[32,5120]{1,0:T(8,128)(2,1)S(1)} custom-call(bf16[128,1280]{1,0:T(8,128)(2,1)S(1)} %collective-permute-done.15.refs_0_, s32[1,128]{1,0:T(1,128)S(1)} %collective-permute-done.6.refs_1_, f32[4,1,1280]{2,1,0:T(1,128)S(1)} %reshape.6.refs_2_, f32[1,1280]{1,0:T(1,128)S(1)} %reshape.7.refs_3_, bf16[4,1280,640]{2,1,0:T(8,128)(2,1)S(1)} %weights_a.1.refs_4_, ...), custom_call_target="tpu_custom_call" | custom-call | flops 1 | bytes 1 | tf_op jit(solution)/shard_map/stage_2/pallas_call | solution.py:100
  88.6 1.3 %collective-permute-done.17.refs_0_ = bf16[128,1280]{1,0:T(8,128)(2,1)S(1)} collective-permute-done((bf16[128,1280]{1,0:T(8,128)(2,1)S(1)}, bf16[128,1280]{1,0:T(8,128)(2,1)S(1)}, u32[]{:S(2)}, u32[]{:S(2)}) %collective-permute-start.17) | collective-permute-done | bytes 327712 | tf_op jit(solution)/shard_map/ppermute | solution.py:189
  89.9 2.9 %copy-done.1 = bf16[4,1280,640]{2,1,0:T(8,128)(2,1)S(1)} copy-done((bf16[4,1280,640]{2,1,0:T(8,128)(2,1)S(1)}, bf16[4,1280,640]{2,1,0:T(8,128)(2,1)}, u32[]{:S(2)}) %copy-start.1) | copy-done | bytes 6553624
  92.7 2.9 %copy-done.3 = bf16[4,1280,640]{2,1,0:T(8,128)(2,1)S(1)} copy-done((bf16[4,1280,640]{2,1,0:T(8,128)(2,1)S(1)}, bf16[4,1280,640]{2,1,0:T(8,128)(2,1)}, u32[]{:S(2)}) %copy-start.3) | copy-done | bytes 6553624
  95.6 5.3 %stage_2.3 = bf16[32,5120]{1,0:T(8,128)(2,1)S(1)} custom-call(bf16[128,1280]{1,0:T(8,128)(2,1)S(1)} %collective-permute-done.17.refs_0_, s32[1,128]{1,0:T(1,128)S(1)} %copy-done.7, f32[4,1,1280]{2,1,0:T(1,128)S(1)} %reshape.6.refs_2_, f32[1,1280]{1,0:T(1,128)S(1)} %reshape.7.refs_3_, bf16[4,1280,640]{2,1,0:T(8,128)(2,1)S(1)} %copy-done.3, ...), custom_call_target="tpu_custom_call" | custom-call | flops 1 | bytes 1 | tf_op jit(solution)/shard_map/stage_2/pallas_call | solution.py:100
  100.9 0.8 broadcast_select_fusion
  (34 shorter events, 0.7 us)
Async XLA Ops:
  0.0 1.7 %copy-start.4 = (bf16[4,160,1920]{2,1,0:T(8,128)(2,1)S(1)}, bf16[4,160,1920]{2,1,0:T(8,128)(2,1)}, u32[]{:S(2)}) copy-start(bf16[4,160,1920]{2,1,0:T(8,128)(2,1)} %qkv.1) | copy-start | bytes 7372804
  1.7 1.1 %copy-start.5 = (bf16[4,80,1280]{2,1,0:T(8,128)(2,1)S(1)}, bf16[4,80,1280]{2,1,0:T(8,128)(2,1)}, u32[]{:S(2)}) copy-start(bf16[4,80,1280]{2,1,0:T(8,128)(2,1)} %out.1) | copy-start | bytes 2457604
  2.8 8.3 %copy-start.6 = (bf16[128,1280]{1,0:T(8,128)(2,1)S(1)}, bf16[128,1280]{1,0:T(8,128)(2,1)}, u32[]{:S(2)}) copy-start(bf16[128,1280]{1,0:T(8,128)(2,1)} %refs_0_.1) | copy-start | bytes 983044
  2.8 21.4 %copy-start.7 = (s32[1,128]{1,0:T(1,128)S(1)}, s32[1,128]{1,0:T(1,128)}, u32[]{:S(2)}) copy-start(s32[1,128]{1,0:T(1,128)} %refs_1_.3) | copy-start | bytes 1540
  2.8 61.1 %copy-start.8 = (f32[4,1280]{1,0:T(4,128)S(1)}, f32[4,1280]{1,0:T(4,128)}, u32[]{:S(2)}) copy-start(f32[4,1280]{1,0:T(4,128)} %param.8) | copy-start | bytes 61444
  2.8 61.1 %copy-start.9 = (f32[1280]{0:T(1024)S(1)}, f32[1280]{0:T(1024)}, u32[]{:S(2)}) copy-start(f32[1280]{0:T(1024)} %param.11) | copy-start | bytes 15364
  3.1 4.6 %collective-permute-start = (bf16[8,160,640]{2,1,0:T(8,128)(2,1)S(1)}, bf16[8,160,640]{2,1,0:T(8,128)(2,1)S(1)}, u32[]{:S(2)}, u32[]{:S(2)}) collective-permute-start(bf16[8,160,640]{2,1,0:T(8,128)(2,1)S(1)} %get-tuple-element.27), channel_id=1, source_target_pairs={{0,4},{4,0},{8,12},{12,8},{16,20},{20,16},{24,28},{28,24},{1,5},{5... | collective-permute-start | bytes 4915208 | tf_op jit(solution)/shard_map/ppermute | solution.py:179
  3.6 20.5 %collective-permute-start.1 = (bf16[4,160,640]{2,1,0:T(8,128)(2,1)S(1)}, bf16[4,160,640]{2,1,0:T(8,128)(2,1)S(1)}, u32[]{:S(2)}, u32[]{:S(2)}) collective-permute-start(bf16[4,160,640]{2,1,0:T(8,128)(2,1)S(1)} %get-tuple-element.26.refs_0_), channel_id=1, source_target_pairs={{0,8},{4,20},{8,0},{12,28},{16,24},{20,4},{24,16},{28,12},{1,9},{5... | collective-permute-start | bytes 2457608 | tf_op jit(solution)/shard_map/ppermute | solution.py:184
  6.2 21.2 %collective-permute-start.2 = (bf16[4,160,640]{2,1,0:T(8,128)(2,1)S(1)}, bf16[4,160,640]{2,1,0:T(8,128)(2,1)S(1)}, u32[]{:S(2)}, u32[]{:S(2)}) collective-permute-start(bf16[4,160,640]{2,1,0:T(8,128)(2,1)S(1)} %get-tuple-element.26.refs_0_), channel_id=1, source_target_pairs={{0,16},{4,12},{8,24},{12,4},{16,0},{20,28},{24,8},{28,20},{1,17},{... | collective-permute-start | bytes 2457608 | tf_op jit(solution)/shard_map/ppermute | solution.py:184
  7.7 34.0 %collective-permute-start.3 = (bf16[4,160,640]{2,1,0:T(8,128)(2,1)S(1)}, bf16[4,160,640]{2,1,0:T(8,128)(2,1)S(1)}, u32[]{:S(2)}, u32[]{:S(2)}) collective-permute-start(bf16[4,160,640]{2,1,0:T(8,128)(2,1)S(1)} %get-tuple-element.30.refs_0_), channel_id=1, source_target_pairs={{0,8},{4,20},{8,0},{12,28},{16,24},{20,4},{24,16},{28,12},{1,9},{5... | collective-permute-start | bytes 2457608 | tf_op jit(solution)/shard_map/ppermute | solution.py:184
  9.6 33.0 %collective-permute-start.4 = (bf16[4,160,640]{2,1,0:T(8,128)(2,1)S(1)}, bf16[4,160,640]{2,1,0:T(8,128)(2,1)S(1)}, u32[]{:S(2)}, u32[]{:S(2)}) collective-permute-start(bf16[4,160,640]{2,1,0:T(8,128)(2,1)S(1)} %get-tuple-element.30.refs_0_), channel_id=1, source_target_pairs={{0,16},{4,12},{8,24},{12,4},{16,0},{20,28},{24,8},{28,20},{1,17},{... | collective-permute-start | bytes 2457608 | tf_op jit(solution)/shard_map/ppermute | solution.py:184
  11.2 17.1 %collective-permute-start.5 = (bf16[128,1280]{1,0:T(8,128)(2,1)S(1)}, bf16[128,1280]{1,0:T(8,128)(2,1)S(1)}, u32[]{:S(2)}, u32[]{:S(2)}) collective-permute-start(bf16[128,1280]{1,0:T(8,128)(2,1)S(1)} %copy-done.6), channel_id=1, source_target_pairs={{0,1},{1,0},{2,3},{3,2},{4,5},{5,4},{6,7},{7,6},{8,9},{9,8},{10,11... | collective-permute-start | bytes 983048 | tf_op jit(solution)/shard_map/ppermute | solution.py:189
  24.2 4.1 %collective-permute-start.6 = (s32[1,128]{1,0:T(1,128)S(1)}, s32[1,128]{1,0:T(1,128)S(1)}, u32[]{:S(2)}, u32[]{:S(2)}) collective-permute-start(s32[1,128]{1,0:T(1,128)S(1)} %copy-done.7), channel_id=1, source_target_pairs={{0,1},{1,0},{2,3},{3,2},{4,5},{5,4},{6,7},{7,6},{8,9},{9,8},{10,11... | collective-permute-start | bytes 1544 | tf_op jit(solution)/shard_map/ppermute | solution.py:189
  42.6 4.0 %collective-permute-start.12 = (bf16[4,160,640]{2,1,0:T(8,128)(2,1)S(1)}, bf16[4,160,640]{2,1,0:T(8,128)(2,1)S(1)}, u32[]{:S(2)}, u32[]{:S(2)}) collective-permute-start(bf16[4,160,640]{2,1,0:T(8,128)(2,1)S(1)} %collective-permute-done.4.refs_3_), channel_id=1, source_target_pairs={{0,4},{4,0},{8,12},{12,8},{16,20},{20,16},{24,28},{28,24},{1,5},{5... | collective-permute-start | bytes 2457608 | tf_op jit(solution)/shard_map/ppermute | solution.py:179
  42.7 20.6 %collective-permute-start.8 = (bf16[4,160,640]{2,1,0:T(8,128)(2,1)S(1)}, bf16[4,160,640]{2,1,0:T(8,128)(2,1)S(1)}, u32[]{:S(2)}, u32[]{:S(2)}) collective-permute-start(bf16[4,160,640]{2,1,0:T(8,128)(2,1)S(1)} %collective-permute-done.4.refs_3_), channel_id=1, source_target_pairs={{0,8},{4,20},{8,0},{12,28},{16,24},{20,4},{24,16},{28,12},{1,9},{5... | collective-permute-start | bytes 2457608 | tf_op jit(solution)/shard_map/ppermute | solution.py:184
  44.7 18.6 %collective-permute-start.7 = (bf16[4,160,640]{2,1,0:T(8,128)(2,1)S(1)}, bf16[4,160,640]{2,1,0:T(8,128)(2,1)S(1)}, u32[]{:S(2)}, u32[]{:S(2)}) collective-permute-start(bf16[4,160,640]{2,1,0:T(8,128)(2,1)S(1)} %collective-permute-done.1.refs_2_), channel_id=1, source_target_pairs={{0,16},{4,12},{8,24},{12,4},{16,0},{20,28},{24,8},{28,20},{1,17},{... | collective-permute-start | bytes 2457608 | tf_op jit(solution)/shard_map/ppermute | solution.py:184
  46.1 17.2 %collective-permute-start.9 = (bf16[4,160,640]{2,1,0:T(8,128)(2,1)S(1)}, bf16[4,160,640]{2,1,0:T(8,128)(2,1)S(1)}, u32[]{:S(2)}, u32[]{:S(2)}) collective-permute-start(bf16[4,160,640]{2,1,0:T(8,128)(2,1)S(1)} %collective-permute-done.1.refs_2_), channel_id=1, source_target_pairs={{0,4},{4,0},{8,12},{12,8},{16,20},{20,16},{24,28},{28,24},{1,5},{5... | collective-permute-start | bytes 2457608 | tf_op jit(solution)/shard_map/ppermute | solution.py:179
  46.1 17.2 %collective-permute-start.10 = (bf16[4,160,640]{2,1,0:T(8,128)(2,1)S(1)}, bf16[4,160,640]{2,1,0:T(8,128)(2,1)S(1)}, u32[]{:S(2)}, u32[]{:S(2)}) collective-permute-start(bf16[4,160,640]{2,1,0:T(8,128)(2,1)S(1)} %collective-permute-done.2.refs_3_), channel_id=1, source_target_pairs={{0,4},{4,0},{8,12},{12,8},{16,20},{20,16},{24,28},{28,24},{1,5},{5... | collective-permute-start | bytes 2457608 | tf_op jit(solution)/shard_map/ppermute | solution.py:179
  46.6 16.7 %collective-permute-start.11 = (bf16[4,160,640]{2,1,0:T(8,128)(2,1)S(1)}, bf16[4,160,640]{2,1,0:T(8,128)(2,1)S(1)}, u32[]{:S(2)}, u32[]{:S(2)}) collective-permute-start(bf16[4,160,640]{2,1,0:T(8,128)(2,1)S(1)} %collective-permute-done.3.refs_2_), channel_id=1, source_target_pairs={{0,4},{4,0},{8,12},{12,8},{16,20},{20,16},{24,28},{28,24},{1,5},{5... | collective-permute-start | bytes 2457608 | tf_op jit(solution)/shard_map/ppermute | solution.py:179
  63.3 2.4 %collective-permute-start.14 = (bf16[4,160,640]{2,1,0:T(8,128)(2,1)S(1)}, bf16[4,160,640]{2,1,0:T(8,128)(2,1)S(1)}, u32[]{:S(2)}, u32[]{:S(2)}) collective-permute-start(bf16[4,160,640]{2,1,0:T(8,128)(2,1)S(1)} %collective-permute-done.8.refs_4_), channel_id=1, source_target_pairs={{0,4},{4,0},{8,12},{12,8},{16,20},{20,16},{24,28},{28,24},{1,5},{5... | collective-permute-start | bytes 2457608 | tf_op jit(solution)/shard_map/ppermute | solution.py:179
  63.8 3.1 %collective-permute-start.13 = (bf16[4,160,640]{2,1,0:T(8,128)(2,1)S(1)}, bf16[4,160,640]{2,1,0:T(8,128)(2,1)S(1)}, u32[]{:S(2)}, u32[]{:S(2)}) collective-permute-start(bf16[4,160,640]{2,1,0:T(8,128)(2,1)S(1)} %collective-permute-done.7.refs_4_), channel_id=1, source_target_pairs={{0,4},{4,0},{8,12},{12,8},{16,20},{20,16},{24,28},{28,24},{1,5},{5... | collective-permute-start | bytes 2457608 | tf_op jit(solution)/shard_map/ppermute | solution.py:179
  66.3 16.9 %copy-start = (bf16[4,1280,640]{2,1,0:T(8,128)(2,1)}, bf16[4,1280,640]{2,1,0:T(8,128)(2,1)S(1)}, u32[]{:S(2)}) copy-start(bf16[4,1280,640]{2,1,0:T(8,128)(2,1)S(1)} %weights_b.1.refs_5_) | copy-start | bytes 19660804
  67.4 15.8 %copy-start.2 = (bf16[4,1280,640]{2,1,0:T(8,128)(2,1)}, bf16[4,1280,640]{2,1,0:T(8,128)(2,1)S(1)}, u32[]{:S(2)}) copy-start(bf16[4,1280,640]{2,1,0:T(8,128)(2,1)S(1)} %weights_a.1.refs_4_) | copy-start | bytes 19660804
  67.5 15.7 %collective-permute-start.15 = (bf16[128,1280]{1,0:T(8,128)(2,1)S(1)}, bf16[128,1280]{1,0:T(8,128)(2,1)S(1)}, u32[]{:S(2)}, u32[]{:S(2)}) collective-permute-start(bf16[128,1280]{1,0:T(8,128)(2,1)S(1)} %stage_1.2), channel_id=1, source_target_pairs={{0,1},{1,0},{2,3},{3,2},{4,5},{5,4},{6,7},{7,6},{8,9},{9,8},{10,11... | collective-permute-start | bytes 983048 | tf_op jit(solution)/shard_map/ppermute | solution.py:189
  74.6 15.3 %collective-permute-start.17 = (bf16[128,1280]{1,0:T(8,128)(2,1)S(1)}, bf16[128,1280]{1,0:T(8,128)(2,1)S(1)}, u32[]{:S(2)}, u32[]{:S(2)}) collective-permute-start(bf16[128,1280]{1,0:T(8,128)(2,1)S(1)} %stage_1.3), channel_id=1, source_target_pairs={{0,1},{1,0},{2,3},{3,2},{4,5},{5,4},{6,7},{7,6},{8,9},{9,8},{10,11... | collective-permute-start | bytes 983048 | tf_op jit(solution)/shard_map/ppermute | solution.py:189
  88.5 12.4 %collective-permute-start.16 = (bf16[32,5120]{1,0:T(8,128)(2,1)S(1)}, bf16[32,5120]{1,0:T(8,128)(2,1)S(1)}, u32[]{:S(2)}, u32[]{:S(2)}) collective-permute-start(bf16[32,5120]{1,0:T(8,128)(2,1)S(1)} %stage_2.2), channel_id=1, source_target_pairs={{0,1},{1,0},{2,3},{3,2},{4,5},{5,4},{6,7},{7,6},{8,9},{9,8},{10,11... | collective-permute-start | bytes 983048 | tf_op jit(solution)/shard_map/ppermute | solution.py:189
  89.9 2.9 %copy-start.1 = (bf16[4,1280,640]{2,1,0:T(8,128)(2,1)S(1)}, bf16[4,1280,640]{2,1,0:T(8,128)(2,1)}, u32[]{:S(2)}) copy-start(bf16[4,1280,640]{2,1,0:T(8,128)(2,1)} %copy-done) | copy-start | bytes 19660804
  92.7 2.9 %copy-start.3 = (bf16[4,1280,640]{2,1,0:T(8,128)(2,1)S(1)}, bf16[4,1280,640]{2,1,0:T(8,128)(2,1)}, u32[]{:S(2)}) copy-start(bf16[4,1280,640]{2,1,0:T(8,128)(2,1)} %copy-done.2) | copy-start | bytes 19660804

commit v4 on v3

--- a/solution.py
+++ b/solution.py
@@ -175,6 +175,31 @@
     )(w_qkv, w_out)
 
 
+def choose_kernel(one_ref, two_ref, out_ref):
+    first = first_stage()
+
+    @pl.when(first)
+    def _():
+        out_ref[...] = one_ref[...]
+
+    @pl.when(jnp.logical_not(first))
+    def _():
+        out_ref[...] = two_ref[...]
+
+
+def choose(one, two):
+    vmem = pl.BlockSpec(memory_space=pltpu.VMEM)
+    return pl.pallas_call(
+        choose_kernel,
+        out_shape=jax.ShapeDtypeStruct(one.shape, one.dtype),
+        in_specs=[vmem] * 2,
+        out_specs=vmem,
+        compiler_params=pltpu.CompilerParams(vmem_limit_bytes=8 * 1024 * 1024),
+        cost_estimate=SMALL,
+        name="choose",
+    )(one, two)
+
+
 def cores(block):
     return lax.ppermute(block, "dp", [(j, j ^ 1) for j in range(lax.axis_size("dp"))])
 
@@ -224,7 +249,7 @@
     back = across(result_other)
     half_other_far, result_other = tie((half_other_far, result_other))
     result_own = run_stage(2, half_other_far, window_ids, gains, merge, weights)
-    return jnp.where(first_stage(), back, result_own)
+    return choose(back, result_own)
 
 
 def plain_section(acts, marks, gain, weight_qkv, weight_out):

time: 102 us -> 98.5 us (0.966)
  local copies, waits for them, and re-layouts: 8.6 us -> 2.87 us
  waiting for transfers between devices: 51.2 us -> 53.7 us
    unnamed x20 -> x12, local copies, waits for them, and re-layouts: 8.58 us -> 2.85 us
    ppermute x5, waiting for transfers between devices: 5.63 us -> 8.13 us  [across(): return lax.ppermute(block, 'phase', [(j, j ^ 1) for j in range(size)])]
  transfers between devices with their start and end apart: 18 -> 18, of which waited for: 10 -> 11; matrix products, arithmetic and copies ran while one was open for 0% -> 0% of each run, Pallas kernels for 11% -> 11%
where the time goes in v4:
time: 98.5 us; the launch traced here: 98.3 us
  waiting for transfers between devices  53.7 us (55%)
  starting transfers between devices  29.1 us (30%)
  Pallas kernels  12.6 us (13%)
  local copies, waits for them, and re-layouts  2.87 us (3%)
    ppermute x6, waiting for transfers between devices, plane(): return lax.ppermute(block, 'dp', pairs)  43.1 us
    ppermute x5, starting transfers between devices, across(): return lax.ppermute(block, 'phase', [(j, j ^ 1) for j in range(size)])  16.5 us
    ppermute x6, starting transfers between devices, plane(): return lax.ppermute(block, 'dp', pairs)  10.9 us
    pallas_call x4, Pallas kernels, run_stage(): pl.pallas_call(functools.partial(stage_kernel, stage), out_shape=jax.Shap...  10.5 us
    ppermute x5, waiting for transfers between devices, across(): return lax.ppermute(block, 'phase', [(j, j ^ 1) for j in range(size)])  8.13 us
    unnamed x12, local copies, waits for them, and re-layouts  2.85 us
    ppermute x7, waiting for transfers between devices, cores(): lax.ppermute(block, 'dp', [(j, j ^ 1) for j in range(lax.axis_size('dp'))])  2.45 us
  transfers between devices with their start and end apart: 18, of which 11 were waited for; matrix products, arithmetic and copies ran while one was open for 0% of the time, Pallas kernels for 11%

profile of v4, /device:TPU:0, one launch (start us, length us, event | category | flops | bytes accessed | tf_op | source)
XLA Modules:
  0.0 98.3 jit_solution(13203391122063108441)
XLA Ops:
  0.0 1.7 %copy-done = bf16[4,160,1920]{2,1,0:T(8,128)(2,1)S(1)} copy-done((bf16[4,160,1920]{2,1,0:T(8,128)(2,1)S(1)}, bf16[4,160,1920]{2,1,0:T(8,128)(2,1)}, u32[]{:S(2)}) %copy-start) | copy-done | bytes 2457624
  1.7 1.1 %copy-done.1 = bf16[4,80,1280]{2,1,0:T(8,128)(2,1)S(1)} copy-done((bf16[4,80,1280]{2,1,0:T(8,128)(2,1)S(1)}, bf16[4,80,1280]{2,1,0:T(8,128)(2,1)}, u32[]{:S(2)}) %copy-start.1) | copy-done | bytes 819224
  2.9 0.3 pack.1
  3.1 0.5 collective-permute-start
  3.6 2.6 %collective-permute-start.1 = (bf16[4,160,640]{2,1,0:T(8,128)(2,1)S(1)}, bf16[4,160,640]{2,1,0:T(8,128)(2,1)S(1)}, u32[]{:S(2)}, u32[]{:S(2)}) collective-permute-start(bf16[4,160,640]{2,1,0:T(8,128)(2,1)S(1)} %get-tuple-element.26.refs_0_), channel_id=1, source_target_pairs={{0,8},{4,20},{8,0},{12,28},{16,24},{20,4},{24,16},{28,12},{1,9},{5... | collective-permute-start | bytes 2457608 | tf_op jit(solution)/shard_map/ppermute | solution.py:209
  6.2 1.5 %collective-permute-start.2 = (bf16[4,160,640]{2,1,0:T(8,128)(2,1)S(1)}, bf16[4,160,640]{2,1,0:T(8,128)(2,1)S(1)}, u32[]{:S(2)}, u32[]{:S(2)}) collective-permute-start(bf16[4,160,640]{2,1,0:T(8,128)(2,1)S(1)} %get-tuple-element.26.refs_0_), channel_id=1, source_target_pairs={{0,16},{4,12},{8,24},{12,4},{16,0},{20,28},{24,8},{28,20},{1,17},{... | collective-permute-start | bytes 2457608 | tf_op jit(solution)/shard_map/ppermute | solution.py:209
  7.7 1.9 %collective-permute-start.3 = (bf16[4,160,640]{2,1,0:T(8,128)(2,1)S(1)}, bf16[4,160,640]{2,1,0:T(8,128)(2,1)S(1)}, u32[]{:S(2)}, u32[]{:S(2)}) collective-permute-start(bf16[4,160,640]{2,1,0:T(8,128)(2,1)S(1)} %get-tuple-element.30.refs_0_), channel_id=1, source_target_pairs={{0,8},{4,20},{8,0},{12,28},{16,24},{20,4},{24,16},{28,12},{1,9},{5... | collective-permute-start | bytes 2457608 | tf_op jit(solution)/shard_map/ppermute | solution.py:209
  9.6 1.5 %collective-permute-start.4 = (bf16[4,160,640]{2,1,0:T(8,128)(2,1)S(1)}, bf16[4,160,640]{2,1,0:T(8,128)(2,1)S(1)}, u32[]{:S(2)}, u32[]{:S(2)}) collective-permute-start(bf16[4,160,640]{2,1,0:T(8,128)(2,1)S(1)} %get-tuple-element.30.refs_0_), channel_id=1, source_target_pairs={{0,16},{4,12},{8,24},{12,4},{16,0},{20,28},{24,8},{28,20},{1,17},{... | collective-permute-start | bytes 2457608 | tf_op jit(solution)/shard_map/ppermute | solution.py:209
  11.2 1.6 %collective-permute-start.5 = (bf16[128,1280]{1,0:T(8,128)(2,1)S(1)}, bf16[128,1280]{1,0:T(8,128)(2,1)S(1)}, u32[]{:S(2)}, u32[]{:S(2)}) collective-permute-start(bf16[128,1280]{1,0:T(8,128)(2,1)S(1)} %copy-done.2), channel_id=1, source_target_pairs={{0,1},{1,0},{2,3},{3,2},{4,5},{5,4},{6,7},{7,6},{8,9},{9,8},{10,11... | collective-permute-start | bytes 983048 | tf_op jit(solution)/shard_map/ppermute | solution.py:214
  12.8 11.4 %collective-permute-done.1.refs_2_ = bf16[4,160,640]{2,1,0:T(8,128)(2,1)S(1)} collective-permute-done((bf16[4,160,640]{2,1,0:T(8,128)(2,1)S(1)}, bf16[4,160,640]{2,1,0:T(8,128)(2,1)S(1)}, u32[]{:S(2)}, u32[]{:S(2)}) %collective-permute-start.1) | collective-permute-done | bytes 819232 | tf_op jit(solution)/shard_map/ppermute | solution.py:209
  24.2 2.6 %collective-permute-start.6 = (s32[1,128]{1,0:T(1,128)S(1)}, s32[1,128]{1,0:T(1,128)S(1)}, u32[]{:S(2)}, u32[]{:S(2)}) collective-permute-start(s32[1,128]{1,0:T(1,128)S(1)} %copy-done.3), channel_id=1, source_target_pairs={{0,1},{1,0},{2,3},{3,2},{4,5},{5,4},{6,7},{7,6},{8,9},{9,8},{10,11... | collective-permute-start | bytes 1544 | tf_op jit(solution)/shard_map/ppermute | solution.py:214
  26.8 0.6 collective-permute-done.2.refs_3_
  27.4 0.9 collective-permute-done.6.refs_1_
  28.3 13.5 %collective-permute-done.3.refs_2_ = bf16[4,160,640]{2,1,0:T(8,128)(2,1)S(1)} collective-permute-done((bf16[4,160,640]{2,1,0:T(8,128)(2,1)S(1)}, bf16[4,160,640]{2,1,0:T(8,128)(2,1)S(1)}, u32[]{:S(2)}, u32[]{:S(2)}) %collective-permute-start.3) | collective-permute-done | bytes 819232 | tf_op jit(solution)/shard_map/ppermute | solution.py:209
  41.7 0.9 collective-permute-done.4.refs_3_
  42.7 2.0 %collective-permute-start.8 = (bf16[4,160,640]{2,1,0:T(8,128)(2,1)S(1)}, bf16[4,160,640]{2,1,0:T(8,128)(2,1)S(1)}, u32[]{:S(2)}, u32[]{:S(2)}) collective-permute-start(bf16[4,160,640]{2,1,0:T(8,128)(2,1)S(1)} %collective-permute-done.4.refs_3_), channel_id=1, source_target_pairs={{0,8},{4,20},{8,0},{12,28},{16,24},{20,4},{24,16},{28,12},{1,9},{5... | collective-permute-start | bytes 2457608 | tf_op jit(solution)/shard_map/ppermute | solution.py:209
  44.7 1.4 %collective-permute-start.7 = (bf16[4,160,640]{2,1,0:T(8,128)(2,1)S(1)}, bf16[4,160,640]{2,1,0:T(8,128)(2,1)S(1)}, u32[]{:S(2)}, u32[]{:S(2)}) collective-permute-start(bf16[4,160,640]{2,1,0:T(8,128)(2,1)S(1)} %collective-permute-done.1.refs_2_), channel_id=1, source_target_pairs={{0,16},{4,12},{8,24},{12,4},{16,0},{20,28},{24,8},{28,20},{1,17},{... | collective-permute-start | bytes 2457608 | tf_op jit(solution)/shard_map/ppermute | solution.py:209
  46.1 0.5 collective-permute-start.10
  46.6 16.7 %collective-permute-done.7.refs_4_ = bf16[4,160,640]{2,1,0:T(8,128)(2,1)S(1)} collective-permute-done((bf16[4,160,640]{2,1,0:T(8,128)(2,1)S(1)}, bf16[4,160,640]{2,1,0:T(8,128)(2,1)S(1)}, u32[]{:S(2)}, u32[]{:S(2)}) %collective-permute-start.7) | collective-permute-done | bytes 819232 | tf_op jit(solution)/shard_map/ppermute | solution.py:209
  63.3 0.5 collective-permute-start.14
  63.9 1.8 %collective-permute-done.14.refs_7_ = bf16[4,160,640]{2,1,0:T(8,128)(2,1)S(1)} collective-permute-done((bf16[4,160,640]{2,1,0:T(8,128)(2,1)S(1)}, bf16[4,160,640]{2,1,0:T(8,128)(2,1)S(1)}, u32[]{:S(2)}, u32[]{:S(2)}) %collective-permute-start.14) | collective-permute-done | bytes 819232 | tf_op jit(solution)/shard_map/ppermute | solution.py:204
  65.7 0.5 weights_b.1.refs_5_
  66.3 0.6 collective-permute-done.13.refs_7_
  66.9 0.5 weights_a.1.refs_4_
  67.5 7.2 %collective-permute-start.15 = (bf16[128,1280]{1,0:T(8,128)(2,1)S(1)}, bf16[128,1280]{1,0:T(8,128)(2,1)S(1)}, u32[]{:S(2)}, u32[]{:S(2)}) collective-permute-start(bf16[128,1280]{1,0:T(8,128)(2,1)S(1)} %stage_1.2), channel_id=1, source_target_pairs={{0,1},{1,0},{2,3},{3,2},{4,5},{5,4},{6,7},{7,6},{8,9},{9,8},{10,11... | collective-permute-start | bytes 983048 | tf_op jit(solution)/shard_map/ppermute | solution.py:214
  74.6 5.1 %collective-permute-start.17 = (bf16[128,1280]{1,0:T(8,128)(2,1)S(1)}, bf16[128,1280]{1,0:T(8,128)(2,1)S(1)}, u32[]{:S(2)}, u32[]{:S(2)}) collective-permute-start(bf16[128,1280]{1,0:T(8,128)(2,1)S(1)} %stage_1.3), channel_id=1, source_target_pairs={{0,1},{1,0},{2,3},{3,2},{4,5},{5,4},{6,7},{7,6},{8,9},{9,8},{10,11... | collective-permute-start | bytes 983048 | tf_op jit(solution)/shard_map/ppermute | solution.py:214
  79.8 3.4 %collective-permute-done.15.refs_0_ = bf16[128,1280]{1,0:T(8,128)(2,1)S(1)} collective-permute-done((bf16[128,1280]{1,0:T(8,128)(2,1)S(1)}, bf16[128,1280]{1,0:T(8,128)(2,1)S(1)}, u32[]{:S(2)}, u32[]{:S(2)}) %collective-permute-start.15) | collective-permute-done | bytes 327712 | tf_op jit(solution)/shard_map/ppermute | solution.py:214
  83.2 5.3 %stage_2.2 = bf16[32,5120]{1,0:T(8,128)(2,1)S(1)} custom-call(bf16[128,1280]{1,0:T(8,128)(2,1)S(1)} %collective-permute-done.15.refs_0_, s32[1,128]{1,0:T(1,128)S(1)} %collective-permute-done.6.refs_1_, f32[4,1,1280]{2,1,0:T(1,128)S(1)} %reshape.6.refs_2_, f32[1,1280]{1,0:T(1,128)S(1)} %reshape.7.refs_3_, bf16[4,1280,640]{2,1,0:T(8,128)(2,1)S(1)} %weights_a.1.refs_4_, ...), custom_call_target="tpu_custom_call" | custom-call | flops 1 | bytes 1 | tf_op jit(solution)/shard_map/stage_2/pallas_call | solution.py:100
  88.5 1.4 %collective-permute-done.17.refs_0_ = bf16[128,1280]{1,0:T(8,128)(2,1)S(1)} collective-permute-done((bf16[128,1280]{1,0:T(8,128)(2,1)S(1)}, bf16[128,1280]{1,0:T(8,128)(2,1)S(1)}, u32[]{:S(2)}, u32[]{:S(2)}) %collective-permute-start.17) | collective-permute-done | bytes 327712 | tf_op jit(solution)/shard_map/ppermute | solution.py:214
  89.9 5.3 %stage_2.3.two_ref = bf16[32,5120]{1,0:T(8,128)(2,1)S(1)} custom-call(bf16[128,1280]{1,0:T(8,128)(2,1)S(1)} %collective-permute-done.17.refs_0_, s32[1,128]{1,0:T(1,128)S(1)} %copy-done.3, f32[4,1,1280]{2,1,0:T(1,128)S(1)} %reshape.6.refs_2_, f32[1,1280]{1,0:T(1,128)S(1)} %reshape.7.refs_3_, bf16[4,1280,640]{2,1,0:T(8,128)(2,1)S(1)} %weights_a.1.refs_4_, ...), custom_call_target="tpu_custom_call" | custom-call | flops 1 | bytes 1 | tf_op jit(solution)/shard_map/stage_2/pallas_call | solution.py:100
  95.1 2.5 %collective-permute-done.16.one_ref = bf16[32,5120]{1,0:T(8,128)(2,1)S(1)} collective-permute-done((bf16[32,5120]{1,0:T(8,128)(2,1)S(1)}, bf16[32,5120]{1,0:T(8,128)(2,1)S(1)}, u32[]{:S(2)}, u32[]{:S(2)}) %collective-permute-start.16) | collective-permute-done | bytes 327712 | tf_op jit(solution)/shard_map/ppermute | solution.py:214
  97.6 0.7 choose.1
  (26 shorter events, 0.4 us)
Async XLA Ops:
  0.0 1.7 %copy-start = (bf16[4,160,1920]{2,1,0:T(8,128)(2,1)S(1)}, bf16[4,160,1920]{2,1,0:T(8,128)(2,1)}, u32[]{:S(2)}) copy-start(bf16[4,160,1920]{2,1,0:T(8,128)(2,1)} %qkv.1) | copy-start | bytes 7372804
  1.7 1.1 %copy-start.1 = (bf16[4,80,1280]{2,1,0:T(8,128)(2,1)S(1)}, bf16[4,80,1280]{2,1,0:T(8,128)(2,1)}, u32[]{:S(2)}) copy-start(bf16[4,80,1280]{2,1,0:T(8,128)(2,1)} %out.1) | copy-start | bytes 2457604
  2.8 8.3 %copy-start.2 = (bf16[128,1280]{1,0:T(8,128)(2,1)S(1)}, bf16[128,1280]{1,0:T(8,128)(2,1)}, u32[]{:S(2)}) copy-start(bf16[128,1280]{1,0:T(8,128)(2,1)} %refs_0_.1) | copy-start | bytes 983044
  2.8 21.4 %copy-start.3 = (s32[1,128]{1,0:T(1,128)S(1)}, s32[1,128]{1,0:T(1,128)}, u32[]{:S(2)}) copy-start(s32[1,128]{1,0:T(1,128)} %refs_1_.3) | copy-start | bytes 1540
  2.8 61.1 %copy-start.4 = (f32[4,1280]{1,0:T(4,128)S(1)}, f32[4,1280]{1,0:T(4,128)}, u32[]{:S(2)}) copy-start(f32[4,1280]{1,0:T(4,128)} %param.8) | copy-start | bytes 61444
  2.8 61.1 %copy-start.5 = (f32[1280]{0:T(1024)S(1)}, f32[1280]{0:T(1024)}, u32[]{:S(2)}) copy-start(f32[1280]{0:T(1024)} %param.11) | copy-start | bytes 15364
  3.1 4.6 %collective-permute-start = (bf16[8,160,640]{2,1,0:T(8,128)(2,1)S(1)}, bf16[8,160,640]{2,1,0:T(8,128)(2,1)S(1)}, u32[]{:S(2)}, u32[]{:S(2)}) collective-permute-start(bf16[8,160,640]{2,1,0:T(8,128)(2,1)S(1)} %get-tuple-element.27), channel_id=1, source_target_pairs={{0,4},{4,0},{8,12},{12,8},{16,20},{20,16},{24,28},{28,24},{1,5},{5... | collective-permute-start | bytes 4915208 | tf_op jit(solution)/shard_map/ppermute | solution.py:204
  3.6 20.5 %collective-permute-start.1 = (bf16[4,160,640]{2,1,0:T(8,128)(2,1)S(1)}, bf16[4,160,640]{2,1,0:T(8,128)(2,1)S(1)}, u32[]{:S(2)}, u32[]{:S(2)}) collective-permute-start(bf16[4,160,640]{2,1,0:T(8,128)(2,1)S(1)} %get-tuple-element.26.refs_0_), channel_id=1, source_target_pairs={{0,8},{4,20},{8,0},{12,28},{16,24},{20,4},{24,16},{28,12},{1,9},{5... | collective-permute-start | bytes 2457608 | tf_op jit(solution)/shard_map/ppermute | solution.py:209
  6.2 21.2 %collective-permute-start.2 = (bf16[4,160,640]{2,1,0:T(8,128)(2,1)S(1)}, bf16[4,160,640]{2,1,0:T(8,128)(2,1)S(1)}, u32[]{:S(2)}, u32[]{:S(2)}) collective-permute-start(bf16[4,160,640]{2,1,0:T(8,128)(2,1)S(1)} %get-tuple-element.26.refs_0_), channel_id=1, source_target_pairs={{0,16},{4,12},{8,24},{12,4},{16,0},{20,28},{24,8},{28,20},{1,17},{... | collective-permute-start | bytes 2457608 | tf_op jit(solution)/shard_map/ppermute | solution.py:209
  7.7 34.0 %collective-permute-start.3 = (bf16[4,160,640]{2,1,0:T(8,128)(2,1)S(1)}, bf16[4,160,640]{2,1,0:T(8,128)(2,1)S(1)}, u32[]{:S(2)}, u32[]{:S(2)}) collective-permute-start(bf16[4,160,640]{2,1,0:T(8,128)(2,1)S(1)} %get-tuple-element.30.refs_0_), channel_id=1, source_target_pairs={{0,8},{4,20},{8,0},{12,28},{16,24},{20,4},{24,16},{28,12},{1,9},{5... | collective-permute-start | bytes 2457608 | tf_op jit(solution)/shard_map/ppermute | solution.py:209
  9.6 33.0 %collective-permute-start.4 = (bf16[4,160,640]{2,1,0:T(8,128)(2,1)S(1)}, bf16[4,160,640]{2,1,0:T(8,128)(2,1)S(1)}, u32[]{:S(2)}, u32[]{:S(2)}) collective-permute-start(bf16[4,160,640]{2,1,0:T(8,128)(2,1)S(1)} %get-tuple-element.30.refs_0_), channel_id=1, source_target_pairs={{0,16},{4,12},{8,24},{12,4},{16,0},{20,28},{24,8},{28,20},{1,17},{... | collective-permute-start | bytes 2457608 | tf_op jit(solution)/shard_map/ppermute | solution.py:209
  11.2 17.1 %collective-permute-start.5 = (bf16[128,1280]{1,0:T(8,128)(2,1)S(1)}, bf16[128,1280]{1,0:T(8,128)(2,1)S(1)}, u32[]{:S(2)}, u32[]{:S(2)}) collective-permute-start(bf16[128,1280]{1,0:T(8,128)(2,1)S(1)} %copy-done.2), channel_id=1, source_target_pairs={{0,1},{1,0},{2,3},{3,2},{4,5},{5,4},{6,7},{7,6},{8,9},{9,8},{10,11... | collective-permute-start | bytes 983048 | tf_op jit(solution)/shard_map/ppermute | solution.py:214
  24.2 4.1 %collective-permute-start.6 = (s32[1,128]{1,0:T(1,128)S(1)}, s32[1,128]{1,0:T(1,128)S(1)}, u32[]{:S(2)}, u32[]{:S(2)}) collective-permute-start(s32[1,128]{1,0:T(1,128)S(1)} %copy-done.3), channel_id=1, source_target_pairs={{0,1},{1,0},{2,3},{3,2},{4,5},{5,4},{6,7},{7,6},{8,9},{9,8},{10,11... | collective-permute-start | bytes 1544 | tf_op jit(solution)/shard_map/ppermute | solution.py:214
  42.6 4.0 %collective-permute-start.12 = (bf16[4,160,640]{2,1,0:T(8,128)(2,1)S(1)}, bf16[4,160,640]{2,1,0:T(8,128)(2,1)S(1)}, u32[]{:S(2)}, u32[]{:S(2)}) collective-permute-start(bf16[4,160,640]{2,1,0:T(8,128)(2,1)S(1)} %collective-permute-done.4.refs_3_), channel_id=1, source_target_pairs={{0,4},{4,0},{8,12},{12,8},{16,20},{20,16},{24,28},{28,24},{1,5},{5... | collective-permute-start | bytes 2457608 | tf_op jit(solution)/shard_map/ppermute | solution.py:204
  42.7 20.6 %collective-permute-start.8 = (bf16[4,160,640]{2,1,0:T(8,128)(2,1)S(1)}, bf16[4,160,640]{2,1,0:T(8,128)(2,1)S(1)}, u32[]{:S(2)}, u32[]{:S(2)}) collective-permute-start(bf16[4,160,640]{2,1,0:T(8,128)(2,1)S(1)} %collective-permute-done.4.refs_3_), channel_id=1, source_target_pairs={{0,8},{4,20},{8,0},{12,28},{16,24},{20,4},{24,16},{28,12},{1,9},{5... | collective-permute-start | bytes 2457608 | tf_op jit(solution)/shard_map/ppermute | solution.py:209
  44.7 18.6 %collective-permute-start.7 = (bf16[4,160,640]{2,1,0:T(8,128)(2,1)S(1)}, bf16[4,160,640]{2,1,0:T(8,128)(2,1)S(1)}, u32[]{:S(2)}, u32[]{:S(2)}) collective-permute-start(bf16[4,160,640]{2,1,0:T(8,128)(2,1)S(1)} %collective-permute-done.1.refs_2_), channel_id=1, source_target_pairs={{0,16},{4,12},{8,24},{12,4},{16,0},{20,28},{24,8},{28,20},{1,17},{... | collective-permute-start | bytes 2457608 | tf_op jit(solution)/shard_map/ppermute | solution.py:209
  46.1 17.2 %collective-permute-start.9 = (bf16[4,160,640]{2,1,0:T(8,128)(2,1)S(1)}, bf16[4,160,640]{2,1,0:T(8,128)(2,1)S(1)}, u32[]{:S(2)}, u32[]{:S(2)}) collective-permute-start(bf16[4,160,640]{2,1,0:T(8,128)(2,1)S(1)} %collective-permute-done.1.refs_2_), channel_id=1, source_target_pairs={{0,4},{4,0},{8,12},{12,8},{16,20},{20,16},{24,28},{28,24},{1,5},{5... | collective-permute-start | bytes 2457608 | tf_op jit(solution)/shard_map/ppermute | solution.py:204
  46.1 17.2 %collective-permute-start.10 = (bf16[4,160,640]{2,1,0:T(8,128)(2,1)S(1)}, bf16[4,160,640]{2,1,0:T(8,128)(2,1)S(1)}, u32[]{:S(2)}, u32[]{:S(2)}) collective-permute-start(bf16[4,160,640]{2,1,0:T(8,128)(2,1)S(1)} %collective-permute-done.2.refs_3_), channel_id=1, source_target_pairs={{0,4},{4,0},{8,12},{12,8},{16,20},{20,16},{24,28},{28,24},{1,5},{5... | collective-permute-start | bytes 2457608 | tf_op jit(solution)/shard_map/ppermute | solution.py:204
  46.6 16.7 %collective-permute-start.11 = (bf16[4,160,640]{2,1,0:T(8,128)(2,1)S(1)}, bf16[4,160,640]{2,1,0:T(8,128)(2,1)S(1)}, u32[]{:S(2)}, u32[]{:S(2)}) collective-permute-start(bf16[4,160,640]{2,1,0:T(8,128)(2,1)S(1)} %collective-permute-done.3.refs_2_), channel_id=1, source_target_pairs={{0,4},{4,0},{8,12},{12,8},{16,20},{20,16},{24,28},{28,24},{1,5},{5... | collective-permute-start | bytes 2457608 | tf_op jit(solution)/shard_map/ppermute | solution.py:204
  63.3 2.4 %collective-permute-start.14 = (bf16[4,160,640]{2,1,0:T(8,128)(2,1)S(1)}, bf16[4,160,640]{2,1,0:T(8,128)(2,1)S(1)}, u32[]{:S(2)}, u32[]{:S(2)}) collective-permute-start(bf16[4,160,640]{2,1,0:T(8,128)(2,1)S(1)} %collective-permute-done.8.refs_4_), channel_id=1, source_target_pairs={{0,4},{4,0},{8,12},{12,8},{16,20},{20,16},{24,28},{28,24},{1,5},{5... | collective-permute-start | bytes 2457608 | tf_op jit(solution)/shard_map/ppermute | solution.py:204
  63.8 3.1 %collective-permute-start.13 = (bf16[4,160,640]{2,1,0:T(8,128)(2,1)S(1)}, bf16[4,160,640]{2,1,0:T(8,128)(2,1)S(1)}, u32[]{:S(2)}, u32[]{:S(2)}) collective-permute-start(bf16[4,160,640]{2,1,0:T(8,128)(2,1)S(1)} %collective-permute-done.7.refs_4_), channel_id=1, source_target_pairs={{0,4},{4,0},{8,12},{12,8},{16,20},{20,16},{24,28},{28,24},{1,5},{5... | collective-permute-start | bytes 2457608 | tf_op jit(solution)/shard_map/ppermute | solution.py:204
  67.5 15.7 %collective-permute-start.15 = (bf16[128,1280]{1,0:T(8,128)(2,1)S(1)}, bf16[128,1280]{1,0:T(8,128)(2,1)S(1)}, u32[]{:S(2)}, u32[]{:S(2)}) collective-permute-start(bf16[128,1280]{1,0:T(8,128)(2,1)S(1)} %stage_1.2), channel_id=1, source_target_pairs={{0,1},{1,0},{2,3},{3,2},{4,5},{5,4},{6,7},{7,6},{8,9},{9,8},{10,11... | collective-permute-start | bytes 983048 | tf_op jit(solution)/shard_map/ppermute | solution.py:214
  74.6 15.3 %collective-permute-start.17 = (bf16[128,1280]{1,0:T(8,128)(2,1)S(1)}, bf16[128,1280]{1,0:T(8,128)(2,1)S(1)}, u32[]{:S(2)}, u32[]{:S(2)}) collective-permute-start(bf16[128,1280]{1,0:T(8,128)(2,1)S(1)} %stage_1.3), channel_id=1, source_target_pairs={{0,1},{1,0},{2,3},{3,2},{4,5},{5,4},{6,7},{7,6},{8,9},{9,8},{10,11... | collective-permute-start | bytes 983048 | tf_op jit(solution)/shard_map/ppermute | solution.py:214
  88.4 9.2 %collective-permute-start.16 = (bf16[32,5120]{1,0:T(8,128)(2,1)S(1)}, bf16[32,5120]{1,0:T(8,128)(2,1)S(1)}, u32[]{:S(2)}, u32[]{:S(2)}) collective-permute-start(bf16[32,5120]{1,0:T(8,128)(2,1)S(1)} %stage_2.2), channel_id=1, source_target_pairs={{0,1},{1,0},{2,3},{3,2},{4,5},{5,4},{6,7},{7,6},{8,9},{9,8},{10,11... | collective-permute-start | bytes 983048 | tf_op jit(solution)/shard_map/ppermute | solution.py:214

commit v5 on v3

--- a/solution.py
+++ b/solution.py
@@ -114,34 +114,54 @@
     )(*args)
 
 
-def assemble_kernel(first, *refs):
-    *blocks, whole = refs
+def assemble_kernel(*refs):
+    blocks, whole = refs[:-2], refs[-2:]
+    turned = flipped()
+    for swapped in (False, True):
+        pl.when(turned == swapped)(
+            functools.partial(put_in_order, blocks, whole[::-1] if swapped else whole)
+        )
+
+
+def put_in_order(blocks, whole):
     me = lax.axis_index("dp")
     one = jnp.where(me % 2 == 0, 2, 4)
-    distances = (0, 1, one, 6 - one, 6, 7 - one, 1 + one, 7)
-    for i, (distance, block) in enumerate(zip(distances, blocks)):
-        owner = jnp.bitwise_xor(me, distance)
-        for unit in range(whole.shape[0]):
-            at = unit + (first if i == 1 else 0)
-            if unit < 3:
-                whole[unit, pl.ds(pl.multiple_of(owner * 160, 16), 160)] = block[at]
-            else:
-                for half in range(2):
-                    where = pl.multiple_of(owner * 80 + half * WIDTH, 16)
-                    whole[unit, pl.ds(where, 80)] = block[at, half * 80 : half * 80 + 80]
-
-
-def assemble(name, own, own_other, first, blocks, others):
+    for which in range(2):
+        for i, distance in enumerate((0, one, 6 - one, 6, 1, 7 - one, 1 + one, 7)):
+            block = blocks[8 * which + i]
+            first = 4 * which if block.shape[0] == 8 else 0
+            owner = jnp.bitwise_xor(me, distance)
+            for unit in range(3):
+                where = pl.ds(pl.multiple_of(owner * 160, 16), 160)
+                whole[which][unit, where] = block[first + unit]
+            for half in range(2):
+                where = pl.ds(pl.multiple_of(owner * 80 + half * WIDTH, 16), 80)
+                whole[which][3, where] = block[first + 3, half * 80 : half * 80 + 80]
+
+
+def assemble(p, q):
     vmem = pl.BlockSpec(memory_space=pltpu.VMEM)
     return pl.pallas_call(
-        functools.partial(assemble_kernel, first),
-        out_shape=jax.ShapeDtypeStruct((own.shape[0], D_VIS, WIDTH), jnp.bfloat16),
-        in_specs=[vmem] * 8,
-        out_specs=vmem,
+        assemble_kernel,
+        out_shape=[jax.ShapeDtypeStruct((4, D_VIS, WIDTH), jnp.bfloat16)] * 2,
+        in_specs=[vmem] * 16,
+        out_specs=[vmem] * 2,
         compiler_params=pltpu.CompilerParams(vmem_limit_bytes=8 * 1024 * 1024),
         cost_estimate=SMALL,
-        name=name,
-    )(own, own_other, *blocks, *others)
+        name="assemble",
+    )(*p, *q)
+
+
+def choose_kernel(one_ref, two_ref, out_ref):
+    first = first_stage()
+
+    @pl.when(first)
+    def _():
+        out_ref[...] = one_ref[...]
+
+    @pl.when(jnp.logical_not(first))
+    def _():
+        out_ref[...] = two_ref[...]
 
 
 def first_stage():
@@ -149,15 +169,21 @@
     return (place == 1) | (place == 2)
 
 
-def pack_kernel(qkv, out, chunk_a, chunk_b, chunks):
-    section = jnp.where(first_stage(), 0, 2)
-    for which, chunk in enumerate((chunk_a, chunk_b)):
+def flipped():
+    return lax.axis_index("phase") % 4 == 2
+
+
+def pack_kernel(qkv, out, chunk_p, chunk_q, chunks):
+    first = jnp.where(first_stage(), 0, 2)
+    turned = jnp.where(flipped(), 1, 0)
+    for which, chunk in enumerate((chunk_p, chunk_q)):
+        section = first + jnp.bitwise_xor(turned, which)
         for i in range(3):
-            unit = qkv[section + which, :, i * WIDTH : (i + 1) * WIDTH]
+            unit = qkv[section, :, i * WIDTH : (i + 1) * WIDTH]
             chunk[i] = unit
             chunks[4 * which + i] = unit
         for half in range(2):
-            unit = out[section + which, :, half * WIDTH : (half + 1) * WIDTH]
+            unit = out[section, :, half * WIDTH : (half + 1) * WIDTH]
             chunk[3, half * 80 : half * 80 + 80] = unit
             chunks[4 * which + 3, half * 80 : half * 80 + 80] = unit
 
@@ -175,6 +201,19 @@
     )(w_qkv, w_out)
 
 
+def choose(name, one, two):
+    vmem = pl.BlockSpec(memory_space=pltpu.VMEM)
+    return pl.pallas_call(
+        choose_kernel,
+        out_shape=jax.ShapeDtypeStruct(one.shape, one.dtype),
+        in_specs=[vmem] * 2,
+        out_specs=vmem,
+        compiler_params=pltpu.CompilerParams(vmem_limit_bytes=8 * 1024 * 1024),
+        cost_estimate=SMALL,
+        name=name,
+    )(one, two)
+
+
 def cores(block):
     return lax.ppermute(block, "dp", [(j, j ^ 1) for j in range(lax.axis_size("dp"))])
 
@@ -182,6 +221,16 @@
 def plane(block, turn):
     pairs = [(j, j ^ (2 if j % 2 == turn else 4)) for j in range(lax.axis_size("dp"))]
     return lax.ppermute(block, "dp", pairs)
+
+
+def planes_or_plane(block):
+    cores_, planes = lax.axis_size("dp"), lax.axis_size("phase")
+    pairs = []
+    for j in range(cores_):
+        for z in range(planes):
+            to = (j, z ^ 3) if z % 4 in (1, 2) else (j ^ (2 if j % 2 == 0 else 4), z)
+            pairs.append((j * planes + z, to[0] * planes + to[1]))
+    return lax.ppermute(block, ("dp", "phase"), pairs)
 
 
 def across(block):
@@ -194,26 +243,21 @@
     gains = norm_gain.reshape(SECTIONS, 1, D_VIS)
     merge = merge_gain.reshape(1, D_VIS)
 
-    chunk_a, chunk_b, chunks = pack(w_qkv, w_out)
-    a1, a2 = plane(chunk_a, 0), plane(chunk_a, 1)
+    chunk_p, chunk_q, chunks = pack(w_qkv, w_out)
+    p1, p2 = plane(chunk_p, 0), plane(chunk_p, 1)
     own_other = cores(chunks)
-    own_other, b, theirs, their_ids = tie((own_other, chunk_b, patches, window_ids))
-    b1, b2 = plane(b, 0), plane(b, 1)
+    own_other, late_q, theirs, their_ids = tie((own_other, chunk_q, patches, window_ids))
+    q2 = plane(late_q, 1)
     other, other_ids = across(theirs), across(their_ids)
-    a1, a2, b1, b2, other, other_ids = tie((a1, a2, b1, b2, other, other_ids))
-    a3, b3 = plane(a1, 1), plane(b2, 0)
-    a1_other, a2_other, b1_other, b2_other = (cores(block) for block in (a1, a2, b1, b2))
-    a3, b3, a1_other, a2_other, b1_other, b2_other = tie(
-        (a3, b3, a1_other, a2_other, b1_other, b2_other)
+    p1, p2, q2, other, other_ids = tie((p1, p2, q2, other, other_ids))
+    q1 = planes_or_plane(choose("relay", p1, chunk_q))
+    p3, q3 = plane(p1, 1), plane(q2, 0)
+    p1_other, p2_other, q2_other = cores(p1), cores(p2), cores(q2)
+    q1, p3, q3, p1_other, p2_other, q2_other = tie((q1, p3, q3, p1_other, p2_other, q2_other))
+    weights = assemble(
+        (chunk_p, p1, p2, p3, own_other, p1_other, p2_other, cores(p3)),
+        (chunk_q, q1, q2, q3, own_other, cores(q1), q2_other, cores(q3)),
     )
-    weights = [
-        assemble(
-            "weights_a", chunk_a, own_other, 0, (a1, a2, a3), (a1_other, a2_other, cores(a3))
-        ),
-        assemble(
-            "weights_b", chunk_b, own_other, 4, (b1, b2, b3), (b1_other, b2_other, cores(b3))
-        ),
-    ]
 
     half_own = run_stage(1, patches, window_ids, gains, merge, weights)
     half_own_far = across(half_own)
@@ -224,7 +268,7 @@
     back = across(result_other)
     half_other_far, result_other = tie((half_other_far, result_other))
     result_own = run_stage(2, half_other_far, window_ids, gains, merge, weights)
-    return jnp.where(first_stage(), back, result_own)
+    return choose("result", back, result_own)
 
 
 def plain_section(acts, marks, gain, weight_qkv, weight_out):

time: 102 us -> 94.6 us (0.927)
  starting transfers between devices: 29.1 us -> 20.5 us
  waiting for transfers between devices: 51.2 us -> 58.1 us
  local copies, waits for them, and re-layouts: 8.6 us -> 2.87 us
    ppermute x0 -> x1, waiting for transfers between devices: none -> 16.3 us  [planes_or_plane(): return lax.ppermute(block, ('dp', 'phase'), pairs)]
    ppermute x6 -> x5, waiting for transfers between devices: 43.1 us -> 31.5 us  [plane(): return lax.ppermute(block, 'dp', pairs)]
    ppermute x5, starting transfers between devices: 16.5 us -> 9.08 us  [across(): return lax.ppermute(block, 'phase', [(j, j ^ 1) for j in range(size)])]
    unnamed x20 -> x12, local copies, waits for them, and re-layouts: 8.58 us -> 2.85 us
    ppermute x6 -> x5, starting transfers between devices: 10.9 us -> 8.07 us  [plane(): return lax.ppermute(block, 'dp', pairs)]
    ppermute x0 -> x1, starting transfers between devices: none -> 1.78 us  [planes_or_plane(): return lax.ppermute(block, ('dp', 'phase'), pairs)]
    ppermute x7, waiting for transfers between devices: 2.44 us -> 4.13 us  [cores(): lax.ppermute(block, 'dp', [(j, j ^ 1) for j in range(lax.axis_size('dp'))])]
  transfers between devices with their start and end apart: 18 -> 18, of which waited for: 10 -> 12; matrix products, arithmetic and copies ran while one was open for 0% -> 0% of each run, Pallas kernels for 11% -> 11%
where the time goes in v5:
time: 94.6 us; the launch traced here: 94.4 us
  waiting for transfers between devices  58.1 us (61%)
  starting transfers between devices  20.5 us (22%)
  Pallas kernels  12.8 us (14%)
  local copies, waits for them, and re-layouts  2.87 us (3%)
    ppermute x5, waiting for transfers between devices, plane(): return lax.ppermute(block, 'dp', pairs)  31.5 us
    ppermute x1, waiting for transfers between devices, planes_or_plane(): return lax.ppermute(block, ('dp', 'phase'), pairs)  16.3 us
    pallas_call x4, Pallas kernels, run_stage(): pl.pallas_call(functools.partial(stage_kernel, stage), out_shape=jax.Shap...  10.7 us
    ppermute x5, starting transfers between devices, across(): return lax.ppermute(block, 'phase', [(j, j ^ 1) for j in range(size)])  9.08 us
    ppermute x5, starting transfers between devices, plane(): return lax.ppermute(block, 'dp', pairs)  8.07 us
    ppermute x5, waiting for transfers between devices, across(): return lax.ppermute(block, 'phase', [(j, j ^ 1) for j in range(size)])  6.26 us
    ppermute x7, waiting for transfers between devices, cores(): lax.ppermute(block, 'dp', [(j, j ^ 1) for j in range(lax.axis_size('dp'))])  4.13 us
    unnamed x12, local copies, waits for them, and re-layouts  2.85 us
  transfers between devices with their start and end apart: 18, of which 12 were waited for; matrix products, arithmetic and copies ran while one was open for 0% of the time, Pallas kernels for 11%

profile of v5, /device:TPU:0, one launch (start us, length us, event | category | flops | bytes accessed | tf_op | source)
XLA Modules:
  0.0 94.4 jit_solution(741630814148805658)
XLA Ops:
  0.0 1.7 %copy-done = bf16[4,160,1920]{2,1,0:T(8,128)(2,1)S(1)} copy-done((bf16[4,160,1920]{2,1,0:T(8,128)(2,1)S(1)}, bf16[4,160,1920]{2,1,0:T(8,128)(2,1)}, u32[]{:S(2)}) %copy-start) | copy-done | bytes 2457624
  1.7 1.1 %copy-done.1 = bf16[4,80,1280]{2,1,0:T(8,128)(2,1)S(1)} copy-done((bf16[4,80,1280]{2,1,0:T(8,128)(2,1)S(1)}, bf16[4,80,1280]{2,1,0:T(8,128)(2,1)}, u32[]{:S(2)}) %copy-start.1) | copy-done | bytes 819224
  2.9 0.3 pack.1
  3.1 0.5 collective-permute-start.2
  3.6 2.6 %collective-permute-start = (bf16[4,160,640]{2,1,0:T(8,128)(2,1)S(1)}, bf16[4,160,640]{2,1,0:T(8,128)(2,1)S(1)}, u32[]{:S(2)}, u32[]{:S(2)}) collective-permute-start(bf16[4,160,640]{2,1,0:T(8,128)(2,1)S(1)} %get-tuple-element.27.refs_0_), channel_id=1, source_target_pairs={{0,8},{4,20},{8,0},{12,28},{16,24},{20,4},{24,16},{28,12},{1,9},{5... | collective-permute-start | bytes 2457608 | tf_op jit(solution)/shard_map/ppermute | solution.py:223
  6.2 1.5 %collective-permute-start.1 = (bf16[4,160,640]{2,1,0:T(8,128)(2,1)S(1)}, bf16[4,160,640]{2,1,0:T(8,128)(2,1)S(1)}, u32[]{:S(2)}, u32[]{:S(2)}) collective-permute-start(bf16[4,160,640]{2,1,0:T(8,128)(2,1)S(1)} %get-tuple-element.27.refs_0_), channel_id=1, source_target_pairs={{0,16},{4,12},{8,24},{12,4},{16,0},{20,28},{24,8},{28,20},{1,17},{... | collective-permute-start | bytes 2457608 | tf_op jit(solution)/shard_map/ppermute | solution.py:223
  7.7 1.9 %collective-permute-start.3 = (bf16[4,160,640]{2,1,0:T(8,128)(2,1)S(1)}, bf16[4,160,640]{2,1,0:T(8,128)(2,1)S(1)}, u32[]{:S(2)}, u32[]{:S(2)}) collective-permute-start(bf16[4,160,640]{2,1,0:T(8,128)(2,1)S(1)} %get-tuple-element.30.two_ref.refs_8_), channel_id=1, source_target_pairs={{0,16},{4,12},{8,24},{12,4},{16,0},{20,28},{24,8},{28,20},{1,17},{... | collective-permute-start | bytes 2457608 | tf_op jit(solution)/shard_map/ppermute | solution.py:223
  9.7 1.6 %collective-permute-start.4 = (bf16[128,1280]{1,0:T(8,128)(2,1)S(1)}, bf16[128,1280]{1,0:T(8,128)(2,1)S(1)}, u32[]{:S(2)}, u32[]{:S(2)}) collective-permute-start(bf16[128,1280]{1,0:T(8,128)(2,1)S(1)} %copy-done.2), channel_id=1, source_target_pairs={{0,1},{1,0},{2,3},{3,2},{4,5},{5,4},{6,7},{7,6},{8,9},{9,8},{10,11... | collective-permute-start | bytes 983048 | tf_op jit(solution)/shard_map/ppermute | solution.py:238
  11.2 0.4 collective-permute-start.5
  11.7 12.5 %collective-permute-done.one_ref.refs_1_ = bf16[4,160,640]{2,1,0:T(8,128)(2,1)S(1)} collective-permute-done((bf16[4,160,640]{2,1,0:T(8,128)(2,1)S(1)}, bf16[4,160,640]{2,1,0:T(8,128)(2,1)S(1)}, u32[]{:S(2)}, u32[]{:S(2)}) %collective-permute-start) | collective-permute-done | bytes 819232 | tf_op jit(solution)/shard_map/ppermute | solution.py:223
  24.2 0.9 collective-permute-done.1.refs_2_
  25.1 8.8 %collective-permute-done.3.refs_10_ = bf16[4,160,640]{2,1,0:T(8,128)(2,1)S(1)} collective-permute-done((bf16[4,160,640]{2,1,0:T(8,128)(2,1)S(1)}, bf16[4,160,640]{2,1,0:T(8,128)(2,1)S(1)}, u32[]{:S(2)}, u32[]{:S(2)}) %collective-permute-start.3) | collective-permute-done | bytes 819232 | tf_op jit(solution)/shard_map/ppermute | solution.py:223
  33.9 1.8 %collective-permute-start.6 = (bf16[4,160,640]{2,1,0:T(8,128)(2,1)S(1)}, bf16[4,160,640]{2,1,0:T(8,128)(2,1)S(1)}, u32[]{:S(2)}, u32[]{:S(2)}) collective-permute-start(bf16[4,160,640]{2,1,0:T(8,128)(2,1)S(1)} %relay.1), channel_id=1, source_target_pairs={{0,8},{1,2},{2,1},{3,11},{4,20},{5,6},{6,5},{7,23},{8,0},{9,10},{1... | collective-permute-start | bytes 2457608 | tf_op jit(solution)/shard_map/ppermute | solution.py:233
  35.7 1.5 %collective-permute-start.7 = (bf16[4,160,640]{2,1,0:T(8,128)(2,1)S(1)}, bf16[4,160,640]{2,1,0:T(8,128)(2,1)S(1)}, u32[]{:S(2)}, u32[]{:S(2)}) collective-permute-start(bf16[4,160,640]{2,1,0:T(8,128)(2,1)S(1)} %collective-permute-done.one_ref.refs_1_), channel_id=1, source_target_pairs={{0,16},{4,12},{8,24},{12,4},{16,0},{20,28},{24,8},{28,20},{1,17},{... | collective-permute-start | bytes 2457608 | tf_op jit(solution)/shard_map/ppermute | solution.py:223
  37.2 0.5 collective-permute-start.11
  37.7 0.5 collective-permute-start.8
  38.3 16.3 %collective-permute-done.6.refs_9_ = bf16[4,160,640]{2,1,0:T(8,128)(2,1)S(1)} collective-permute-done((bf16[4,160,640]{2,1,0:T(8,128)(2,1)S(1)}, bf16[4,160,640]{2,1,0:T(8,128)(2,1)S(1)}, u32[]{:S(2)}, u32[]{:S(2)}) %collective-permute-start.6) | collective-permute-done | bytes 819232 | tf_op jit(solution)/shard_map/ppermute | solution.py:233
  54.6 2.3 %collective-permute-done.7.refs_3_ = bf16[4,160,640]{2,1,0:T(8,128)(2,1)S(1)} collective-permute-done((bf16[4,160,640]{2,1,0:T(8,128)(2,1)S(1)}, bf16[4,160,640]{2,1,0:T(8,128)(2,1)S(1)}, u32[]{:S(2)}, u32[]{:S(2)}) %collective-permute-start.7) | collective-permute-done | bytes 819232 | tf_op jit(solution)/shard_map/ppermute | solution.py:223
  56.9 7.0 %collective-permute-done.8.refs_11_ = bf16[4,160,640]{2,1,0:T(8,128)(2,1)S(1)} collective-permute-done((bf16[4,160,640]{2,1,0:T(8,128)(2,1)S(1)}, bf16[4,160,640]{2,1,0:T(8,128)(2,1)S(1)}, u32[]{:S(2)}, u32[]{:S(2)}) %collective-permute-start.8) | collective-permute-done | bytes 819232 | tf_op jit(solution)/shard_map/ppermute | solution.py:223
  63.9 0.5 collective-permute-start.13
  64.4 1.8 %collective-permute-done.12.refs_7_ = bf16[4,160,640]{2,1,0:T(8,128)(2,1)S(1)} collective-permute-done((bf16[4,160,640]{2,1,0:T(8,128)(2,1)S(1)}, bf16[4,160,640]{2,1,0:T(8,128)(2,1)S(1)}, u32[]{:S(2)}, u32[]{:S(2)}) %collective-permute-start.12) | collective-permute-done | bytes 819232 | tf_op jit(solution)/shard_map/ppermute | solution.py:218
  66.2 1.2 %collective-permute-done.13.refs_13_ = bf16[4,160,640]{2,1,0:T(8,128)(2,1)S(1)} collective-permute-done((bf16[4,160,640]{2,1,0:T(8,128)(2,1)S(1)}, bf16[4,160,640]{2,1,0:T(8,128)(2,1)S(1)}, u32[]{:S(2)}, u32[]{:S(2)}) %collective-permute-start.13) | collective-permute-done | bytes 819232 | tf_op jit(solution)/shard_map/ppermute | solution.py:218
  67.4 1.2 %collective-permute-done.14.refs_15_ = bf16[4,160,640]{2,1,0:T(8,128)(2,1)S(1)} collective-permute-done((bf16[4,160,640]{2,1,0:T(8,128)(2,1)S(1)}, bf16[4,160,640]{2,1,0:T(8,128)(2,1)S(1)}, u32[]{:S(2)}, u32[]{:S(2)}) %collective-permute-start.14) | collective-permute-done | bytes 819232 | tf_op jit(solution)/shard_map/ppermute | solution.py:218
  68.6 1.0 %assemble.1 = (bf16[4,1280,640]{2,1,0:T(8,128)(2,1)S(1)}, bf16[4,1280,640]{2,1,0:T(8,128)(2,1)S(1)}) custom-call(bf16[4,160,640]{2,1,0:T(8,128)(2,1)S(1)} %get-tuple-element.27.refs_0_, bf16[4,160,640]{2,1,0:T(8,128)(2,1)S(1)} %collective-permute-done.one_ref.refs_1_, bf16[4,160,640]{2,1,0:T(8,128)(2,1)S(1)} %collective-permute-done.1.refs_2_, ...), custom_call_target="tpu_custom_call" | custom-call | flops 1 | bytes 1 | tf_op jit(solution)/shard_map/assemble/pallas_call | solution.py:144
  69.7 0.2 stage_1.3
  69.9 6.9 %collective-permute-start.17 = (bf16[128,1280]{1,0:T(8,128)(2,1)S(1)}, bf16[128,1280]{1,0:T(8,128)(2,1)S(1)}, u32[]{:S(2)}, u32[]{:S(2)}) collective-permute-start(bf16[128,1280]{1,0:T(8,128)(2,1)S(1)} %stage_1.3), channel_id=1, source_target_pairs={{0,1},{1,0},{2,3},{3,2},{4,5},{5,4},{6,7},{7,6},{8,9},{9,8},{10,11... | collective-permute-start | bytes 983048 | tf_op jit(solution)/shard_map/ppermute | solution.py:238
  76.8 3.4 %collective-permute-done.15.refs_0_ = bf16[128,1280]{1,0:T(8,128)(2,1)S(1)} collective-permute-done((bf16[128,1280]{1,0:T(8,128)(2,1)S(1)}, bf16[128,1280]{1,0:T(8,128)(2,1)S(1)}, u32[]{:S(2)}, u32[]{:S(2)}) %collective-permute-start.15) | collective-permute-done | bytes 327712 | tf_op jit(solution)/shard_map/ppermute | solution.py:238
  80.2 5.3 %stage_2.2 = bf16[32,5120]{1,0:T(8,128)(2,1)S(1)} custom-call(bf16[128,1280]{1,0:T(8,128)(2,1)S(1)} %collective-permute-done.15.refs_0_, s32[1,128]{1,0:T(1,128)S(1)} %collective-permute-done.5.refs_1_, f32[4,1,1280]{2,1,0:T(1,128)S(1)} %reshape.6.refs_2_, f32[1,1280]{1,0:T(1,128)S(1)} %reshape.7.refs_3_, ...), custom_call_target="tpu_custom_call" | custom-call | flops 1 | bytes 1 | tf_op jit(solution)/shard_map/stage_2/pallas_call | solution.py:100
  85.6 0.9 collective-permute-done.17.refs_0_
  86.5 5.3 %stage_2.3.two_ref = bf16[32,5120]{1,0:T(8,128)(2,1)S(1)} custom-call(bf16[128,1280]{1,0:T(8,128)(2,1)S(1)} %collective-permute-done.17.refs_0_, s32[1,128]{1,0:T(1,128)S(1)} %copy-done.3, f32[4,1,1280]{2,1,0:T(1,128)S(1)} %reshape.6.refs_2_, f32[1,1280]{1,0:T(1,128)S(1)} %reshape.7.refs_3_, bf16[4,1280,640]{2,1,0:T(8,128)(2,1)S(1)} %get-tuple-element.43.refs_4_, ...), custom_call_target="tpu_custom_call" | custom-call | flops 1 | bytes 1 | tf_op jit(solution)/shard_map/stage_2/pallas_call | solution.py:100
  91.7 2.0 %collective-permute-done.16.one_ref = bf16[32,5120]{1,0:T(8,128)(2,1)S(1)} collective-permute-done((bf16[32,5120]{1,0:T(8,128)(2,1)S(1)}, bf16[32,5120]{1,0:T(8,128)(2,1)S(1)}, u32[]{:S(2)}, u32[]{:S(2)}) %collective-permute-start.16) | collective-permute-done | bytes 327712 | tf_op jit(solution)/shard_map/ppermute | solution.py:238
  93.7 0.7 result.1
  (26 shorter events, 0.3 us)
Async XLA Ops:
  0.0 1.7 %copy-start = (bf16[4,160,1920]{2,1,0:T(8,128)(2,1)S(1)}, bf16[4,160,1920]{2,1,0:T(8,128)(2,1)}, u32[]{:S(2)}) copy-start(bf16[4,160,1920]{2,1,0:T(8,128)(2,1)} %qkv.1) | copy-start | bytes 7372804
  1.7 1.1 %copy-start.1 = (bf16[4,80,1280]{2,1,0:T(8,128)(2,1)S(1)}, bf16[4,80,1280]{2,1,0:T(8,128)(2,1)}, u32[]{:S(2)}) copy-start(bf16[4,80,1280]{2,1,0:T(8,128)(2,1)} %out.1) | copy-start | bytes 2457604
  2.8 6.8 %copy-start.2 = (bf16[128,1280]{1,0:T(8,128)(2,1)S(1)}, bf16[128,1280]{1,0:T(8,128)(2,1)}, u32[]{:S(2)}) copy-start(bf16[128,1280]{1,0:T(8,128)(2,1)} %refs_0_.1) | copy-start | bytes 983044
  2.8 8.4 %copy-start.3 = (s32[1,128]{1,0:T(1,128)S(1)}, s32[1,128]{1,0:T(1,128)}, u32[]{:S(2)}) copy-start(s32[1,128]{1,0:T(1,128)} %refs_1_.3) | copy-start | bytes 1540
  2.8 61.6 %copy-start.4 = (f32[4,1280]{1,0:T(4,128)S(1)}, f32[4,1280]{1,0:T(4,128)}, u32[]{:S(2)}) copy-start(f32[4,1280]{1,0:T(4,128)} %param.8) | copy-start | bytes 61444
  2.8 61.6 %copy-start.5 = (f32[1280]{0:T(1024)S(1)}, f32[1280]{0:T(1024)}, u32[]{:S(2)}) copy-start(f32[1280]{0:T(1024)} %param.11) | copy-start | bytes 15364
  3.1 4.6 %collective-permute-start.2 = (bf16[8,160,640]{2,1,0:T(8,128)(2,1)S(1)}, bf16[8,160,640]{2,1,0:T(8,128)(2,1)S(1)}, u32[]{:S(2)}, u32[]{:S(2)}) collective-permute-start(bf16[8,160,640]{2,1,0:T(8,128)(2,1)S(1)} %get-tuple-element.28), channel_id=1, source_target_pairs={{0,4},{4,0},{8,12},{12,8},{16,20},{20,16},{24,28},{28,24},{1,5},{5... | collective-permute-start | bytes 4915208 | tf_op jit(solution)/shard_map/ppermute | solution.py:218
  3.6 20.5 %collective-permute-start = (bf16[4,160,640]{2,1,0:T(8,128)(2,1)S(1)}, bf16[4,160,640]{2,1,0:T(8,128)(2,1)S(1)}, u32[]{:S(2)}, u32[]{:S(2)}) collective-permute-start(bf16[4,160,640]{2,1,0:T(8,128)(2,1)S(1)} %get-tuple-element.27.refs_0_), channel_id=1, source_target_pairs={{0,8},{4,20},{8,0},{12,28},{16,24},{20,4},{24,16},{28,12},{1,9},{5... | collective-permute-start | bytes 2457608 | tf_op jit(solution)/shard_map/ppermute | solution.py:223
  6.2 18.9 %collective-permute-start.1 = (bf16[4,160,640]{2,1,0:T(8,128)(2,1)S(1)}, bf16[4,160,640]{2,1,0:T(8,128)(2,1)S(1)}, u32[]{:S(2)}, u32[]{:S(2)}) collective-permute-start(bf16[4,160,640]{2,1,0:T(8,128)(2,1)S(1)} %get-tuple-element.27.refs_0_), channel_id=1, source_target_pairs={{0,16},{4,12},{8,24},{12,4},{16,0},{20,28},{24,8},{28,20},{1,17},{... | collective-permute-start | bytes 2457608 | tf_op jit(solution)/shard_map/ppermute | solution.py:223
  7.7 26.1 %collective-permute-start.3 = (bf16[4,160,640]{2,1,0:T(8,128)(2,1)S(1)}, bf16[4,160,640]{2,1,0:T(8,128)(2,1)S(1)}, u32[]{:S(2)}, u32[]{:S(2)}) collective-permute-start(bf16[4,160,640]{2,1,0:T(8,128)(2,1)S(1)} %get-tuple-element.30.two_ref.refs_8_), channel_id=1, source_target_pairs={{0,16},{4,12},{8,24},{12,4},{16,0},{20,28},{24,8},{28,20},{1,17},{... | collective-permute-start | bytes 2457608 | tf_op jit(solution)/shard_map/ppermute | solution.py:223
  9.7 15.4 %collective-permute-start.4 = (bf16[128,1280]{1,0:T(8,128)(2,1)S(1)}, bf16[128,1280]{1,0:T(8,128)(2,1)S(1)}, u32[]{:S(2)}, u32[]{:S(2)}) collective-permute-start(bf16[128,1280]{1,0:T(8,128)(2,1)S(1)} %copy-done.2), channel_id=1, source_target_pairs={{0,1},{1,0},{2,3},{3,2},{4,5},{5,4},{6,7},{7,6},{8,9},{9,8},{10,11... | collective-permute-start | bytes 983048 | tf_op jit(solution)/shard_map/ppermute | solution.py:238
  11.2 13.8 %collective-permute-start.5 = (s32[1,128]{1,0:T(1,128)S(1)}, s32[1,128]{1,0:T(1,128)S(1)}, u32[]{:S(2)}, u32[]{:S(2)}) collective-permute-start(s32[1,128]{1,0:T(1,128)S(1)} %copy-done.3), channel_id=1, source_target_pairs={{0,1},{1,0},{2,3},{3,2},{4,5},{5,4},{6,7},{7,6},{8,9},{9,8},{10,11... | collective-permute-start | bytes 1544 | tf_op jit(solution)/shard_map/ppermute | solution.py:238
  33.9 20.6 %collective-permute-start.6 = (bf16[4,160,640]{2,1,0:T(8,128)(2,1)S(1)}, bf16[4,160,640]{2,1,0:T(8,128)(2,1)S(1)}, u32[]{:S(2)}, u32[]{:S(2)}) collective-permute-start(bf16[4,160,640]{2,1,0:T(8,128)(2,1)S(1)} %relay.1), channel_id=1, source_target_pairs={{0,8},{1,2},{2,1},{3,11},{4,20},{5,6},{6,5},{7,23},{8,0},{9,10},{1... | collective-permute-start | bytes 2457608 | tf_op jit(solution)/shard_map/ppermute | solution.py:233
  35.7 21.2 %collective-permute-start.7 = (bf16[4,160,640]{2,1,0:T(8,128)(2,1)S(1)}, bf16[4,160,640]{2,1,0:T(8,128)(2,1)S(1)}, u32[]{:S(2)}, u32[]{:S(2)}) collective-permute-start(bf16[4,160,640]{2,1,0:T(8,128)(2,1)S(1)} %collective-permute-done.one_ref.refs_1_), channel_id=1, source_target_pairs={{0,16},{4,12},{8,24},{12,4},{16,0},{20,28},{24,8},{28,20},{1,17},{... | collective-permute-start | bytes 2457608 | tf_op jit(solution)/shard_map/ppermute | solution.py:223
  37.2 19.7 %collective-permute-start.9 = (bf16[4,160,640]{2,1,0:T(8,128)(2,1)S(1)}, bf16[4,160,640]{2,1,0:T(8,128)(2,1)S(1)}, u32[]{:S(2)}, u32[]{:S(2)}) collective-permute-start(bf16[4,160,640]{2,1,0:T(8,128)(2,1)S(1)} %collective-permute-done.one_ref.refs_1_), channel_id=1, source_target_pairs={{0,4},{4,0},{8,12},{12,8},{16,20},{20,16},{24,28},{28,24},{1,5},{5... | collective-permute-start | bytes 2457608 | tf_op jit(solution)/shard_map/ppermute | solution.py:218
  37.2 19.7 %collective-permute-start.11 = (bf16[4,160,640]{2,1,0:T(8,128)(2,1)S(1)}, bf16[4,160,640]{2,1,0:T(8,128)(2,1)S(1)}, u32[]{:S(2)}, u32[]{:S(2)}) collective-permute-start(bf16[4,160,640]{2,1,0:T(8,128)(2,1)S(1)} %collective-permute-done.3.refs_10_), channel_id=1, source_target_pairs={{0,4},{4,0},{8,12},{12,8},{16,20},{20,16},{24,28},{28,24},{1,5},{5... | collective-permute-start | bytes 2457608 | tf_op jit(solution)/shard_map/ppermute | solution.py:218
  37.7 26.1 %collective-permute-start.8 = (bf16[4,160,640]{2,1,0:T(8,128)(2,1)S(1)}, bf16[4,160,640]{2,1,0:T(8,128)(2,1)S(1)}, u32[]{:S(2)}, u32[]{:S(2)}) collective-permute-start(bf16[4,160,640]{2,1,0:T(8,128)(2,1)S(1)} %collective-permute-done.3.refs_10_), channel_id=1, source_target_pairs={{0,8},{4,20},{8,0},{12,28},{16,24},{20,4},{24,16},{28,12},{1,9},{5... | collective-permute-start | bytes 2457608 | tf_op jit(solution)/shard_map/ppermute | solution.py:223
  54.5 9.3 %collective-permute-start.10 = (bf16[4,160,640]{2,1,0:T(8,128)(2,1)S(1)}, bf16[4,160,640]{2,1,0:T(8,128)(2,1)S(1)}, u32[]{:S(2)}, u32[]{:S(2)}) collective-permute-start(bf16[4,160,640]{2,1,0:T(8,128)(2,1)S(1)} %collective-permute-done.1.refs_2_), channel_id=1, source_target_pairs={{0,4},{4,0},{8,12},{12,8},{16,20},{20,16},{24,28},{28,24},{1,5},{5... | collective-permute-start | bytes 2457608 | tf_op jit(solution)/shard_map/ppermute | solution.py:218
  63.9 2.3 %collective-permute-start.12 = (bf16[4,160,640]{2,1,0:T(8,128)(2,1)S(1)}, bf16[4,160,640]{2,1,0:T(8,128)(2,1)S(1)}, u32[]{:S(2)}, u32[]{:S(2)}) collective-permute-start(bf16[4,160,640]{2,1,0:T(8,128)(2,1)S(1)} %collective-permute-done.7.refs_3_), channel_id=1, source_target_pairs={{0,4},{4,0},{8,12},{12,8},{16,20},{20,16},{24,28},{28,24},{1,5},{5... | collective-permute-start | bytes 2457608 | tf_op jit(solution)/shard_map/ppermute | solution.py:218
  63.9 3.5 %collective-permute-start.13 = (bf16[4,160,640]{2,1,0:T(8,128)(2,1)S(1)}, bf16[4,160,640]{2,1,0:T(8,128)(2,1)S(1)}, u32[]{:S(2)}, u32[]{:S(2)}) collective-permute-start(bf16[4,160,640]{2,1,0:T(8,128)(2,1)S(1)} %collective-permute-done.6.refs_9_), channel_id=1, source_target_pairs={{0,4},{4,0},{8,12},{12,8},{16,20},{20,16},{24,28},{28,24},{1,5},{5... | collective-permute-start | bytes 2457608 | tf_op jit(solution)/shard_map/ppermute | solution.py:218
  64.4 4.2 %collective-permute-start.14 = (bf16[4,160,640]{2,1,0:T(8,128)(2,1)S(1)}, bf16[4,160,640]{2,1,0:T(8,128)(2,1)S(1)}, u32[]{:S(2)}, u32[]{:S(2)}) collective-permute-start(bf16[4,160,640]{2,1,0:T(8,128)(2,1)S(1)} %collective-permute-done.8.refs_11_), channel_id=1, source_target_pairs={{0,4},{4,0},{8,12},{12,8},{16,20},{20,16},{24,28},{28,24},{1,5},{5... | collective-permute-start | bytes 2457608 | tf_op jit(solution)/shard_map/ppermute | solution.py:218
  69.6 10.6 %collective-permute-start.15 = (bf16[128,1280]{1,0:T(8,128)(2,1)S(1)}, bf16[128,1280]{1,0:T(8,128)(2,1)S(1)}, u32[]{:S(2)}, u32[]{:S(2)}) collective-permute-start(bf16[128,1280]{1,0:T(8,128)(2,1)S(1)} %stage_1.2), channel_id=1, source_target_pairs={{0,1},{1,0},{2,3},{3,2},{4,5},{5,4},{6,7},{7,6},{8,9},{9,8},{10,11... | collective-permute-start | bytes 983048 | tf_op jit(solution)/shard_map/ppermute | solution.py:238
  69.9 16.6 %collective-permute-start.17 = (bf16[128,1280]{1,0:T(8,128)(2,1)S(1)}, bf16[128,1280]{1,0:T(8,128)(2,1)S(1)}, u32[]{:S(2)}, u32[]{:S(2)}) collective-permute-start(bf16[128,1280]{1,0:T(8,128)(2,1)S(1)} %stage_1.3), channel_id=1, source_target_pairs={{0,1},{1,0},{2,3},{3,2},{4,5},{5,4},{6,7},{7,6},{8,9},{9,8},{10,11... | collective-permute-start | bytes 983048 | tf_op jit(solution)/shard_map/ppermute | solution.py:238
  85.5 8.2 %collective-permute-start.16 = (bf16[32,5120]{1,0:T(8,128)(2,1)S(1)}, bf16[32,5120]{1,0:T(8,128)(2,1)S(1)}, u32[]{:S(2)}, u32[]{:S(2)}) collective-permute-start(bf16[32,5120]{1,0:T(8,128)(2,1)S(1)} %stage_2.2), channel_id=1, source_target_pairs={{0,1},{1,0},{2,3},{3,2},{4,5},{5,4},{6,7},{7,6},{8,9},{9,8},{10,11... | collective-permute-start | bytes 983048 | tf_op jit(solution)/shard_map/ppermute | solution.py:238

commit v6 on v5

--- a/solution.py
+++ b/solution.py
@@ -114,13 +114,16 @@
     )(*args)
 
 
-def assemble_kernel(*refs):
-    blocks, whole = refs[:-2], refs[-2:]
-    turned = flipped()
-    for swapped in (False, True):
-        pl.when(turned == swapped)(
-            functools.partial(put_in_order, blocks, whole[::-1] if swapped else whole)
-        )
+def assemble_kernel(stage, n_given, *refs):
+    blocks, whole = refs[n_given : n_given + 16], refs[n_given + 16 :]
+    turned, early = flipped(), first_stage()
+    if stage == 2:
+        pl.when(jnp.logical_not(early))(functools.partial(put_in_order, blocks, whole))
+    else:
+        for swapped in (False, True):
+            pl.when(early & (turned == swapped))(
+                functools.partial(put_in_order, blocks, whole[::-1] if swapped else whole)
+            )
 
 
 def put_in_order(blocks, whole):
@@ -139,17 +142,18 @@
                 whole[which][3, where] = block[first + 3, half * 80 : half * 80 + 80]
 
 
-def assemble(p, q):
+def assemble(stage, p, q, given=()):
     vmem = pl.BlockSpec(memory_space=pltpu.VMEM)
     return pl.pallas_call(
-        assemble_kernel,
+        functools.partial(assemble_kernel, stage, len(given)),
         out_shape=[jax.ShapeDtypeStruct((4, D_VIS, WIDTH), jnp.bfloat16)] * 2,
-        in_specs=[vmem] * 16,
+        in_specs=[vmem] * (len(given) + 16),
         out_specs=[vmem] * 2,
+        input_output_aliases={i: i for i in range(len(given))},
         compiler_params=pltpu.CompilerParams(vmem_limit_bytes=8 * 1024 * 1024),
         cost_estimate=SMALL,
         name="assemble",
-    )(*p, *q)
+    )(*given, *p, *q)
 
 
 def choose_kernel(one_ref, two_ref, out_ref):
@@ -223,12 +227,12 @@
     return lax.ppermute(block, "dp", pairs)
 
 
-def planes_or_plane(block):
-    cores_, planes = lax.axis_size("dp"), lax.axis_size("phase")
+def by_stage(block, one, two):
+    planes = lax.axis_size("phase")
     pairs = []
-    for j in range(cores_):
+    for j in range(lax.axis_size("dp")):
         for z in range(planes):
-            to = (j, z ^ 3) if z % 4 in (1, 2) else (j ^ (2 if j % 2 == 0 else 4), z)
+            to = (one if z % 4 in (1, 2) else two)(j, z)
             pairs.append((j * planes + z, to[0] * planes + to[1]))
     return lax.ppermute(block, ("dp", "phase"), pairs)
 
@@ -248,22 +252,29 @@
     own_other = cores(chunks)
     own_other, late_q, theirs, their_ids = tie((own_other, chunk_q, patches, window_ids))
     q2 = plane(late_q, 1)
+
+    def core(j, z):
+        return j ^ 1, z
+
+    q1_two = by_stage(late_q, core, lambda j, z: (j ^ (2 if j % 2 == 0 else 4), z))
     other, other_ids = across(theirs), across(their_ids)
-    p1, p2, q2, other, other_ids = tie((p1, p2, q2, other, other_ids))
-    q1 = planes_or_plane(choose("relay", p1, chunk_q))
+    p1, p2, q2, q1_two, other, other_ids = tie((p1, p2, q2, q1_two, other, other_ids))
+    q1 = by_stage(p1, lambda j, z: (j, z ^ 3), core)
     p3, q3 = plane(p1, 1), plane(q2, 0)
-    p1_other, p2_other, q2_other = cores(p1), cores(p2), cores(q2)
-    q1, p3, q3, p1_other, p2_other, q2_other = tie((q1, p3, q3, p1_other, p2_other, q2_other))
-    weights = assemble(
-        (chunk_p, p1, p2, p3, own_other, p1_other, p2_other, cores(p3)),
-        (chunk_q, q1, q2, q3, own_other, cores(q1), q2_other, cores(q3)),
-    )
+    near = [cores(block) for block in (p1, p2, q2, q1_two)]
+    q1, p3, q3, near[0], near[1], near[2] = tie((q1, p3, q3, near[0], near[1], near[2]))
+    p = (chunk_p, p1, p2, p3, own_other, near[0], near[1], cores(p3))
+    q = (chunk_q, q1, q2, q3, own_other, cores(q1), near[2], cores(q3))
+    weights = assemble(1, p, q)
 
     half_own = run_stage(1, patches, window_ids, gains, merge, weights)
     half_own_far = across(half_own)
     half_own, other = tie((half_own, other))
     half_other = run_stage(1, other, other_ids, gains, merge, weights)
     half_other_far = across(half_other)
+    q = (chunk_q, q1_two, q2, q3, own_other, near[3], near[2], q[7])
+    half_other, *blocks = tie((half_other, *p, *q))
+    weights = assemble(2, blocks[:8], blocks[8:], weights)
     result_other = run_stage(2, half_own_far, other_ids, gains, merge, weights)
     back = across(result_other)
     half_other_far, result_other = tie((half_other_far, result_other))

time: 94.6 us -> 93.9 us (level)
  waiting for transfers between devices: 58.1 us -> 53.6 us
  starting transfers between devices: 20.5 us -> 23.1 us
  local copies, waits for them, and re-layouts: 2.87 us -> 4.29 us
    ppermute x1 -> x2, waiting for transfers between devices: 16.3 us -> 14.2 us  [by_stage(): return lax.ppermute(block, ('dp', 'phase'), pairs)]
    ppermute x7 -> x8, waiting for transfers between devices: 4.13 us -> 2.22 us  [cores(): lax.ppermute(block, 'dp', [(j, j ^ 1) for j in range(lax.axis_size('dp'))])]
    ppermute x5, starting transfers between devices: 8.07 us -> 9.05 us  [plane(): return lax.ppermute(block, 'dp', pairs)]
    ppermute x5, waiting for transfers between devices: 31.5 us -> 30.5 us  [plane(): return lax.ppermute(block, 'dp', pairs)]
    ppermute x5, starting transfers between devices: 9.08 us -> 10 us  [across(): return lax.ppermute(block, 'phase', [(j, j ^ 1) for j in range(size)])]
    ppermute x7 -> x8, starting transfers between devices: 1.54 us -> 2.13 us  [cores(): lax.ppermute(block, 'dp', [(j, j ^ 1) for j in range(lax.axis_size('dp'))])]
    ppermute x1 -> x2, starting transfers between devices: 1.78 us -> 1.9 us  [by_stage(): return lax.ppermute(block, ('dp', 'phase'), pairs)]
    unnamed x12 -> x8, local copies, waits for them, and re-layouts: 2.85 us -> 2.85 us
  transfers between devices with their start and end apart: 18 -> 20, of which waited for: 12 -> 11; matrix products, arithmetic and copies ran while one was open for 0% -> 2% of each run, Pallas kernels for 11% -> 12%
where the time goes in v6:
time: 93.9 us; the launch traced here: 93.6 us
  waiting for transfers between devices  53.6 us (57%)
  starting transfers between devices  23.1 us (25%)
  Pallas kernels  12.5 us (13%)
  local copies, waits for them, and re-layouts  4.29 us (5%)
    ppermute x5, waiting for transfers between devices, plane(): return lax.ppermute(block, 'dp', pairs)  30.5 us
    ppermute x2, waiting for transfers between devices, by_stage(): return lax.ppermute(block, ('dp', 'phase'), pairs)  14.2 us
    pallas_call x4, Pallas kernels, run_stage(): pl.pallas_call(functools.partial(stage_kernel, stage), out_shape=jax.Shap...  10.5 us
    ppermute x5, starting transfers between devices, across(): return lax.ppermute(block, 'phase', [(j, j ^ 1) for j in range(size)])  10 us
    ppermute x5, starting transfers between devices, plane(): return lax.ppermute(block, 'dp', pairs)  9.05 us
    ppermute x5, waiting for transfers between devices, across(): return lax.ppermute(block, 'phase', [(j, j ^ 1) for j in range(size)])  6.72 us
    unnamed x8, local copies, waits for them, and re-layouts  2.85 us
    ppermute x8, waiting for transfers between devices, cores(): lax.ppermute(block, 'dp', [(j, j ^ 1) for j in range(lax.axis_size('dp'))])  2.22 us
  transfers between devices with their start and end apart: 20, of which 11 were waited for; matrix products, arithmetic and copies ran while one was open for 2% of the time, Pallas kernels for 12%

profile of v6, /device:TPU:0, one launch (start us, length us, event | category | flops | bytes accessed | tf_op | source)
XLA Modules:
  0.0 93.6 jit_solution(295373078323974959)
XLA Ops:
  0.0 1.7 %copy-done = bf16[4,160,1920]{2,1,0:T(8,128)(2,1)S(1)} copy-done((bf16[4,160,1920]{2,1,0:T(8,128)(2,1)S(1)}, bf16[4,160,1920]{2,1,0:T(8,128)(2,1)}, u32[]{:S(2)}) %copy-start) | copy-done | bytes 2457624
  1.7 1.1 %copy-done.1 = bf16[4,80,1280]{2,1,0:T(8,128)(2,1)S(1)} copy-done((bf16[4,80,1280]{2,1,0:T(8,128)(2,1)S(1)}, bf16[4,80,1280]{2,1,0:T(8,128)(2,1)}, u32[]{:S(2)}) %copy-start.1) | copy-done | bytes 819224
  3.1 0.5 collective-permute-start.2
  3.6 2.6 %collective-permute-start.1 = (bf16[4,160,640]{2,1,0:T(8,128)(2,1)S(1)}, bf16[4,160,640]{2,1,0:T(8,128)(2,1)S(1)}, u32[]{:S(2)}, u32[]{:S(2)}) collective-permute-start(bf16[4,160,640]{2,1,0:T(8,128)(2,1)S(1)} %get-tuple-element.68.refs_0_.refs_2_), channel_id=1, source_target_pairs={{0,16},{4,12},{8,24},{12,4},{16,0},{20,28},{24,8},{28,20},{1,17},{... | collective-permute-start | bytes 2457608 | tf_op jit(solution)/shard_map/ppermute | solution.py:227
  6.2 1.5 %collective-permute-start = (bf16[4,160,640]{2,1,0:T(8,128)(2,1)S(1)}, bf16[4,160,640]{2,1,0:T(8,128)(2,1)S(1)}, u32[]{:S(2)}, u32[]{:S(2)}) collective-permute-start(bf16[4,160,640]{2,1,0:T(8,128)(2,1)S(1)} %get-tuple-element.68.refs_0_.refs_2_), channel_id=1, source_target_pairs={{0,8},{4,20},{8,0},{12,28},{16,24},{20,4},{24,16},{28,12},{1,9},{5... | collective-permute-start | bytes 2457608 | tf_op jit(solution)/shard_map/ppermute | solution.py:227
  7.7 1.9 %collective-permute-start.4 = (bf16[4,160,640]{2,1,0:T(8,128)(2,1)S(1)}, bf16[4,160,640]{2,1,0:T(8,128)(2,1)S(1)}, u32[]{:S(2)}, u32[]{:S(2)}) collective-permute-start(bf16[4,160,640]{2,1,0:T(8,128)(2,1)S(1)} %get-tuple-element.76.refs_8_.refs_10_), channel_id=1, source_target_pairs={{0,8},{1,5},{2,6},{3,11},{4,20},{5,1},{6,2},{7,23},{8,0},{9,13},{1... | collective-permute-start | bytes 2457608 | tf_op jit(solution)/shard_map/ppermute | solution.py:237
  9.6 1.5 %collective-permute-start.3 = (bf16[4,160,640]{2,1,0:T(8,128)(2,1)S(1)}, bf16[4,160,640]{2,1,0:T(8,128)(2,1)S(1)}, u32[]{:S(2)}, u32[]{:S(2)}) collective-permute-start(bf16[4,160,640]{2,1,0:T(8,128)(2,1)S(1)} %get-tuple-element.76.refs_8_.refs_10_), channel_id=1, source_target_pairs={{0,16},{4,12},{8,24},{12,4},{16,0},{20,28},{24,8},{28,20},{1,17},{... | collective-permute-start | bytes 2457608 | tf_op jit(solution)/shard_map/ppermute | solution.py:227
  11.3 12.9 %collective-permute-done.1.refs_2_.refs_4_ = bf16[4,160,640]{2,1,0:T(8,128)(2,1)S(1)} collective-permute-done((bf16[4,160,640]{2,1,0:T(8,128)(2,1)S(1)}, bf16[4,160,640]{2,1,0:T(8,128)(2,1)S(1)}, u32[]{:S(2)}, u32[]{:S(2)}) %collective-permute-start.1) | collective-permute-done | bytes 819232 | tf_op jit(solution)/shard_map/ppermute | solution.py:227
  24.2 2.5 %collective-permute-start.6 = (s32[1,128]{1,0:T(1,128)}, s32[1,128]{1,0:T(1,128)S(1)}, u32[]{:S(2)}, u32[]{:S(2)}) collective-permute-start(s32[1,128]{1,0:T(1,128)} %refs_1_.3), channel_id=1, source_target_pairs={{0,1},{1,0},{2,3},{3,2},{4,5},{5,4},{6,7},{7,6},{8,9},{9,8},{10,11... | collective-permute-start | bytes 1544 | tf_op jit(solution)/shard_map/ppermute | solution.py:242
  26.8 0.6 collective-permute-done.refs_1_.refs_3_
  27.4 1.0 %collective-permute-done.6.refs_1_ = s32[1,128]{1,0:T(1,128)S(1)} collective-permute-done((s32[1,128]{1,0:T(1,128)}, s32[1,128]{1,0:T(1,128)S(1)}, u32[]{:S(2)}, u32[]{:S(2)}) %collective-permute-start.6) | collective-permute-done | bytes 544 | tf_op jit(solution)/shard_map/ppermute | solution.py:242
  28.4 14.2 %collective-permute-done.4.refs_11_ = bf16[4,160,640]{2,1,0:T(8,128)(2,1)S(1)} collective-permute-done((bf16[4,160,640]{2,1,0:T(8,128)(2,1)S(1)}, bf16[4,160,640]{2,1,0:T(8,128)(2,1)S(1)}, u32[]{:S(2)}, u32[]{:S(2)}) %collective-permute-start.4) | collective-permute-done | bytes 819232 | tf_op jit(solution)/shard_map/ppermute | solution.py:237
  42.7 0.4 collective-permute-start.12
  43.1 1.8 %collective-permute-start.9 = (bf16[4,160,640]{2,1,0:T(8,128)(2,1)S(1)}, bf16[4,160,640]{2,1,0:T(8,128)(2,1)S(1)}, u32[]{:S(2)}, u32[]{:S(2)}) collective-permute-start(bf16[4,160,640]{2,1,0:T(8,128)(2,1)S(1)} %collective-permute-done.3.refs_10_.refs_12_), channel_id=1, source_target_pairs={{0,8},{4,20},{8,0},{12,28},{16,24},{20,4},{24,16},{28,12},{1,9},{5... | collective-permute-start | bytes 2457608 | tf_op jit(solution)/shard_map/ppermute | solution.py:227
  44.9 1.7 %collective-permute-start.8 = (bf16[4,160,640]{2,1,0:T(8,128)(2,1)S(1)}, bf16[4,160,640]{2,1,0:T(8,128)(2,1)S(1)}, u32[]{:S(2)}, u32[]{:S(2)}) collective-permute-start(bf16[4,160,640]{2,1,0:T(8,128)(2,1)S(1)} %collective-permute-done.refs_1_.refs_3_), channel_id=1, source_target_pairs={{0,16},{4,12},{8,24},{12,4},{16,0},{20,28},{24,8},{28,20},{1,17},{... | collective-permute-start | bytes 2457608 | tf_op jit(solution)/shard_map/ppermute | solution.py:227
  46.6 16.4 %collective-permute-done.9.refs_11_.refs_13_ = bf16[4,160,640]{2,1,0:T(8,128)(2,1)S(1)} collective-permute-done((bf16[4,160,640]{2,1,0:T(8,128)(2,1)S(1)}, bf16[4,160,640]{2,1,0:T(8,128)(2,1)S(1)}, u32[]{:S(2)}, u32[]{:S(2)}) %collective-permute-start.9) | collective-permute-done | bytes 819232 | tf_op jit(solution)/shard_map/ppermute | solution.py:227
  63.1 0.6 collective-permute-done.8.refs_3_.refs_5_
  63.6 0.4 collective-permute-start.14
  64.1 0.4 collective-permute-start.15
  64.7 0.7 reshape.7.refs_3_
  65.4 0.7 reshape.6.refs_2_
  66.1 1.0 %collective-permute-done.13.refs_7_.refs_9_ = bf16[4,160,640]{2,1,0:T(8,128)(2,1)S(1)} collective-permute-done((bf16[4,160,640]{2,1,0:T(8,128)(2,1)S(1)}, bf16[4,160,640]{2,1,0:T(8,128)(2,1)S(1)}, u32[]{:S(2)}, u32[]{:S(2)}) %collective-permute-start.13) | collective-permute-done | bytes 819232 | tf_op jit(solution)/shard_map/ppermute | solution.py:222
  67.2 1.2 %collective-permute-done.15.refs_15_.refs_17_ = bf16[4,160,640]{2,1,0:T(8,128)(2,1)S(1)} collective-permute-done((bf16[4,160,640]{2,1,0:T(8,128)(2,1)S(1)}, bf16[4,160,640]{2,1,0:T(8,128)(2,1)S(1)}, u32[]{:S(2)}, u32[]{:S(2)}) %collective-permute-start.15) | collective-permute-done | bytes 819232 | tf_op jit(solution)/shard_map/ppermute | solution.py:222
  68.3 1.6 %collective-permute-start.16 = (bf16[128,1280]{1,0:T(8,128)(2,1)S(1)}, bf16[128,1280]{1,0:T(8,128)(2,1)S(1)}, u32[]{:S(2)}, u32[]{:S(2)}) collective-permute-start(bf16[128,1280]{1,0:T(8,128)(2,1)S(1)} %stage_1.2), channel_id=1, source_target_pairs={{0,1},{1,0},{2,3},{3,2},{4,5},{5,4},{6,7},{7,6},{8,9},{9,8},{10,11... | collective-permute-start | bytes 983048 | tf_op jit(solution)/shard_map/ppermute | solution.py:242
  69.9 5.6 %collective-permute-start.19 = (bf16[128,1280]{1,0:T(8,128)(2,1)S(1)}, bf16[128,1280]{1,0:T(8,128)(2,1)S(1)}, u32[]{:S(2)}, u32[]{:S(2)}) collective-permute-start(bf16[128,1280]{1,0:T(8,128)(2,1)S(1)} %stage_1.3), channel_id=1, source_target_pairs={{0,1},{1,0},{2,3},{3,2},{4,5},{5,4},{6,7},{7,6},{8,9},{9,8},{10,11... | collective-permute-start | bytes 983048 | tf_op jit(solution)/shard_map/ppermute | solution.py:242
  75.6 1.0 %assemble.3 = (bf16[4,1280,640]{2,1,0:T(8,128)(2,1)S(1)}, bf16[4,1280,640]{2,1,0:T(8,128)(2,1)S(1)}) custom-call(bf16[4,1280,640]{2,1,0:T(8,128)(2,1)S(1)} %get-tuple-element.62.refs_4_.refs_0_, bf16[4,1280,640]{2,1,0:T(8,128)(2,1)S(1)} %get-tuple-element.63.refs_5_.refs_1_, ...), custom_call_target="tpu_custom_call", output_to_operand_aliasing={{0}: (0, {}), {1}: (1, {})} | custom-call | flops 1 | bytes 1 | tf_op jit(solution)/shard_map/assemble/pallas_call | solution.py:147
  76.6 2.4 %collective-permute-done.16.refs_0_ = bf16[128,1280]{1,0:T(8,128)(2,1)S(1)} collective-permute-done((bf16[128,1280]{1,0:T(8,128)(2,1)S(1)}, bf16[128,1280]{1,0:T(8,128)(2,1)S(1)}, u32[]{:S(2)}, u32[]{:S(2)}) %collective-permute-start.16) | collective-permute-done | bytes 327712 | tf_op jit(solution)/shard_map/ppermute | solution.py:242
  78.9 5.3 %stage_2.2 = bf16[32,5120]{1,0:T(8,128)(2,1)S(1)} custom-call(bf16[128,1280]{1,0:T(8,128)(2,1)S(1)} %collective-permute-done.16.refs_0_, s32[1,128]{1,0:T(1,128)S(1)} %collective-permute-done.6.refs_1_, f32[4,1,1280]{2,1,0:T(1,128)S(1)} %reshape.6.refs_2_, f32[1,1280]{1,0:T(1,128)S(1)} %reshape.7.refs_3_, ...), custom_call_target="tpu_custom_call" | custom-call | flops 1 | bytes 1 | tf_op jit(solution)/shard_map/stage_2/pallas_call | solution.py:100
  84.3 1.1 %collective-permute-done.19.refs_0_ = bf16[128,1280]{1,0:T(8,128)(2,1)S(1)} collective-permute-done((bf16[128,1280]{1,0:T(8,128)(2,1)S(1)}, bf16[128,1280]{1,0:T(8,128)(2,1)S(1)}, u32[]{:S(2)}, u32[]{:S(2)}) %collective-permute-start.19) | collective-permute-done | bytes 327712 | tf_op jit(solution)/shard_map/ppermute | solution.py:242
  85.4 5.3 %stage_2.3.two_ref = bf16[32,5120]{1,0:T(8,128)(2,1)S(1)} custom-call(bf16[128,1280]{1,0:T(8,128)(2,1)S(1)} %collective-permute-done.19.refs_0_, s32[1,128]{1,0:T(1,128)S(1)} %copy-done.3, f32[4,1,1280]{2,1,0:T(1,128)S(1)} %reshape.6.refs_2_, f32[1,1280]{1,0:T(1,128)S(1)} %reshape.7.refs_3_, bf16[4,1280,640]{2,1,0:T(8,128)(2,1)S(1)} %get-tuple-element.84.refs_4_, ...), custom_call_target="tpu_custom_call" | custom-call | flops 1 | bytes 1 | tf_op jit(solution)/shard_map/stage_2/pallas_call | solution.py:100
  90.7 2.2 %collective-permute-done.18.one_ref = bf16[32,5120]{1,0:T(8,128)(2,1)S(1)} collective-permute-done((bf16[32,5120]{1,0:T(8,128)(2,1)S(1)}, bf16[32,5120]{1,0:T(8,128)(2,1)S(1)}, u32[]{:S(2)}, u32[]{:S(2)}) %collective-permute-start.18) | collective-permute-done | bytes 327712 | tf_op jit(solution)/shard_map/ppermute | solution.py:242
  92.9 0.7 result.1
  (26 shorter events, 1.0 us)
Async XLA Ops:
  0.0 1.7 %copy-start = (bf16[4,160,1920]{2,1,0:T(8,128)(2,1)S(1)}, bf16[4,160,1920]{2,1,0:T(8,128)(2,1)}, u32[]{:S(2)}) copy-start(bf16[4,160,1920]{2,1,0:T(8,128)(2,1)} %qkv.1) | copy-start | bytes 7372804
  1.7 1.1 %copy-start.1 = (bf16[4,80,1280]{2,1,0:T(8,128)(2,1)S(1)}, bf16[4,80,1280]{2,1,0:T(8,128)(2,1)}, u32[]{:S(2)}) copy-start(bf16[4,80,1280]{2,1,0:T(8,128)(2,1)} %out.1) | copy-start | bytes 2457604
  3.1 4.6 %collective-permute-start.2 = (bf16[8,160,640]{2,1,0:T(8,128)(2,1)S(1)}, bf16[8,160,640]{2,1,0:T(8,128)(2,1)S(1)}, u32[]{:S(2)}, u32[]{:S(2)}) collective-permute-start(bf16[8,160,640]{2,1,0:T(8,128)(2,1)S(1)} %get-tuple-element.47), channel_id=1, source_target_pairs={{0,4},{4,0},{8,12},{12,8},{16,20},{20,16},{24,28},{28,24},{1,5},{5... | collective-permute-start | bytes 4915208 | tf_op jit(solution)/shard_map/ppermute | solution.py:222
  3.6 20.6 %collective-permute-start.1 = (bf16[4,160,640]{2,1,0:T(8,128)(2,1)S(1)}, bf16[4,160,640]{2,1,0:T(8,128)(2,1)S(1)}, u32[]{:S(2)}, u32[]{:S(2)}) collective-permute-start(bf16[4,160,640]{2,1,0:T(8,128)(2,1)S(1)} %get-tuple-element.68.refs_0_.refs_2_), channel_id=1, source_target_pairs={{0,16},{4,12},{8,24},{12,4},{16,0},{20,28},{24,8},{28,20},{1,17},{... | collective-permute-start | bytes 2457608 | tf_op jit(solution)/shard_map/ppermute | solution.py:227
  6.2 21.2 %collective-permute-start = (bf16[4,160,640]{2,1,0:T(8,128)(2,1)S(1)}, bf16[4,160,640]{2,1,0:T(8,128)(2,1)S(1)}, u32[]{:S(2)}, u32[]{:S(2)}) collective-permute-start(bf16[4,160,640]{2,1,0:T(8,128)(2,1)S(1)} %get-tuple-element.68.refs_0_.refs_2_), channel_id=1, source_target_pairs={{0,8},{4,20},{8,0},{12,28},{16,24},{20,4},{24,16},{28,12},{1,9},{5... | collective-permute-start | bytes 2457608 | tf_op jit(solution)/shard_map/ppermute | solution.py:227
  7.7 34.9 %collective-permute-start.4 = (bf16[4,160,640]{2,1,0:T(8,128)(2,1)S(1)}, bf16[4,160,640]{2,1,0:T(8,128)(2,1)S(1)}, u32[]{:S(2)}, u32[]{:S(2)}) collective-permute-start(bf16[4,160,640]{2,1,0:T(8,128)(2,1)S(1)} %get-tuple-element.76.refs_8_.refs_10_), channel_id=1, source_target_pairs={{0,8},{1,5},{2,6},{3,11},{4,20},{5,1},{6,2},{7,23},{8,0},{9,13},{1... | collective-permute-start | bytes 2457608 | tf_op jit(solution)/shard_map/ppermute | solution.py:237
  9.6 33.0 %collective-permute-start.3 = (bf16[4,160,640]{2,1,0:T(8,128)(2,1)S(1)}, bf16[4,160,640]{2,1,0:T(8,128)(2,1)S(1)}, u32[]{:S(2)}, u32[]{:S(2)}) collective-permute-start(bf16[4,160,640]{2,1,0:T(8,128)(2,1)S(1)} %get-tuple-element.76.refs_8_.refs_10_), channel_id=1, source_target_pairs={{0,16},{4,12},{8,24},{12,4},{16,0},{20,28},{24,8},{28,20},{1,17},{... | collective-permute-start | bytes 2457608 | tf_op jit(solution)/shard_map/ppermute | solution.py:227
  11.1 17.3 %collective-permute-start.5 = (bf16[128,1280]{1,0:T(8,128)(2,1)}, bf16[128,1280]{1,0:T(8,128)(2,1)S(1)}, u32[]{:S(2)}, u32[]{:S(2)}) collective-permute-start(bf16[128,1280]{1,0:T(8,128)(2,1)} %refs_0_.1), channel_id=1, source_target_pairs={{0,1},{1,0},{2,3},{3,2},{4,5},{5,4},{6,7},{7,6},{8,9},{9,8},{10,11... | collective-permute-start | bytes 983048 | tf_op jit(solution)/shard_map/ppermute | solution.py:242
  24.2 4.2 %collective-permute-start.6 = (s32[1,128]{1,0:T(1,128)}, s32[1,128]{1,0:T(1,128)S(1)}, u32[]{:S(2)}, u32[]{:S(2)}) collective-permute-start(s32[1,128]{1,0:T(1,128)} %refs_1_.3), channel_id=1, source_target_pairs={{0,1},{1,0},{2,3},{3,2},{4,5},{5,4},{6,7},{7,6},{8,9},{9,8},{10,11... | collective-permute-start | bytes 1544 | tf_op jit(solution)/shard_map/ppermute | solution.py:242
  42.6 4.0 %collective-permute-start.11 = (bf16[4,160,640]{2,1,0:T(8,128)(2,1)S(1)}, bf16[4,160,640]{2,1,0:T(8,128)(2,1)S(1)}, u32[]{:S(2)}, u32[]{:S(2)}) collective-permute-start(bf16[4,160,640]{2,1,0:T(8,128)(2,1)S(1)} %collective-permute-done.1.refs_2_.refs_4_), channel_id=1, source_target_pairs={{0,4},{4,0},{8,12},{12,8},{16,20},{20,16},{24,28},{28,24},{1,5},{5... | collective-permute-start | bytes 2457608 | tf_op jit(solution)/shard_map/ppermute | solution.py:222
  42.7 3.9 %collective-permute-start.12 = (bf16[4,160,640]{2,1,0:T(8,128)(2,1)S(1)}, bf16[4,160,640]{2,1,0:T(8,128)(2,1)S(1)}, u32[]{:S(2)}, u32[]{:S(2)}) collective-permute-start(bf16[4,160,640]{2,1,0:T(8,128)(2,1)S(1)} %collective-permute-done.3.refs_10_.refs_12_), channel_id=1, source_target_pairs={{0,4},{4,0},{8,12},{12,8},{16,20},{20,16},{24,28},{28,24},{1,5},{5... | collective-permute-start | bytes 2457608 | tf_op jit(solution)/shard_map/ppermute | solution.py:222
  43.1 20.0 %collective-permute-start.9 = (bf16[4,160,640]{2,1,0:T(8,128)(2,1)S(1)}, bf16[4,160,640]{2,1,0:T(8,128)(2,1)S(1)}, u32[]{:S(2)}, u32[]{:S(2)}) collective-permute-start(bf16[4,160,640]{2,1,0:T(8,128)(2,1)S(1)} %collective-permute-done.3.refs_10_.refs_12_), channel_id=1, source_target_pairs={{0,8},{4,20},{8,0},{12,28},{16,24},{20,4},{24,16},{28,12},{1,9},{5... | collective-permute-start | bytes 2457608 | tf_op jit(solution)/shard_map/ppermute | solution.py:227
  44.9 18.2 %collective-permute-start.10 = (bf16[4,160,640]{2,1,0:T(8,128)(2,1)S(1)}, bf16[4,160,640]{2,1,0:T(8,128)(2,1)S(1)}, u32[]{:S(2)}, u32[]{:S(2)}) collective-permute-start(bf16[4,160,640]{2,1,0:T(8,128)(2,1)S(1)} %collective-permute-done.refs_1_.refs_3_), channel_id=1, source_target_pairs={{0,4},{4,0},{8,12},{12,8},{16,20},{20,16},{24,28},{28,24},{1,5},{5... | collective-permute-start | bytes 2457608 | tf_op jit(solution)/shard_map/ppermute | solution.py:222
  44.9 18.7 %collective-permute-start.8 = (bf16[4,160,640]{2,1,0:T(8,128)(2,1)S(1)}, bf16[4,160,640]{2,1,0:T(8,128)(2,1)S(1)}, u32[]{:S(2)}, u32[]{:S(2)}) collective-permute-start(bf16[4,160,640]{2,1,0:T(8,128)(2,1)S(1)} %collective-permute-done.refs_1_.refs_3_), channel_id=1, source_target_pairs={{0,16},{4,12},{8,24},{12,4},{16,0},{20,28},{24,8},{28,20},{1,17},{... | collective-permute-start | bytes 2457608 | tf_op jit(solution)/shard_map/ppermute | solution.py:227
  46.6 17.0 %collective-permute-start.7 = (bf16[4,160,640]{2,1,0:T(8,128)(2,1)S(1)}, bf16[4,160,640]{2,1,0:T(8,128)(2,1)S(1)}, u32[]{:S(2)}, u32[]{:S(2)}) collective-permute-start(bf16[4,160,640]{2,1,0:T(8,128)(2,1)S(1)} %collective-permute-done.refs_1_.refs_3_), channel_id=1, source_target_pairs={{0,4},{1,2},{2,1},{3,7},{4,0},{5,6},{6,5},{7,3},{8,12},{9,10},{10,... | collective-permute-start | bytes 2457608 | tf_op jit(solution)/shard_map/ppermute | solution.py:237
  63.6 2.5 %collective-permute-start.14 = (bf16[4,160,640]{2,1,0:T(8,128)(2,1)S(1)}, bf16[4,160,640]{2,1,0:T(8,128)(2,1)S(1)}, u32[]{:S(2)}, u32[]{:S(2)}) collective-permute-start(bf16[4,160,640]{2,1,0:T(8,128)(2,1)S(1)} %collective-permute-done.7.refs_9_), channel_id=1, source_target_pairs={{0,4},{4,0},{8,12},{12,8},{16,20},{20,16},{24,28},{28,24},{1,5},{5... | collective-permute-start | bytes 2457608 | tf_op jit(solution)/shard_map/ppermute | solution.py:222
  64.0 3.1 %collective-permute-start.13 = (bf16[4,160,640]{2,1,0:T(8,128)(2,1)S(1)}, bf16[4,160,640]{2,1,0:T(8,128)(2,1)S(1)}, u32[]{:S(2)}, u32[]{:S(2)}) collective-permute-start(bf16[4,160,640]{2,1,0:T(8,128)(2,1)S(1)} %collective-permute-done.8.refs_3_.refs_5_), channel_id=1, source_target_pairs={{0,4},{4,0},{8,12},{12,8},{16,20},{20,16},{24,28},{28,24},{1,5},{5... | collective-permute-start | bytes 2457608 | tf_op jit(solution)/shard_map/ppermute | solution.py:222
  64.1 4.2 %collective-permute-start.15 = (bf16[4,160,640]{2,1,0:T(8,128)(2,1)S(1)}, bf16[4,160,640]{2,1,0:T(8,128)(2,1)S(1)}, u32[]{:S(2)}, u32[]{:S(2)}) collective-permute-start(bf16[4,160,640]{2,1,0:T(8,128)(2,1)S(1)} %collective-permute-done.9.refs_11_.refs_13_), channel_id=1, source_target_pairs={{0,4},{4,0},{8,12},{12,8},{16,20},{20,16},{24,28},{28,24},{1,5},{5... | collective-permute-start | bytes 2457608 | tf_op jit(solution)/shard_map/ppermute | solution.py:222
  64.5 11.0 %collective-permute-start.17 = (bf16[4,160,640]{2,1,0:T(8,128)(2,1)S(1)}, bf16[4,160,640]{2,1,0:T(8,128)(2,1)S(1)}, u32[]{:S(2)}, u32[]{:S(2)}) collective-permute-start(bf16[4,160,640]{2,1,0:T(8,128)(2,1)S(1)} %collective-permute-done.4.refs_11_), channel_id=1, source_target_pairs={{0,4},{4,0},{8,12},{12,8},{16,20},{20,16},{24,28},{28,24},{1,5},{5... | collective-permute-start | bytes 2457608 | tf_op jit(solution)/shard_map/ppermute | solution.py:222
  66.1 2.2 %copy-start.2 = (bf16[128,1280]{1,0:T(8,128)(2,1)S(1)}, bf16[128,1280]{1,0:T(8,128)(2,1)}, u32[]{:S(2)}) copy-start(bf16[128,1280]{1,0:T(8,128)(2,1)} %refs_0_.1) | copy-start | bytes 983044
  66.1 2.2 %copy-start.3 = (s32[1,128]{1,0:T(1,128)S(1)}, s32[1,128]{1,0:T(1,128)}, u32[]{:S(2)}) copy-start(s32[1,128]{1,0:T(1,128)} %refs_1_.3) | copy-start | bytes 1540
  68.3 10.6 %collective-permute-start.16 = (bf16[128,1280]{1,0:T(8,128)(2,1)S(1)}, bf16[128,1280]{1,0:T(8,128)(2,1)S(1)}, u32[]{:S(2)}, u32[]{:S(2)}) collective-permute-start(bf16[128,1280]{1,0:T(8,128)(2,1)S(1)} %stage_1.2), channel_id=1, source_target_pairs={{0,1},{1,0},{2,3},{3,2},{4,5},{5,4},{6,7},{7,6},{8,9},{9,8},{10,11... | collective-permute-start | bytes 983048 | tf_op jit(solution)/shard_map/ppermute | solution.py:242
  69.9 15.5 %collective-permute-start.19 = (bf16[128,1280]{1,0:T(8,128)(2,1)S(1)}, bf16[128,1280]{1,0:T(8,128)(2,1)S(1)}, u32[]{:S(2)}, u32[]{:S(2)}) collective-permute-start(bf16[128,1280]{1,0:T(8,128)(2,1)S(1)} %stage_1.3), channel_id=1, source_target_pairs={{0,1},{1,0},{2,3},{3,2},{4,5},{5,4},{6,7},{7,6},{8,9},{9,8},{10,11... | collective-permute-start | bytes 983048 | tf_op jit(solution)/shard_map/ppermute | solution.py:242
  84.2 8.7 %collective-permute-start.18 = (bf16[32,5120]{1,0:T(8,128)(2,1)S(1)}, bf16[32,5120]{1,0:T(8,128)(2,1)S(1)}, u32[]{:S(2)}, u32[]{:S(2)}) collective-permute-start(bf16[32,5120]{1,0:T(8,128)(2,1)S(1)} %stage_2.2), channel_id=1, source_target_pairs={{0,1},{1,0},{2,3},{3,2},{4,5},{5,4},{6,7},{7,6},{8,9},{9,8},{10,11... | collective-permute-start | bytes 983048 | tf_op jit(solution)/shard_map/ppermute | solution.py:242

commit v7 on v6

--- a/solution.py
+++ b/solution.py
@@ -262,7 +262,8 @@
     q1 = by_stage(p1, lambda j, z: (j, z ^ 3), core)
     p3, q3 = plane(p1, 1), plane(q2, 0)
     near = [cores(block) for block in (p1, p2, q2, q1_two)]
-    q1, p3, q3, near[0], near[1], near[2] = tie((q1, p3, q3, near[0], near[1], near[2]))
+    p3, q3, near[0], near[1] = tie((p3, q3, near[0], near[1]))
+    q1, near[2] = tie((q1, near[2]))
     p = (chunk_p, p1, p2, p3, own_other, near[0], near[1], cores(p3))
     q = (chunk_q, q1, q2, q3, own_other, cores(q1), near[2], cores(q3))
     weights = assemble(1, p, q)

time: 93.9 us -> 92.8 us (0.988)
  waiting for transfers between devices: 53.6 us -> 52 us
    ppermute x8, waiting for transfers between devices: 2.22 us -> 1.27 us  [cores(): lax.ppermute(block, 'dp', [(j, j ^ 1) for j in range(lax.axis_size('dp'))])]
where the time goes in v7:
time: 92.8 us; the launch traced here: 92.5 us
  waiting for transfers between devices  52 us (56%)
  starting transfers between devices  23.5 us (25%)
  Pallas kernels  12.5 us (13%)
  local copies, waits for them, and re-layouts  4.29 us (5%)
    ppermute x5, waiting for transfers between devices, plane(): return lax.ppermute(block, 'dp', pairs)  29.9 us
    ppermute x2, waiting for transfers between devices, by_stage(): return lax.ppermute(block, ('dp', 'phase'), pairs)  14.2 us
    pallas_call x4, Pallas kernels, run_stage(): pl.pallas_call(functools.partial(stage_kernel, stage), out_shape=jax.Shap...  10.5 us
    ppermute x5, starting transfers between devices, across(): return lax.ppermute(block, 'phase', [(j, j ^ 1) for j in range(size)])  10 us
    ppermute x5, starting transfers between devices, plane(): return lax.ppermute(block, 'dp', pairs)  9.13 us
    ppermute x5, waiting for transfers between devices, across(): return lax.ppermute(block, 'phase', [(j, j ^ 1) for j in range(size)])  6.71 us
    unnamed x8, local copies, waits for them, and re-layouts  2.85 us
    ppermute x2, starting transfers between devices, by_stage(): return lax.ppermute(block, ('dp', 'phase'), pairs)  2.3 us
  transfers between devices with their start and end apart: 20, of which 11 were waited for; matrix products, arithmetic and copies ran while one was open for 2% of the time, Pallas kernels for 12%

profile of v7, /device:TPU:0, one launch (start us, length us, event | category | flops | bytes accessed | tf_op | source)
XLA Modules:
  0.0 92.5 jit_solution(14068041940107379970)
XLA Ops:
  0.0 1.7 %copy-done = bf16[4,160,1920]{2,1,0:T(8,128)(2,1)S(1)} copy-done((bf16[4,160,1920]{2,1,0:T(8,128)(2,1)S(1)}, bf16[4,160,1920]{2,1,0:T(8,128)(2,1)}, u32[]{:S(2)}) %copy-start) | copy-done | bytes 2457624
  1.7 1.1 %copy-done.1 = bf16[4,80,1280]{2,1,0:T(8,128)(2,1)S(1)} copy-done((bf16[4,80,1280]{2,1,0:T(8,128)(2,1)S(1)}, bf16[4,80,1280]{2,1,0:T(8,128)(2,1)}, u32[]{:S(2)}) %copy-start.1) | copy-done | bytes 819224
  3.1 0.5 collective-permute-start.2
  3.6 2.6 %collective-permute-start.1 = (bf16[4,160,640]{2,1,0:T(8,128)(2,1)S(1)}, bf16[4,160,640]{2,1,0:T(8,128)(2,1)S(1)}, u32[]{:S(2)}, u32[]{:S(2)}) collective-permute-start(bf16[4,160,640]{2,1,0:T(8,128)(2,1)S(1)} %get-tuple-element.68.refs_0_.refs_2_), channel_id=1, source_target_pairs={{0,16},{4,12},{8,24},{12,4},{16,0},{20,28},{24,8},{28,20},{1,17},{... | collective-permute-start | bytes 2457608 | tf_op jit(solution)/shard_map/ppermute | solution.py:227
  6.2 1.5 %collective-permute-start = (bf16[4,160,640]{2,1,0:T(8,128)(2,1)S(1)}, bf16[4,160,640]{2,1,0:T(8,128)(2,1)S(1)}, u32[]{:S(2)}, u32[]{:S(2)}) collective-permute-start(bf16[4,160,640]{2,1,0:T(8,128)(2,1)S(1)} %get-tuple-element.68.refs_0_.refs_2_), channel_id=1, source_target_pairs={{0,8},{4,20},{8,0},{12,28},{16,24},{20,4},{24,16},{28,12},{1,9},{5... | collective-permute-start | bytes 2457608 | tf_op jit(solution)/shard_map/ppermute | solution.py:227
  7.7 1.9 %collective-permute-start.4 = (bf16[4,160,640]{2,1,0:T(8,128)(2,1)S(1)}, bf16[4,160,640]{2,1,0:T(8,128)(2,1)S(1)}, u32[]{:S(2)}, u32[]{:S(2)}) collective-permute-start(bf16[4,160,640]{2,1,0:T(8,128)(2,1)S(1)} %get-tuple-element.76.refs_8_.refs_10_), channel_id=1, source_target_pairs={{0,8},{1,5},{2,6},{3,11},{4,20},{5,1},{6,2},{7,23},{8,0},{9,13},{1... | collective-permute-start | bytes 2457608 | tf_op jit(solution)/shard_map/ppermute | solution.py:237
  9.6 1.5 %collective-permute-start.3 = (bf16[4,160,640]{2,1,0:T(8,128)(2,1)S(1)}, bf16[4,160,640]{2,1,0:T(8,128)(2,1)S(1)}, u32[]{:S(2)}, u32[]{:S(2)}) collective-permute-start(bf16[4,160,640]{2,1,0:T(8,128)(2,1)S(1)} %get-tuple-element.76.refs_8_.refs_10_), channel_id=1, source_target_pairs={{0,16},{4,12},{8,24},{12,4},{16,0},{20,28},{24,8},{28,20},{1,17},{... | collective-permute-start | bytes 2457608 | tf_op jit(solution)/shard_map/ppermute | solution.py:227
  11.3 12.9 %collective-permute-done.1.refs_2_.refs_4_ = bf16[4,160,640]{2,1,0:T(8,128)(2,1)S(1)} collective-permute-done((bf16[4,160,640]{2,1,0:T(8,128)(2,1)S(1)}, bf16[4,160,640]{2,1,0:T(8,128)(2,1)S(1)}, u32[]{:S(2)}, u32[]{:S(2)}) %collective-permute-start.1) | collective-permute-done | bytes 819232 | tf_op jit(solution)/shard_map/ppermute | solution.py:227
  24.2 2.5 %collective-permute-start.6 = (s32[1,128]{1,0:T(1,128)}, s32[1,128]{1,0:T(1,128)S(1)}, u32[]{:S(2)}, u32[]{:S(2)}) collective-permute-start(s32[1,128]{1,0:T(1,128)} %refs_1_.3), channel_id=1, source_target_pairs={{0,1},{1,0},{2,3},{3,2},{4,5},{5,4},{6,7},{7,6},{8,9},{9,8},{10,11... | collective-permute-start | bytes 1544 | tf_op jit(solution)/shard_map/ppermute | solution.py:242
  26.8 0.6 collective-permute-done.refs_1_.refs_3_
  27.4 1.0 %collective-permute-done.6.refs_1_ = s32[1,128]{1,0:T(1,128)S(1)} collective-permute-done((s32[1,128]{1,0:T(1,128)}, s32[1,128]{1,0:T(1,128)S(1)}, u32[]{:S(2)}, u32[]{:S(2)}) %collective-permute-start.6) | collective-permute-done | bytes 544 | tf_op jit(solution)/shard_map/ppermute | solution.py:242
  28.4 14.2 %collective-permute-done.4.refs_11_ = bf16[4,160,640]{2,1,0:T(8,128)(2,1)S(1)} collective-permute-done((bf16[4,160,640]{2,1,0:T(8,128)(2,1)S(1)}, bf16[4,160,640]{2,1,0:T(8,128)(2,1)S(1)}, u32[]{:S(2)}, u32[]{:S(2)}) %collective-permute-start.4) | collective-permute-done | bytes 819232 | tf_op jit(solution)/shard_map/ppermute | solution.py:237
  42.7 0.4 collective-permute-start.12
  43.1 1.8 %collective-permute-start.8 = (bf16[4,160,640]{2,1,0:T(8,128)(2,1)S(1)}, bf16[4,160,640]{2,1,0:T(8,128)(2,1)S(1)}, u32[]{:S(2)}, u32[]{:S(2)}) collective-permute-start(bf16[4,160,640]{2,1,0:T(8,128)(2,1)S(1)} %collective-permute-done.3.refs_10_.refs_12_), channel_id=1, source_target_pairs={{0,8},{4,20},{8,0},{12,28},{16,24},{20,4},{24,16},{28,12},{1,9},{5... | collective-permute-start | bytes 2457608 | tf_op jit(solution)/shard_map/ppermute | solution.py:227
  44.9 0.4 collective-permute-start.9
  45.4 1.7 %collective-permute-start.7 = (bf16[4,160,640]{2,1,0:T(8,128)(2,1)S(1)}, bf16[4,160,640]{2,1,0:T(8,128)(2,1)S(1)}, u32[]{:S(2)}, u32[]{:S(2)}) collective-permute-start(bf16[4,160,640]{2,1,0:T(8,128)(2,1)S(1)} %collective-permute-done.refs_1_.refs_3_), channel_id=1, source_target_pairs={{0,16},{4,12},{8,24},{12,4},{16,0},{20,28},{24,8},{28,20},{1,17},{... | collective-permute-start | bytes 2457608 | tf_op jit(solution)/shard_map/ppermute | solution.py:227
  47.3 15.5 %collective-permute-done.8.refs_11_.refs_13_ = bf16[4,160,640]{2,1,0:T(8,128)(2,1)S(1)} collective-permute-done((bf16[4,160,640]{2,1,0:T(8,128)(2,1)S(1)}, bf16[4,160,640]{2,1,0:T(8,128)(2,1)S(1)}, u32[]{:S(2)}, u32[]{:S(2)}) %collective-permute-start.8) | collective-permute-done | bytes 819232 | tf_op jit(solution)/shard_map/ppermute | solution.py:227
  62.8 0.9 collective-permute-done.7.refs_3_.refs_5_
  63.6 0.4 collective-permute-start.11
  64.1 0.4 collective-permute-start.17
  64.5 0.7 reshape.7.refs_3_
  65.2 0.7 reshape.6.refs_2_
  66.0 1.1 %collective-permute-done.15.refs_15_.refs_17_ = bf16[4,160,640]{2,1,0:T(8,128)(2,1)S(1)} collective-permute-done((bf16[4,160,640]{2,1,0:T(8,128)(2,1)S(1)}, bf16[4,160,640]{2,1,0:T(8,128)(2,1)S(1)}, u32[]{:S(2)}, u32[]{:S(2)}) %collective-permute-start.15) | collective-permute-done | bytes 819232 | tf_op jit(solution)/shard_map/ppermute | solution.py:222
  67.2 0.8 collective-permute-start.16
  68.0 6.4 %collective-permute-start.19 = (bf16[128,1280]{1,0:T(8,128)(2,1)S(1)}, bf16[128,1280]{1,0:T(8,128)(2,1)S(1)}, u32[]{:S(2)}, u32[]{:S(2)}) collective-permute-start(bf16[128,1280]{1,0:T(8,128)(2,1)S(1)} %stage_1.3), channel_id=1, source_target_pairs={{0,1},{1,0},{2,3},{3,2},{4,5},{5,4},{6,7},{7,6},{8,9},{9,8},{10,11... | collective-permute-start | bytes 983048 | tf_op jit(solution)/shard_map/ppermute | solution.py:242
  74.4 1.0 %assemble.3 = (bf16[4,1280,640]{2,1,0:T(8,128)(2,1)S(1)}, bf16[4,1280,640]{2,1,0:T(8,128)(2,1)S(1)}) custom-call(bf16[4,1280,640]{2,1,0:T(8,128)(2,1)S(1)} %get-tuple-element.62.refs_4_.refs_0_, bf16[4,1280,640]{2,1,0:T(8,128)(2,1)S(1)} %get-tuple-element.63.refs_5_.refs_1_, ...), custom_call_target="tpu_custom_call", output_to_operand_aliasing={{0}: (0, {}), {1}: (1, {})} | custom-call | flops 1 | bytes 1 | tf_op jit(solution)/shard_map/assemble/pallas_call | solution.py:147
  75.4 2.3 %collective-permute-done.16.refs_0_ = bf16[128,1280]{1,0:T(8,128)(2,1)S(1)} collective-permute-done((bf16[128,1280]{1,0:T(8,128)(2,1)S(1)}, bf16[128,1280]{1,0:T(8,128)(2,1)S(1)}, u32[]{:S(2)}, u32[]{:S(2)}) %collective-permute-start.16) | collective-permute-done | bytes 327712 | tf_op jit(solution)/shard_map/ppermute | solution.py:242
  77.8 5.3 %stage_2.2 = bf16[32,5120]{1,0:T(8,128)(2,1)S(1)} custom-call(bf16[128,1280]{1,0:T(8,128)(2,1)S(1)} %collective-permute-done.16.refs_0_, s32[1,128]{1,0:T(1,128)S(1)} %collective-permute-done.6.refs_1_, f32[4,1,1280]{2,1,0:T(1,128)S(1)} %reshape.6.refs_2_, f32[1,1280]{1,0:T(1,128)S(1)} %reshape.7.refs_3_, ...), custom_call_target="tpu_custom_call" | custom-call | flops 1 | bytes 1 | tf_op jit(solution)/shard_map/stage_2/pallas_call | solution.py:100
  83.1 1.1 %collective-permute-done.19.refs_0_ = bf16[128,1280]{1,0:T(8,128)(2,1)S(1)} collective-permute-done((bf16[128,1280]{1,0:T(8,128)(2,1)S(1)}, bf16[128,1280]{1,0:T(8,128)(2,1)S(1)}, u32[]{:S(2)}, u32[]{:S(2)}) %collective-permute-start.19) | collective-permute-done | bytes 327712 | tf_op jit(solution)/shard_map/ppermute | solution.py:242
  84.2 5.3 %stage_2.3.two_ref = bf16[32,5120]{1,0:T(8,128)(2,1)S(1)} custom-call(bf16[128,1280]{1,0:T(8,128)(2,1)S(1)} %collective-permute-done.19.refs_0_, s32[1,128]{1,0:T(1,128)S(1)} %copy-done.3, f32[4,1,1280]{2,1,0:T(1,128)S(1)} %reshape.6.refs_2_, f32[1,1280]{1,0:T(1,128)S(1)} %reshape.7.refs_3_, bf16[4,1280,640]{2,1,0:T(8,128)(2,1)S(1)} %get-tuple-element.84.refs_4_, ...), custom_call_target="tpu_custom_call" | custom-call | flops 1 | bytes 1 | tf_op jit(solution)/shard_map/stage_2/pallas_call | solution.py:100
  89.5 2.2 %collective-permute-done.18.one_ref = bf16[32,5120]{1,0:T(8,128)(2,1)S(1)} collective-permute-done((bf16[32,5120]{1,0:T(8,128)(2,1)S(1)}, bf16[32,5120]{1,0:T(8,128)(2,1)S(1)}, u32[]{:S(2)}, u32[]{:S(2)}) %collective-permute-start.18) | collective-permute-done | bytes 327712 | tf_op jit(solution)/shard_map/ppermute | solution.py:242
  91.7 0.7 result.1
  (26 shorter events, 1.0 us)
Async XLA Ops:
  0.0 1.7 %copy-start = (bf16[4,160,1920]{2,1,0:T(8,128)(2,1)S(1)}, bf16[4,160,1920]{2,1,0:T(8,128)(2,1)}, u32[]{:S(2)}) copy-start(bf16[4,160,1920]{2,1,0:T(8,128)(2,1)} %qkv.1) | copy-start | bytes 7372804
  1.7 1.1 %copy-start.1 = (bf16[4,80,1280]{2,1,0:T(8,128)(2,1)S(1)}, bf16[4,80,1280]{2,1,0:T(8,128)(2,1)}, u32[]{:S(2)}) copy-start(bf16[4,80,1280]{2,1,0:T(8,128)(2,1)} %out.1) | copy-start | bytes 2457604
  3.1 4.6 %collective-permute-start.2 = (bf16[8,160,640]{2,1,0:T(8,128)(2,1)S(1)}, bf16[8,160,640]{2,1,0:T(8,128)(2,1)S(1)}, u32[]{:S(2)}, u32[]{:S(2)}) collective-permute-start(bf16[8,160,640]{2,1,0:T(8,128)(2,1)S(1)} %get-tuple-element.47), channel_id=1, source_target_pairs={{0,4},{4,0},{8,12},{12,8},{16,20},{20,16},{24,28},{28,24},{1,5},{5... | collective-permute-start | bytes 4915208 | tf_op jit(solution)/shard_map/ppermute | solution.py:222
  3.6 20.6 %collective-permute-start.1 = (bf16[4,160,640]{2,1,0:T(8,128)(2,1)S(1)}, bf16[4,160,640]{2,1,0:T(8,128)(2,1)S(1)}, u32[]{:S(2)}, u32[]{:S(2)}) collective-permute-start(bf16[4,160,640]{2,1,0:T(8,128)(2,1)S(1)} %get-tuple-element.68.refs_0_.refs_2_), channel_id=1, source_target_pairs={{0,16},{4,12},{8,24},{12,4},{16,0},{20,28},{24,8},{28,20},{1,17},{... | collective-permute-start | bytes 2457608 | tf_op jit(solution)/shard_map/ppermute | solution.py:227
  6.2 21.2 %collective-permute-start = (bf16[4,160,640]{2,1,0:T(8,128)(2,1)S(1)}, bf16[4,160,640]{2,1,0:T(8,128)(2,1)S(1)}, u32[]{:S(2)}, u32[]{:S(2)}) collective-permute-start(bf16[4,160,640]{2,1,0:T(8,128)(2,1)S(1)} %get-tuple-element.68.refs_0_.refs_2_), channel_id=1, source_target_pairs={{0,8},{4,20},{8,0},{12,28},{16,24},{20,4},{24,16},{28,12},{1,9},{5... | collective-permute-start | bytes 2457608 | tf_op jit(solution)/shard_map/ppermute | solution.py:227
  7.7 34.9 %collective-permute-start.4 = (bf16[4,160,640]{2,1,0:T(8,128)(2,1)S(1)}, bf16[4,160,640]{2,1,0:T(8,128)(2,1)S(1)}, u32[]{:S(2)}, u32[]{:S(2)}) collective-permute-start(bf16[4,160,640]{2,1,0:T(8,128)(2,1)S(1)} %get-tuple-element.76.refs_8_.refs_10_), channel_id=1, source_target_pairs={{0,8},{1,5},{2,6},{3,11},{4,20},{5,1},{6,2},{7,23},{8,0},{9,13},{1... | collective-permute-start | bytes 2457608 | tf_op jit(solution)/shard_map/ppermute | solution.py:237
  9.6 33.0 %collective-permute-start.3 = (bf16[4,160,640]{2,1,0:T(8,128)(2,1)S(1)}, bf16[4,160,640]{2,1,0:T(8,128)(2,1)S(1)}, u32[]{:S(2)}, u32[]{:S(2)}) collective-permute-start(bf16[4,160,640]{2,1,0:T(8,128)(2,1)S(1)} %get-tuple-element.76.refs_8_.refs_10_), channel_id=1, source_target_pairs={{0,16},{4,12},{8,24},{12,4},{16,0},{20,28},{24,8},{28,20},{1,17},{... | collective-permute-start | bytes 2457608 | tf_op jit(solution)/shard_map/ppermute | solution.py:227
  11.1 17.3 %collective-permute-start.5 = (bf16[128,1280]{1,0:T(8,128)(2,1)}, bf16[128,1280]{1,0:T(8,128)(2,1)S(1)}, u32[]{:S(2)}, u32[]{:S(2)}) collective-permute-start(bf16[128,1280]{1,0:T(8,128)(2,1)} %refs_0_.1), channel_id=1, source_target_pairs={{0,1},{1,0},{2,3},{3,2},{4,5},{5,4},{6,7},{7,6},{8,9},{9,8},{10,11... | collective-permute-start | bytes 983048 | tf_op jit(solution)/shard_map/ppermute | solution.py:242
  24.2 4.2 %collective-permute-start.6 = (s32[1,128]{1,0:T(1,128)}, s32[1,128]{1,0:T(1,128)S(1)}, u32[]{:S(2)}, u32[]{:S(2)}) collective-permute-start(s32[1,128]{1,0:T(1,128)} %refs_1_.3), channel_id=1, source_target_pairs={{0,1},{1,0},{2,3},{3,2},{4,5},{5,4},{6,7},{7,6},{8,9},{9,8},{10,11... | collective-permute-start | bytes 1544 | tf_op jit(solution)/shard_map/ppermute | solution.py:242
  42.6 2.8 %collective-permute-start.13 = (bf16[4,160,640]{2,1,0:T(8,128)(2,1)S(1)}, bf16[4,160,640]{2,1,0:T(8,128)(2,1)S(1)}, u32[]{:S(2)}, u32[]{:S(2)}) collective-permute-start(bf16[4,160,640]{2,1,0:T(8,128)(2,1)S(1)} %collective-permute-done.3.refs_10_.refs_12_), channel_id=1, source_target_pairs={{0,4},{4,0},{8,12},{12,8},{16,20},{20,16},{24,28},{28,24},{1,5},{5... | collective-permute-start | bytes 2457608 | tf_op jit(solution)/shard_map/ppermute | solution.py:222
  42.7 4.4 %collective-permute-start.12 = (bf16[4,160,640]{2,1,0:T(8,128)(2,1)S(1)}, bf16[4,160,640]{2,1,0:T(8,128)(2,1)S(1)}, u32[]{:S(2)}, u32[]{:S(2)}) collective-permute-start(bf16[4,160,640]{2,1,0:T(8,128)(2,1)S(1)} %collective-permute-done.refs_1_.refs_3_), channel_id=1, source_target_pairs={{0,4},{1,2},{2,1},{3,7},{4,0},{5,6},{6,5},{7,3},{8,12},{9,10},{10,... | collective-permute-start | bytes 2457608 | tf_op jit(solution)/shard_map/ppermute | solution.py:237
  43.1 19.7 %collective-permute-start.8 = (bf16[4,160,640]{2,1,0:T(8,128)(2,1)S(1)}, bf16[4,160,640]{2,1,0:T(8,128)(2,1)S(1)}, u32[]{:S(2)}, u32[]{:S(2)}) collective-permute-start(bf16[4,160,640]{2,1,0:T(8,128)(2,1)S(1)} %collective-permute-done.3.refs_10_.refs_12_), channel_id=1, source_target_pairs={{0,8},{4,20},{8,0},{12,28},{16,24},{20,4},{24,16},{28,12},{1,9},{5... | collective-permute-start | bytes 2457608 | tf_op jit(solution)/shard_map/ppermute | solution.py:227
  44.9 2.4 %collective-permute-start.10 = (bf16[4,160,640]{2,1,0:T(8,128)(2,1)S(1)}, bf16[4,160,640]{2,1,0:T(8,128)(2,1)S(1)}, u32[]{:S(2)}, u32[]{:S(2)}) collective-permute-start(bf16[4,160,640]{2,1,0:T(8,128)(2,1)S(1)} %collective-permute-done.1.refs_2_.refs_4_), channel_id=1, source_target_pairs={{0,4},{4,0},{8,12},{12,8},{16,20},{20,16},{24,28},{28,24},{1,5},{5... | collective-permute-start | bytes 2457608 | tf_op jit(solution)/shard_map/ppermute | solution.py:222
  44.9 17.8 %collective-permute-start.9 = (bf16[4,160,640]{2,1,0:T(8,128)(2,1)S(1)}, bf16[4,160,640]{2,1,0:T(8,128)(2,1)S(1)}, u32[]{:S(2)}, u32[]{:S(2)}) collective-permute-start(bf16[4,160,640]{2,1,0:T(8,128)(2,1)S(1)} %collective-permute-done.refs_1_.refs_3_), channel_id=1, source_target_pairs={{0,4},{4,0},{8,12},{12,8},{16,20},{20,16},{24,28},{28,24},{1,5},{5... | collective-permute-start | bytes 2457608 | tf_op jit(solution)/shard_map/ppermute | solution.py:222
  45.4 18.3 %collective-permute-start.7 = (bf16[4,160,640]{2,1,0:T(8,128)(2,1)S(1)}, bf16[4,160,640]{2,1,0:T(8,128)(2,1)S(1)}, u32[]{:S(2)}, u32[]{:S(2)}) collective-permute-start(bf16[4,160,640]{2,1,0:T(8,128)(2,1)S(1)} %collective-permute-done.refs_1_.refs_3_), channel_id=1, source_target_pairs={{0,16},{4,12},{8,24},{12,4},{16,0},{20,28},{24,8},{28,20},{1,17},{... | collective-permute-start | bytes 2457608 | tf_op jit(solution)/shard_map/ppermute | solution.py:227
  47.1 18.9 %collective-permute-start.14 = (bf16[4,160,640]{2,1,0:T(8,128)(2,1)S(1)}, bf16[4,160,640]{2,1,0:T(8,128)(2,1)S(1)}, u32[]{:S(2)}, u32[]{:S(2)}) collective-permute-start(bf16[4,160,640]{2,1,0:T(8,128)(2,1)S(1)} %collective-permute-done.12.refs_9_), channel_id=1, source_target_pairs={{0,4},{4,0},{8,12},{12,8},{16,20},{20,16},{24,28},{28,24},{1,5},{5... | collective-permute-start | bytes 2457608 | tf_op jit(solution)/shard_map/ppermute | solution.py:222
  63.6 2.4 %collective-permute-start.11 = (bf16[4,160,640]{2,1,0:T(8,128)(2,1)S(1)}, bf16[4,160,640]{2,1,0:T(8,128)(2,1)S(1)}, u32[]{:S(2)}, u32[]{:S(2)}) collective-permute-start(bf16[4,160,640]{2,1,0:T(8,128)(2,1)S(1)} %collective-permute-done.7.refs_3_.refs_5_), channel_id=1, source_target_pairs={{0,4},{4,0},{8,12},{12,8},{16,20},{20,16},{24,28},{28,24},{1,5},{5... | collective-permute-start | bytes 2457608 | tf_op jit(solution)/shard_map/ppermute | solution.py:222
  64.0 3.1 %collective-permute-start.15 = (bf16[4,160,640]{2,1,0:T(8,128)(2,1)S(1)}, bf16[4,160,640]{2,1,0:T(8,128)(2,1)S(1)}, u32[]{:S(2)}, u32[]{:S(2)}) collective-permute-start(bf16[4,160,640]{2,1,0:T(8,128)(2,1)S(1)} %collective-permute-done.8.refs_11_.refs_13_), channel_id=1, source_target_pairs={{0,4},{4,0},{8,12},{12,8},{16,20},{20,16},{24,28},{28,24},{1,5},{5... | collective-permute-start | bytes 2457608 | tf_op jit(solution)/shard_map/ppermute | solution.py:222
  64.1 10.3 %collective-permute-start.17 = (bf16[4,160,640]{2,1,0:T(8,128)(2,1)S(1)}, bf16[4,160,640]{2,1,0:T(8,128)(2,1)S(1)}, u32[]{:S(2)}, u32[]{:S(2)}) collective-permute-start(bf16[4,160,640]{2,1,0:T(8,128)(2,1)S(1)} %collective-permute-done.4.refs_11_), channel_id=1, source_target_pairs={{0,4},{4,0},{8,12},{12,8},{16,20},{20,16},{24,28},{28,24},{1,5},{5... | collective-permute-start | bytes 2457608 | tf_op jit(solution)/shard_map/ppermute | solution.py:222
  66.0 1.2 %copy-start.2 = (bf16[128,1280]{1,0:T(8,128)(2,1)S(1)}, bf16[128,1280]{1,0:T(8,128)(2,1)}, u32[]{:S(2)}) copy-start(bf16[128,1280]{1,0:T(8,128)(2,1)} %refs_0_.1) | copy-start | bytes 983044
  66.0 1.2 %copy-start.3 = (s32[1,128]{1,0:T(1,128)S(1)}, s32[1,128]{1,0:T(1,128)}, u32[]{:S(2)}) copy-start(s32[1,128]{1,0:T(1,128)} %refs_1_.3) | copy-start | bytes 1540
  67.2 10.6 %collective-permute-start.16 = (bf16[128,1280]{1,0:T(8,128)(2,1)S(1)}, bf16[128,1280]{1,0:T(8,128)(2,1)S(1)}, u32[]{:S(2)}, u32[]{:S(2)}) collective-permute-start(bf16[128,1280]{1,0:T(8,128)(2,1)S(1)} %stage_1.2), channel_id=1, source_target_pairs={{0,1},{1,0},{2,3},{3,2},{4,5},{5,4},{6,7},{7,6},{8,9},{9,8},{10,11... | collective-permute-start | bytes 983048 | tf_op jit(solution)/shard_map/ppermute | solution.py:242
  68.0 16.2 %collective-permute-start.19 = (bf16[128,1280]{1,0:T(8,128)(2,1)S(1)}, bf16[128,1280]{1,0:T(8,128)(2,1)S(1)}, u32[]{:S(2)}, u32[]{:S(2)}) collective-permute-start(bf16[128,1280]{1,0:T(8,128)(2,1)S(1)} %stage_1.3), channel_id=1, source_target_pairs={{0,1},{1,0},{2,3},{3,2},{4,5},{5,4},{6,7},{7,6},{8,9},{9,8},{10,11... | collective-permute-start | bytes 983048 | tf_op jit(solution)/shard_map/ppermute | solution.py:242
  83.0 8.7 %collective-permute-start.18 = (bf16[32,5120]{1,0:T(8,128)(2,1)S(1)}, bf16[32,5120]{1,0:T(8,128)(2,1)S(1)}, u32[]{:S(2)}, u32[]{:S(2)}) collective-permute-start(bf16[32,5120]{1,0:T(8,128)(2,1)S(1)} %stage_2.2), channel_id=1, source_target_pairs={{0,1},{1,0},{2,3},{3,2},{4,5},{5,4},{6,7},{7,6},{8,9},{9,8},{10,11... | collective-permute-start | bytes 983048 | tf_op jit(solution)/shard_map/ppermute | solution.py:242

commit v8 on v7

--- a/solution.py
+++ b/solution.py
@@ -69,7 +69,9 @@
     rows = flow.shape[0]
     flow[...] = acts_ref[...].astype(jnp.float32)
     for i, held in enumerate((one_ref, two_ref)):
-        normed = normed_rows(flow[...], gain_ref[2 * stage - 2 + i]).astype(jnp.bfloat16)
+        normed = normed_rows(
+            flow[...], gain_ref[2 * stage - 2 + i : 2 * stage - 1 + i]
+        ).astype(jnp.bfloat16)
         qkv = [
             jnp.dot(normed, held[j], preferred_element_type=jnp.float32).astype(jnp.bfloat16)
             for j in range(3)
@@ -244,7 +246,7 @@
 
 def staged_body(patches, window_ids, norm_gain, w_qkv, w_out, merge_gain):
     tie = lax.optimization_barrier
-    gains = norm_gain.reshape(SECTIONS, 1, D_VIS)
+    gains = norm_gain
     merge = merge_gain.reshape(1, D_VIS)
 
     chunk_p, chunk_q, chunks = pack(w_qkv, w_out)

time: 92.8 us -> 92.7 us (level)
    unnamed x8 -> x10, local copies, waits for them, and re-layouts: 2.85 us -> 2.85 us
  transfers between devices with their start and end apart: 20 -> 20, of which waited for: 11 -> 12; matrix products, arithmetic and copies ran while one was open for 2% -> 1% of each run, Pallas kernels for 12% -> 13%
where the time goes in v8:
time: 92.7 us; the launch traced here: 92.5 us
  waiting for transfers between devices  52.8 us (57%)
  starting transfers between devices  23.5 us (25%)
  Pallas kernels  12.6 us (14%)
  local copies, waits for them, and re-layouts  3.55 us (4%)
    ppermute x5, waiting for transfers between devices, plane(): return lax.ppermute(block, 'dp', pairs)  29.9 us
    ppermute x2, waiting for transfers between devices, by_stage(): return lax.ppermute(block, ('dp', 'phase'), pairs)  14.2 us
    pallas_call x4, Pallas kernels, run_stage(): pl.pallas_call(functools.partial(stage_kernel, stage), out_shape=jax.Shap...  10.6 us
    ppermute x5, starting transfers between devices, across(): return lax.ppermute(block, 'phase', [(j, j ^ 1) for j in range(size)])  10 us
    ppermute x5, starting transfers between devices, plane(): return lax.ppermute(block, 'dp', pairs)  9.13 us
    ppermute x5, waiting for transfers between devices, across(): return lax.ppermute(block, 'phase', [(j, j ^ 1) for j in range(size)])  6.69 us
    unnamed x10, local copies, waits for them, and re-layouts  2.85 us
    ppermute x2, starting transfers between devices, by_stage(): return lax.ppermute(block, ('dp', 'phase'), pairs)  2.3 us
  transfers between devices with their start and end apart: 20, of which 12 were waited for; matrix products, arithmetic and copies ran while one was open for 1% of the time, Pallas kernels for 13%

profile of v8, /device:TPU:0, one launch (start us, length us, event | category | flops | bytes accessed | tf_op | source)
XLA Modules:
  0.0 92.5 jit_solution(10611386099556729710)
XLA Ops:
  0.0 1.7 %copy-done = bf16[4,160,1920]{2,1,0:T(8,128)(2,1)S(1)} copy-done((bf16[4,160,1920]{2,1,0:T(8,128)(2,1)S(1)}, bf16[4,160,1920]{2,1,0:T(8,128)(2,1)}, u32[]{:S(2)}) %copy-start) | copy-done | bytes 2457624
  1.7 1.1 %copy-done.1 = bf16[4,80,1280]{2,1,0:T(8,128)(2,1)S(1)} copy-done((bf16[4,80,1280]{2,1,0:T(8,128)(2,1)S(1)}, bf16[4,80,1280]{2,1,0:T(8,128)(2,1)}, u32[]{:S(2)}) %copy-start.1) | copy-done | bytes 819224
  3.1 0.5 collective-permute-start.2
  3.6 2.6 %collective-permute-start.1 = (bf16[4,160,640]{2,1,0:T(8,128)(2,1)S(1)}, bf16[4,160,640]{2,1,0:T(8,128)(2,1)S(1)}, u32[]{:S(2)}, u32[]{:S(2)}) collective-permute-start(bf16[4,160,640]{2,1,0:T(8,128)(2,1)S(1)} %get-tuple-element.68.refs_0_.refs_2_), channel_id=1, source_target_pairs={{0,16},{4,12},{8,24},{12,4},{16,0},{20,28},{24,8},{28,20},{1,17},{... | collective-permute-start | bytes 2457608 | tf_op jit(solution)/shard_map/ppermute | solution.py:229
  6.2 1.5 %collective-permute-start = (bf16[4,160,640]{2,1,0:T(8,128)(2,1)S(1)}, bf16[4,160,640]{2,1,0:T(8,128)(2,1)S(1)}, u32[]{:S(2)}, u32[]{:S(2)}) collective-permute-start(bf16[4,160,640]{2,1,0:T(8,128)(2,1)S(1)} %get-tuple-element.68.refs_0_.refs_2_), channel_id=1, source_target_pairs={{0,8},{4,20},{8,0},{12,28},{16,24},{20,4},{24,16},{28,12},{1,9},{5... | collective-permute-start | bytes 2457608 | tf_op jit(solution)/shard_map/ppermute | solution.py:229
  7.7 1.9 %collective-permute-start.4 = (bf16[4,160,640]{2,1,0:T(8,128)(2,1)S(1)}, bf16[4,160,640]{2,1,0:T(8,128)(2,1)S(1)}, u32[]{:S(2)}, u32[]{:S(2)}) collective-permute-start(bf16[4,160,640]{2,1,0:T(8,128)(2,1)S(1)} %get-tuple-element.76.refs_8_.refs_10_), channel_id=1, source_target_pairs={{0,8},{1,5},{2,6},{3,11},{4,20},{5,1},{6,2},{7,23},{8,0},{9,13},{1... | collective-permute-start | bytes 2457608 | tf_op jit(solution)/shard_map/ppermute | solution.py:239
  9.6 1.5 %collective-permute-start.3 = (bf16[4,160,640]{2,1,0:T(8,128)(2,1)S(1)}, bf16[4,160,640]{2,1,0:T(8,128)(2,1)S(1)}, u32[]{:S(2)}, u32[]{:S(2)}) collective-permute-start(bf16[4,160,640]{2,1,0:T(8,128)(2,1)S(1)} %get-tuple-element.76.refs_8_.refs_10_), channel_id=1, source_target_pairs={{0,16},{4,12},{8,24},{12,4},{16,0},{20,28},{24,8},{28,20},{1,17},{... | collective-permute-start | bytes 2457608 | tf_op jit(solution)/shard_map/ppermute | solution.py:229
  11.3 12.9 %collective-permute-done.1.refs_2_.refs_4_ = bf16[4,160,640]{2,1,0:T(8,128)(2,1)S(1)} collective-permute-done((bf16[4,160,640]{2,1,0:T(8,128)(2,1)S(1)}, bf16[4,160,640]{2,1,0:T(8,128)(2,1)S(1)}, u32[]{:S(2)}, u32[]{:S(2)}) %collective-permute-start.1) | collective-permute-done | bytes 819232 | tf_op jit(solution)/shard_map/ppermute | solution.py:229
  24.2 2.5 %collective-permute-start.6 = (s32[1,128]{1,0:T(1,128)}, s32[1,128]{1,0:T(1,128)S(1)}, u32[]{:S(2)}, u32[]{:S(2)}) collective-permute-start(s32[1,128]{1,0:T(1,128)} %refs_1_.3), channel_id=1, source_target_pairs={{0,1},{1,0},{2,3},{3,2},{4,5},{5,4},{6,7},{7,6},{8,9},{9,8},{10,11... | collective-permute-start | bytes 1544 | tf_op jit(solution)/shard_map/ppermute | solution.py:244
  26.8 0.6 collective-permute-done.refs_1_.refs_3_
  27.4 1.0 %collective-permute-done.6.refs_1_ = s32[1,128]{1,0:T(1,128)S(1)} collective-permute-done((s32[1,128]{1,0:T(1,128)}, s32[1,128]{1,0:T(1,128)S(1)}, u32[]{:S(2)}, u32[]{:S(2)}) %collective-permute-start.6) | collective-permute-done | bytes 544 | tf_op jit(solution)/shard_map/ppermute | solution.py:244
  28.4 14.2 %collective-permute-done.4.refs_11_ = bf16[4,160,640]{2,1,0:T(8,128)(2,1)S(1)} collective-permute-done((bf16[4,160,640]{2,1,0:T(8,128)(2,1)S(1)}, bf16[4,160,640]{2,1,0:T(8,128)(2,1)S(1)}, u32[]{:S(2)}, u32[]{:S(2)}) %collective-permute-start.4) | collective-permute-done | bytes 819232 | tf_op jit(solution)/shard_map/ppermute | solution.py:239
  42.7 0.4 collective-permute-start.12
  43.1 1.8 %collective-permute-start.8 = (bf16[4,160,640]{2,1,0:T(8,128)(2,1)S(1)}, bf16[4,160,640]{2,1,0:T(8,128)(2,1)S(1)}, u32[]{:S(2)}, u32[]{:S(2)}) collective-permute-start(bf16[4,160,640]{2,1,0:T(8,128)(2,1)S(1)} %collective-permute-done.3.refs_10_.refs_12_), channel_id=1, source_target_pairs={{0,8},{4,20},{8,0},{12,28},{16,24},{20,4},{24,16},{28,12},{1,9},{5... | collective-permute-start | bytes 2457608 | tf_op jit(solution)/shard_map/ppermute | solution.py:229
  44.9 0.4 collective-permute-start.9
  45.4 1.7 %collective-permute-start.7 = (bf16[4,160,640]{2,1,0:T(8,128)(2,1)S(1)}, bf16[4,160,640]{2,1,0:T(8,128)(2,1)S(1)}, u32[]{:S(2)}, u32[]{:S(2)}) collective-permute-start(bf16[4,160,640]{2,1,0:T(8,128)(2,1)S(1)} %collective-permute-done.refs_1_.refs_3_), channel_id=1, source_target_pairs={{0,16},{4,12},{8,24},{12,4},{16,0},{20,28},{24,8},{28,20},{1,17},{... | collective-permute-start | bytes 2457608 | tf_op jit(solution)/shard_map/ppermute | solution.py:229
  47.3 15.5 %collective-permute-done.8.refs_11_.refs_13_ = bf16[4,160,640]{2,1,0:T(8,128)(2,1)S(1)} collective-permute-done((bf16[4,160,640]{2,1,0:T(8,128)(2,1)S(1)}, bf16[4,160,640]{2,1,0:T(8,128)(2,1)S(1)}, u32[]{:S(2)}, u32[]{:S(2)}) %collective-permute-start.8) | collective-permute-done | bytes 819232 | tf_op jit(solution)/shard_map/ppermute | solution.py:229
  62.8 0.9 collective-permute-done.7.refs_3_.refs_5_
  63.6 0.4 collective-permute-start.11
  64.1 0.4 collective-permute-start.17
  64.5 0.7 reshape.3.refs_3_
  65.3 0.7 collective-permute-done.11.refs_7_.refs_9_
  66.0 1.2 %collective-permute-done.15.refs_15_.refs_17_ = bf16[4,160,640]{2,1,0:T(8,128)(2,1)S(1)} collective-permute-done((bf16[4,160,640]{2,1,0:T(8,128)(2,1)S(1)}, bf16[4,160,640]{2,1,0:T(8,128)(2,1)S(1)}, u32[]{:S(2)}, u32[]{:S(2)}) %collective-permute-start.15) | collective-permute-done | bytes 819232 | tf_op jit(solution)/shard_map/ppermute | solution.py:224
  67.2 0.8 collective-permute-start.16
  68.0 6.4 %collective-permute-start.19 = (bf16[128,1280]{1,0:T(8,128)(2,1)S(1)}, bf16[128,1280]{1,0:T(8,128)(2,1)S(1)}, u32[]{:S(2)}, u32[]{:S(2)}) collective-permute-start(bf16[128,1280]{1,0:T(8,128)(2,1)S(1)} %stage_1.3), channel_id=1, source_target_pairs={{0,1},{1,0},{2,3},{3,2},{4,5},{5,4},{6,7},{7,6},{8,9},{9,8},{10,11... | collective-permute-start | bytes 983048 | tf_op jit(solution)/shard_map/ppermute | solution.py:244
  74.4 1.0 %assemble.3 = (bf16[4,1280,640]{2,1,0:T(8,128)(2,1)S(1)}, bf16[4,1280,640]{2,1,0:T(8,128)(2,1)S(1)}) custom-call(bf16[4,1280,640]{2,1,0:T(8,128)(2,1)S(1)} %get-tuple-element.62.refs_4_.refs_0_, bf16[4,1280,640]{2,1,0:T(8,128)(2,1)S(1)} %get-tuple-element.63.refs_5_.refs_1_, ...), custom_call_target="tpu_custom_call", output_to_operand_aliasing={{0}: (0, {}), {1}: (1, {})} | custom-call | flops 1 | bytes 1 | tf_op jit(solution)/shard_map/assemble/pallas_call | solution.py:149
  75.4 2.4 %collective-permute-done.16.refs_0_ = bf16[128,1280]{1,0:T(8,128)(2,1)S(1)} collective-permute-done((bf16[128,1280]{1,0:T(8,128)(2,1)S(1)}, bf16[128,1280]{1,0:T(8,128)(2,1)S(1)}, u32[]{:S(2)}, u32[]{:S(2)}) %collective-permute-start.16) | collective-permute-done | bytes 327712 | tf_op jit(solution)/shard_map/ppermute | solution.py:244
  77.8 5.3 %stage_2.2 = bf16[32,5120]{1,0:T(8,128)(2,1)S(1)} custom-call(bf16[128,1280]{1,0:T(8,128)(2,1)S(1)} %collective-permute-done.16.refs_0_, s32[1,128]{1,0:T(1,128)S(1)} %collective-permute-done.6.refs_1_, f32[4,1280]{1,0:T(4,128)S(1)} %copy-done.2, f32[1,1280]{1,0:T(1,128)S(1)} %reshape.3.refs_3_, bf16[4,1280,640]{2,1,0:T(8,128)(2,1)S(1)} %get-tuple-element.84.refs_4_, ...), custom_call_target="tpu_custom_call" | custom-call | flops 1 | bytes 1 | tf_op jit(solution)/shard_map/stage_2/pallas_call | solution.py:102
  83.2 1.1 %collective-permute-done.19.refs_0_ = bf16[128,1280]{1,0:T(8,128)(2,1)S(1)} collective-permute-done((bf16[128,1280]{1,0:T(8,128)(2,1)S(1)}, bf16[128,1280]{1,0:T(8,128)(2,1)S(1)}, u32[]{:S(2)}, u32[]{:S(2)}) %collective-permute-start.19) | collective-permute-done | bytes 327712 | tf_op jit(solution)/shard_map/ppermute | solution.py:244
  84.3 5.3 %stage_2.3.two_ref = bf16[32,5120]{1,0:T(8,128)(2,1)S(1)} custom-call(bf16[128,1280]{1,0:T(8,128)(2,1)S(1)} %collective-permute-done.19.refs_0_, s32[1,128]{1,0:T(1,128)S(1)} %copy-done.4, f32[4,1280]{1,0:T(4,128)S(1)} %copy-done.2, f32[1,1280]{1,0:T(1,128)S(1)} %reshape.3.refs_3_, bf16[4,1280,640]{2,1,0:T(8,128)(2,1)S(1)} %get-tuple-element.84.refs_4_, ...), custom_call_target="tpu_custom_call" | custom-call | flops 1 | bytes 1 | tf_op jit(solution)/shard_map/stage_2/pallas_call | solution.py:102
  89.6 2.2 %collective-permute-done.18.one_ref = bf16[32,5120]{1,0:T(8,128)(2,1)S(1)} collective-permute-done((bf16[32,5120]{1,0:T(8,128)(2,1)S(1)}, bf16[32,5120]{1,0:T(8,128)(2,1)S(1)}, u32[]{:S(2)}, u32[]{:S(2)}) %collective-permute-start.18) | collective-permute-done | bytes 327712 | tf_op jit(solution)/shard_map/ppermute | solution.py:244
  91.8 0.7 result.1
  (27 shorter events, 1.0 us)
Async XLA Ops:
  0.0 1.7 %copy-start = (bf16[4,160,1920]{2,1,0:T(8,128)(2,1)S(1)}, bf16[4,160,1920]{2,1,0:T(8,128)(2,1)}, u32[]{:S(2)}) copy-start(bf16[4,160,1920]{2,1,0:T(8,128)(2,1)} %qkv.1) | copy-start | bytes 7372804
  1.7 1.1 %copy-start.1 = (bf16[4,80,1280]{2,1,0:T(8,128)(2,1)S(1)}, bf16[4,80,1280]{2,1,0:T(8,128)(2,1)}, u32[]{:S(2)}) copy-start(bf16[4,80,1280]{2,1,0:T(8,128)(2,1)} %out.1) | copy-start | bytes 2457604
  3.1 4.6 %collective-permute-start.2 = (bf16[8,160,640]{2,1,0:T(8,128)(2,1)S(1)}, bf16[8,160,640]{2,1,0:T(8,128)(2,1)S(1)}, u32[]{:S(2)}, u32[]{:S(2)}) collective-permute-start(bf16[8,160,640]{2,1,0:T(8,128)(2,1)S(1)} %get-tuple-element.47), channel_id=1, source_target_pairs={{0,4},{4,0},{8,12},{12,8},{16,20},{20,16},{24,28},{28,24},{1,5},{5... | collective-permute-start | bytes 4915208 | tf_op jit(solution)/shard_map/ppermute | solution.py:224
  3.6 20.6 %collective-permute-start.1 = (bf16[4,160,640]{2,1,0:T(8,128)(2,1)S(1)}, bf16[4,160,640]{2,1,0:T(8,128)(2,1)S(1)}, u32[]{:S(2)}, u32[]{:S(2)}) collective-permute-start(bf16[4,160,640]{2,1,0:T(8,128)(2,1)S(1)} %get-tuple-element.68.refs_0_.refs_2_), channel_id=1, source_target_pairs={{0,16},{4,12},{8,24},{12,4},{16,0},{20,28},{24,8},{28,20},{1,17},{... | collective-permute-start | bytes 2457608 | tf_op jit(solution)/shard_map/ppermute | solution.py:229
  6.2 21.2 %collective-permute-start = (bf16[4,160,640]{2,1,0:T(8,128)(2,1)S(1)}, bf16[4,160,640]{2,1,0:T(8,128)(2,1)S(1)}, u32[]{:S(2)}, u32[]{:S(2)}) collective-permute-start(bf16[4,160,640]{2,1,0:T(8,128)(2,1)S(1)} %get-tuple-element.68.refs_0_.refs_2_), channel_id=1, source_target_pairs={{0,8},{4,20},{8,0},{12,28},{16,24},{20,4},{24,16},{28,12},{1,9},{5... | collective-permute-start | bytes 2457608 | tf_op jit(solution)/shard_map/ppermute | solution.py:229
  7.7 34.9 %collective-permute-start.4 = (bf16[4,160,640]{2,1,0:T(8,128)(2,1)S(1)}, bf16[4,160,640]{2,1,0:T(8,128)(2,1)S(1)}, u32[]{:S(2)}, u32[]{:S(2)}) collective-permute-start(bf16[4,160,640]{2,1,0:T(8,128)(2,1)S(1)} %get-tuple-element.76.refs_8_.refs_10_), channel_id=1, source_target_pairs={{0,8},{1,5},{2,6},{3,11},{4,20},{5,1},{6,2},{7,23},{8,0},{9,13},{1... | collective-permute-start | bytes 2457608 | tf_op jit(solution)/shard_map/ppermute | solution.py:239
  9.6 33.0 %collective-permute-start.3 = (bf16[4,160,640]{2,1,0:T(8,128)(2,1)S(1)}, bf16[4,160,640]{2,1,0:T(8,128)(2,1)S(1)}, u32[]{:S(2)}, u32[]{:S(2)}) collective-permute-start(bf16[4,160,640]{2,1,0:T(8,128)(2,1)S(1)} %get-tuple-element.76.refs_8_.refs_10_), channel_id=1, source_target_pairs={{0,16},{4,12},{8,24},{12,4},{16,0},{20,28},{24,8},{28,20},{1,17},{... | collective-permute-start | bytes 2457608 | tf_op jit(solution)/shard_map/ppermute | solution.py:229
  11.1 17.3 %collective-permute-start.5 = (bf16[128,1280]{1,0:T(8,128)(2,1)}, bf16[128,1280]{1,0:T(8,128)(2,1)S(1)}, u32[]{:S(2)}, u32[]{:S(2)}) collective-permute-start(bf16[128,1280]{1,0:T(8,128)(2,1)} %refs_0_.1), channel_id=1, source_target_pairs={{0,1},{1,0},{2,3},{3,2},{4,5},{5,4},{6,7},{7,6},{8,9},{9,8},{10,11... | collective-permute-start | bytes 983048 | tf_op jit(solution)/shard_map/ppermute | solution.py:244
  24.2 4.2 %collective-permute-start.6 = (s32[1,128]{1,0:T(1,128)}, s32[1,128]{1,0:T(1,128)S(1)}, u32[]{:S(2)}, u32[]{:S(2)}) collective-permute-start(s32[1,128]{1,0:T(1,128)} %refs_1_.3), channel_id=1, source_target_pairs={{0,1},{1,0},{2,3},{3,2},{4,5},{5,4},{6,7},{7,6},{8,9},{9,8},{10,11... | collective-permute-start | bytes 1544 | tf_op jit(solution)/shard_map/ppermute | solution.py:244
  42.6 2.8 %collective-permute-start.13 = (bf16[4,160,640]{2,1,0:T(8,128)(2,1)S(1)}, bf16[4,160,640]{2,1,0:T(8,128)(2,1)S(1)}, u32[]{:S(2)}, u32[]{:S(2)}) collective-permute-start(bf16[4,160,640]{2,1,0:T(8,128)(2,1)S(1)} %collective-permute-done.3.refs_10_.refs_12_), channel_id=1, source_target_pairs={{0,4},{4,0},{8,12},{12,8},{16,20},{20,16},{24,28},{28,24},{1,5},{5... | collective-permute-start | bytes 2457608 | tf_op jit(solution)/shard_map/ppermute | solution.py:224
  42.7 4.4 %collective-permute-start.12 = (bf16[4,160,640]{2,1,0:T(8,128)(2,1)S(1)}, bf16[4,160,640]{2,1,0:T(8,128)(2,1)S(1)}, u32[]{:S(2)}, u32[]{:S(2)}) collective-permute-start(bf16[4,160,640]{2,1,0:T(8,128)(2,1)S(1)} %collective-permute-done.refs_1_.refs_3_), channel_id=1, source_target_pairs={{0,4},{1,2},{2,1},{3,7},{4,0},{5,6},{6,5},{7,3},{8,12},{9,10},{10,... | collective-permute-start | bytes 2457608 | tf_op jit(solution)/shard_map/ppermute | solution.py:239
  43.1 19.7 %collective-permute-start.8 = (bf16[4,160,640]{2,1,0:T(8,128)(2,1)S(1)}, bf16[4,160,640]{2,1,0:T(8,128)(2,1)S(1)}, u32[]{:S(2)}, u32[]{:S(2)}) collective-permute-start(bf16[4,160,640]{2,1,0:T(8,128)(2,1)S(1)} %collective-permute-done.3.refs_10_.refs_12_), channel_id=1, source_target_pairs={{0,8},{4,20},{8,0},{12,28},{16,24},{20,4},{24,16},{28,12},{1,9},{5... | collective-permute-start | bytes 2457608 | tf_op jit(solution)/shard_map/ppermute | solution.py:229
  44.9 2.4 %collective-permute-start.10 = (bf16[4,160,640]{2,1,0:T(8,128)(2,1)S(1)}, bf16[4,160,640]{2,1,0:T(8,128)(2,1)S(1)}, u32[]{:S(2)}, u32[]{:S(2)}) collective-permute-start(bf16[4,160,640]{2,1,0:T(8,128)(2,1)S(1)} %collective-permute-done.1.refs_2_.refs_4_), channel_id=1, source_target_pairs={{0,4},{4,0},{8,12},{12,8},{16,20},{20,16},{24,28},{28,24},{1,5},{5... | collective-permute-start | bytes 2457608 | tf_op jit(solution)/shard_map/ppermute | solution.py:224
  44.9 17.8 %collective-permute-start.9 = (bf16[4,160,640]{2,1,0:T(8,128)(2,1)S(1)}, bf16[4,160,640]{2,1,0:T(8,128)(2,1)S(1)}, u32[]{:S(2)}, u32[]{:S(2)}) collective-permute-start(bf16[4,160,640]{2,1,0:T(8,128)(2,1)S(1)} %collective-permute-done.refs_1_.refs_3_), channel_id=1, source_target_pairs={{0,4},{4,0},{8,12},{12,8},{16,20},{20,16},{24,28},{28,24},{1,5},{5... | collective-permute-start | bytes 2457608 | tf_op jit(solution)/shard_map/ppermute | solution.py:224
  45.4 18.3 %collective-permute-start.7 = (bf16[4,160,640]{2,1,0:T(8,128)(2,1)S(1)}, bf16[4,160,640]{2,1,0:T(8,128)(2,1)S(1)}, u32[]{:S(2)}, u32[]{:S(2)}) collective-permute-start(bf16[4,160,640]{2,1,0:T(8,128)(2,1)S(1)} %collective-permute-done.refs_1_.refs_3_), channel_id=1, source_target_pairs={{0,16},{4,12},{8,24},{12,4},{16,0},{20,28},{24,8},{28,20},{1,17},{... | collective-permute-start | bytes 2457608 | tf_op jit(solution)/shard_map/ppermute | solution.py:229
  47.1 18.1 %collective-permute-start.14 = (bf16[4,160,640]{2,1,0:T(8,128)(2,1)S(1)}, bf16[4,160,640]{2,1,0:T(8,128)(2,1)S(1)}, u32[]{:S(2)}, u32[]{:S(2)}) collective-permute-start(bf16[4,160,640]{2,1,0:T(8,128)(2,1)S(1)} %collective-permute-done.12.refs_9_), channel_id=1, source_target_pairs={{0,4},{4,0},{8,12},{12,8},{16,20},{20,16},{24,28},{28,24},{1,5},{5... | collective-permute-start | bytes 2457608 | tf_op jit(solution)/shard_map/ppermute | solution.py:224
  63.6 2.4 %collective-permute-start.11 = (bf16[4,160,640]{2,1,0:T(8,128)(2,1)S(1)}, bf16[4,160,640]{2,1,0:T(8,128)(2,1)S(1)}, u32[]{:S(2)}, u32[]{:S(2)}) collective-permute-start(bf16[4,160,640]{2,1,0:T(8,128)(2,1)S(1)} %collective-permute-done.7.refs_3_.refs_5_), channel_id=1, source_target_pairs={{0,4},{4,0},{8,12},{12,8},{16,20},{20,16},{24,28},{28,24},{1,5},{5... | collective-permute-start | bytes 2457608 | tf_op jit(solution)/shard_map/ppermute | solution.py:224
  64.0 3.1 %collective-permute-start.15 = (bf16[4,160,640]{2,1,0:T(8,128)(2,1)S(1)}, bf16[4,160,640]{2,1,0:T(8,128)(2,1)S(1)}, u32[]{:S(2)}, u32[]{:S(2)}) collective-permute-start(bf16[4,160,640]{2,1,0:T(8,128)(2,1)S(1)} %collective-permute-done.8.refs_11_.refs_13_), channel_id=1, source_target_pairs={{0,4},{4,0},{8,12},{12,8},{16,20},{20,16},{24,28},{28,24},{1,5},{5... | collective-permute-start | bytes 2457608 | tf_op jit(solution)/shard_map/ppermute | solution.py:224
  64.1 10.3 %collective-permute-start.17 = (bf16[4,160,640]{2,1,0:T(8,128)(2,1)S(1)}, bf16[4,160,640]{2,1,0:T(8,128)(2,1)S(1)}, u32[]{:S(2)}, u32[]{:S(2)}) collective-permute-start(bf16[4,160,640]{2,1,0:T(8,128)(2,1)S(1)} %collective-permute-done.4.refs_11_), channel_id=1, source_target_pairs={{0,4},{4,0},{8,12},{12,8},{16,20},{20,16},{24,28},{28,24},{1,5},{5... | collective-permute-start | bytes 2457608 | tf_op jit(solution)/shard_map/ppermute | solution.py:224
  65.2 1.9 %copy-start.2 = (f32[4,1280]{1,0:T(4,128)S(1)}, f32[4,1280]{1,0:T(4,128)}, u32[]{:S(2)}) copy-start(f32[4,1280]{1,0:T(4,128)} %refs_2_.7) | copy-start | bytes 61444
  65.2 1.9 %copy-start.3 = (bf16[128,1280]{1,0:T(8,128)(2,1)S(1)}, bf16[128,1280]{1,0:T(8,128)(2,1)}, u32[]{:S(2)}) copy-start(bf16[128,1280]{1,0:T(8,128)(2,1)} %refs_0_.1) | copy-start | bytes 983044
  65.2 1.9 %copy-start.4 = (s32[1,128]{1,0:T(1,128)S(1)}, s32[1,128]{1,0:T(1,128)}, u32[]{:S(2)}) copy-start(s32[1,128]{1,0:T(1,128)} %refs_1_.3) | copy-start | bytes 1540
  67.2 10.6 %collective-permute-start.16 = (bf16[128,1280]{1,0:T(8,128)(2,1)S(1)}, bf16[128,1280]{1,0:T(8,128)(2,1)S(1)}, u32[]{:S(2)}, u32[]{:S(2)}) collective-permute-start(bf16[128,1280]{1,0:T(8,128)(2,1)S(1)} %stage_1.2), channel_id=1, source_target_pairs={{0,1},{1,0},{2,3},{3,2},{4,5},{5,4},{6,7},{7,6},{8,9},{9,8},{10,11... | collective-permute-start | bytes 983048 | tf_op jit(solution)/shard_map/ppermute | solution.py:244
  68.0 16.3 %collective-permute-start.19 = (bf16[128,1280]{1,0:T(8,128)(2,1)S(1)}, bf16[128,1280]{1,0:T(8,128)(2,1)S(1)}, u32[]{:S(2)}, u32[]{:S(2)}) collective-permute-start(bf16[128,1280]{1,0:T(8,128)(2,1)S(1)} %stage_1.3), channel_id=1, source_target_pairs={{0,1},{1,0},{2,3},{3,2},{4,5},{5,4},{6,7},{7,6},{8,9},{9,8},{10,11... | collective-permute-start | bytes 983048 | tf_op jit(solution)/shard_map/ppermute | solution.py:244
  83.1 8.7 %collective-permute-start.18 = (bf16[32,5120]{1,0:T(8,128)(2,1)S(1)}, bf16[32,5120]{1,0:T(8,128)(2,1)S(1)}, u32[]{:S(2)}, u32[]{:S(2)}) collective-permute-start(bf16[32,5120]{1,0:T(8,128)(2,1)S(1)} %stage_2.2), channel_id=1, source_target_pairs={{0,1},{1,0},{2,3},{3,2},{4,5},{5,4},{6,7},{7,6},{8,9},{9,8},{10,11... | collective-permute-start | bytes 983048 | tf_op jit(solution)/shard_map/ppermute | solution.py:244
